TPU v7x, 512 devices: a whole 4x4x16 slice. The times are simulated.
512 devices in a mesh: seq: 128 (over x, z, y_lo), fsdp: 4 (over y_hi, core).
Axes of the slice: x: 4, y: 4 (y_hi: 2, y_lo: 2; y = y_hi * 2 + y_lo), z: 16, core: 2. Of those that a mesh axis runs over, the one named last changes fastest.
Arguments:
- tokens: bfloat16 [16384, 1024], P('seq', 'fsdp'), may hold values from -6 to 6
- w_in: bfloat16 [1024, 3, 1024], P('fsdp'), may hold values from -0.1875 to 0.1875
- short_w: float32 [3, 3, 1024], P(None, None, 'fsdp'), may hold values from -3.5 to 3.5
- long_filter: float32 [1024, 16384], P('fsdp', 'seq'), may hold values from -1.5 to 1.5, as said below
- skip_gain: float32 [1024], P('fsdp'), may hold values from -4 to 4
- w_out: bfloat16 [1024, 1024], P(None, 'fsdp'), may hold values from -0.1875 to 0.1875
Outputs:
- result: float32 [16384, 1024], P('seq', 'fsdp')
Inputs may be any that keep to these rules, and one draw needn't show every extreme that they name: `long_filter`: filter taps of each channel.
All inputs are finite; a program needn't handle non-finite values.
Results may differ from a plain program's by a relative error of at most 0.0034.
Values may be sent and summed in bfloat16 or wider, within the bound.
No kernel may reach another device: no remote copies, remote signals or barrier semaphores. Data moves between devices by JAX's collectives and lax.ppermute only.
A program may use at most 64 MiB of HBM per device.

v0:
```python
import math

import jax
import jax.numpy as jnp
from jax import lax
from jax.sharding import PartitionSpec as P


def from_behind(shard, axis, by):
    peers = lax.axis_size(axis)
    pairs = [(i, i + by) for i in range(peers) if 0 <= i + by < peers]
    return lax.ppermute(shard, axis, pairs)


def product_hi(left, right):
    return jnp.dot(left, right, precision=lax.Precision.HIGHEST, preferred_element_type=jnp.float32)


def unit_roots(rows, cols, period, sign):
    phase = rows[:, None] * cols[None, :] % period
    angle = sign * 2.0 * math.pi / period * phase.astype(jnp.float32)
    return (jnp.cos(angle), jnp.sin(angle))


def left_apply(mat_re, mat_im, data_re, data_im):
    shape = (mat_re.shape[0],) + data_re.shape[1:]
    flat_re = data_re.reshape(data_re.shape[0], -1)
    out_re = product_hi(mat_re, flat_re)
    out_im = product_hi(mat_im, flat_re)
    if data_im is not None:
        flat_im = data_im.reshape(data_im.shape[0], -1)
        out_re = out_re - product_hi(mat_im, flat_im)
        out_im = out_im + product_hi(mat_re, flat_im)
    return (out_re.reshape(shape), out_im.reshape(shape))


def middle_apply(mat_re, mat_im, data_re, data_im):

    def contract(matrix, data):
        return jnp.einsum("dr,csrg->csdg", matrix, data, precision=lax.Precision.HIGHEST)

    return (
        contract(mat_re, data_re) - contract(mat_im, data_im),
        contract(mat_re, data_im) + contract(mat_im, data_re),
    )


def on_device(tokens, w_in, short_w, long_filter, skip_gain, w_out):
    seq_count = lax.axis_size("seq")
    seq_index = lax.axis_index("seq")
    fsdp_index = lax.axis_index("fsdp")
    local_tok, local_feat = tokens.shape
    channels = short_w.shape[2]
    weights = w_in.reshape(w_in.shape[0], -1)
    partial_proj = jnp.dot(tokens, weights, preferred_element_type=jnp.float32).reshape(
        local_tok, 3, -1
    )
    projected = lax.psum_scatter(partial_proj, "fsdp", scatter_dimension=2, tiled=True)
    edge_rows = from_behind(projected[-2:], "seq", 1)
    extended = jnp.concatenate([edge_rows, projected], axis=0)
    mixed = short_w[0] * extended[2:] + short_w[1] * extended[1:-1] + short_w[2] * extended[:-2]
    query = mixed[:, 0]
    signal = mixed[:, 1] * mixed[:, 2]
    block_len = local_tok // seq_count
    double = 2 * seq_count
    period = double * local_tok
    slot_ids = jnp.arange(double, dtype=jnp.int32)
    owner_ids = slot_ids // 2
    freq_order = jnp.where(
        slot_ids % 2 == 0, owner_ids, jnp.where(owner_ids == 0, seq_count, double - owner_ids)
    )
    sources = jnp.arange(seq_count, dtype=jnp.int32)
    local_rows = jnp.arange(block_len, dtype=jnp.int32)
    offsets = seq_index * block_len + local_rows
    first_re, first_im = unit_roots(freq_order, sources, double, -1.0)
    twist_re, twist_im = unit_roots(freq_order, offsets, period, -1.0)
    local_re, local_im = unit_roots(sources, sources, seq_count, -1.0)
    inner_re, inner_im = unit_roots(sources, local_rows, local_tok, -1.0)
    short_re, short_im = unit_roots(local_rows, local_rows, block_len, -1.0)
    last_re, last_im = unit_roots(sources, freq_order, double, 1.0)
    last_re = last_re * (1.0 / period)
    last_im = last_im * (1.0 / period)
    stacked = jnp.concatenate([signal, long_filter.T], axis=1)
    arrived = lax.all_to_all(stacked, "seq", split_axis=0, concat_axis=0, tiled=True)
    spec_re, spec_im = left_apply(
        first_re, first_im, arrived.reshape(seq_count, block_len, 2 * channels), None
    )
    groups = 2 * channels
    twist_r = twist_re[:, :, None]
    twist_i = twist_im[:, :, None]
    spec_re, spec_im = (
        spec_re * twist_r - spec_im * twist_i,
        spec_re * twist_i + spec_im * twist_r,
    )
    outgoing = jnp.stack([spec_re, spec_im]).reshape(2, seq_count, 2, block_len * groups)
    landed = lax.all_to_all(outgoing, "seq", split_axis=1, concat_axis=1, tiled=True)
    part_re, part_im = left_apply(local_re, local_im, landed[0], landed[1])
    part_re = part_re.reshape(seq_count, 2, block_len, groups)
    part_im = part_im.reshape(seq_count, 2, block_len, groups)
    inner_r = inner_re[:, None, :, None]
    inner_i = inner_im[:, None, :, None]
    part_re, part_im = (
        part_re * inner_r - part_im * inner_i,
        part_re * inner_i + part_im * inner_r,
    )
    freq_re, freq_im = middle_apply(short_re, short_im, part_re, part_im)
    sig_re = freq_re[..., :channels]
    sig_im = freq_im[..., :channels]
    ker_re = freq_re[..., channels:]
    ker_im = freq_im[..., channels:]
    prod_re = sig_re * ker_re - sig_im * ker_im
    prod_im = sig_re * ker_im + sig_im * ker_re
    kept = prod_re.shape[-1]
    back_re, back_im = middle_apply(short_re, -short_im, prod_re, prod_im)
    back_re, back_im = (
        back_re * inner_r + back_im * inner_i,
        back_im * inner_r - back_re * inner_i,
    )
    time_re, time_im = left_apply(local_re, -local_im, back_re, back_im)
    returning = jnp.stack([time_re, time_im]).reshape(2, seq_count, 2, block_len * kept)
    gone = lax.all_to_all(returning, "seq", split_axis=1, concat_axis=1, tiled=True)
    gone_re = gone[0].reshape(double, block_len, kept)
    gone_im = gone[1].reshape(double, block_len, kept)
    wave_re = gone_re * twist_r + gone_im * twist_i
    wave_im = gone_im * twist_r - gone_re * twist_i
    outcome_time = product_hi(last_re, wave_re.reshape(double, -1)) - product_hi(
        last_im, wave_im.reshape(double, -1)
    )
    home_data = lax.all_to_all(outcome_time, "seq", split_axis=0, concat_axis=0, tiled=True)
    gated = (query * (home_data + skip_gain * signal)).astype(jnp.bfloat16)
    feat_start = fsdp_index * local_feat
    out_rows_w = lax.dynamic_slice_in_dim(
        lax.all_gather(w_out, "fsdp", axis=1, tiled=True), feat_start, local_feat, 0
    )
    return lax.dot_general(
        lax.all_gather(gated, "fsdp", axis=1, tiled=True),
        out_rows_w,
        (((1,), (1,)), ((), ())),
        preferred_element_type=jnp.float32,
    )


def solution(mesh):
    in_specs = (
        P("seq", "fsdp"),
        P("fsdp", None, None),
        P(None, None, "fsdp"),
        P("fsdp", "seq"),
        P("fsdp"),
        P(None, "fsdp"),
    )
    out_specs = P("seq", "fsdp")
    return jax.shard_map(
        on_device, mesh=mesh, in_specs=in_specs, out_specs=out_specs, check_vma=False
    )
```

profile of v0, /device:TPU:1, one launch (start us, length us, event | category | flops | bytes accessed | tf_op | source)
XLA Modules:
  0.0 273.9 jit_solution(14499709979188143181)
XLA Ops:
  6.5 1.7 copy.10
  8.3 1.8 fusion
  10.1 56.2 %reduce-scatter.2.cloned.1.call-done = f32[128,3,256]{2,0,1:T(8,128)} async-done(((f32[128,3,1024]{2,0,1:T(8,128)}), f32[128,3,256]{2,0,1:T(8,128)}) %reduce-scatter.2.cloned.1.call-update) | async-done | bytes 393232 | tf_op jit(solution)/shard_map/reduce_scatter | solution.py:58
  66.3 0.7 slice.68
  67.1 2.2 collective-permute-start
  69.4 0.6 collective-permute-done
  70.0 1.4 fusion.8
  71.5 1.0 copy.12
  72.5 20.1 %all-to-all-start = ((f32[128,1,512]{2,1,0:T(1,128)}), f32[128,1,512]{2,1,0:T(1,128)S(1)}, u32[]{:S(2)}, u32[]{:S(2)}) async-start(f32[128,1,512]{2,1,0:T(1,128)} %copy.12), calls=%async_computation.1 | async-start | bytes 524288 | tf_op jit(solution)/shard_map/all_to_all | solution.py:84
  92.6 19.2 %all-to-all-done = f32[128,1,512]{2,1,0:T(1,128)S(1)} async-done(((f32[128,1,512]{2,1,0:T(1,128)}), f32[128,1,512]{2,1,0:T(1,128)S(1)}, u32[]{:S(2)}, u32[]{:S(2)}) %all-to-all-start) | async-done | bytes 262176 | tf_op jit(solution)/shard_map/all_to_all | solution.py:84
  111.8 1.1 fusion.12
  112.9 1.2 multiply_subtract_fusion.1
  114.2 0.3 stack.13
  114.5 0.3 stack.12
  114.8 0.5 pad_maximum_fusion
  115.2 59.8 %all_to_all.34 = f32[2,128,2,512]{3,2,0,1:T(2,128)S(1)} all-to-all(f32[2,128,2,512]{3,2,0,1:T(2,128)S(1)} %pad_maximum_fusion), channel_id=1, replica_groups=mesh['seq'=128,'fsdp'=4] {'seq'}, dimensions={1} | all-to-all | bytes 2097152 | tf_op jit(solution)/shard_map/all_to_all | solution.py:96
  175.1 0.4 fusion.136
  175.5 0.8 fusion.75
  176.4 0.8 fusion.71
  177.2 0.1 copy.21
  177.3 0.8 convolution_add_fusion
  178.2 0.9 multiply_subtract_fusion
  179.1 0.4 sub.98
  179.6 0.4 add.178
  180.0 0.5 subtract_bitcast_fusion
  180.5 0.4 multiply_subtract_fusion.2
  180.9 0.2 multiply_add_fusion.2
  181.2 0.6 fusion.62
  181.9 0.6 fusion.68
  182.5 0.6 convolution_add_fusion.1
  183.2 0.2 stack_reshape.7
  183.4 0.6 convolution_subtract_fusion.1
  184.0 0.2 stack_reshape.6
  184.2 1.0 maximum_bitcast_fusion
  185.2 11.0 %all-to-all-start.2 = ((f32[2,128,2,256]{3,2,0,1:T(2,128)}), f32[2,128,2,256]{3,2,0,1:T(2,128)S(1)}, u32[]{:S(2)}, u32[]{:S(2)}) async-start(f32[2,128,2,256]{3,2,0,1:T(2,128)} %maximum_bitcast_fusion), calls=%async_computation.3 | async-start | bytes 1048576 | tf_op jit(solution)/shard_map/all_to_all | solution.py:121
  196.2 0.3 all-gather.2.cloned.1.call-start
  196.4 0.5 all-gather.2.cloned.1.call-update
  196.9 29.6 %all-to-all-done.2 = f32[2,128,2,256]{3,2,0,1:T(2,128)S(1)} async-done(((f32[2,128,2,256]{3,2,0,1:T(2,128)}), f32[2,128,2,256]{3,2,0,1:T(2,128)S(1)}, u32[]{:S(2)}, u32[]{:S(2)}) %all-to-all-start.2) | async-done | bytes 524320 | tf_op jit(solution)/shard_map/all_to_all | solution.py:121
  226.5 0.2 fusion.137
  226.7 0.2 reshape_squeeze.15
  226.9 0.2 reshape_squeeze.14
  227.1 0.9 fusion.18
  227.9 0.8 fusion.2
  228.8 0.8 copy.17
  229.6 9.5 %all-to-all-start.3 = ((f32[128,1,256]{2,1,0:T(1,128)}), f32[128,1,256]{2,1,0:T(1,128)S(1)}, u32[]{:S(2)}, u32[]{:S(2)}) async-start(f32[128,1,256]{2,1,0:T(1,128)} %copy.17), calls=%async_computation.4 | async-start | bytes 262144 | tf_op jit(solution)/shard_map/all_to_all | solution.py:129
  239.1 15.5 %all-to-all-done.3 = f32[128,1,256]{2,1,0:T(1,128)S(1)} async-done(((f32[128,1,256]{2,1,0:T(1,128)}), f32[128,1,256]{2,1,0:T(1,128)S(1)}, u32[]{:S(2)}, u32[]{:S(2)}) %all-to-all-start.3) | async-done | bytes 131104 | tf_op jit(solution)/shard_map/all_to_all | solution.py:129
  254.6 10.5 %all_gather.6 = bf16[128,1024]{1,0:T(8,128)(2,1)S(1)} all-gather(bf16[128,256]{1,0:T(8,128)(2,1)S(1)} %fusion.32), channel_id=1, replica_groups=mesh['seq'=128,'fsdp'=4] {'fsdp'}, dimensions={1}, use_global_device_ids=true | all-gather | bytes 327680 | tf_op jit(solution)/shard_map/all_gather | solution.py:136
  265.1 2.0 fusion.3
  (21 shorter events, 0.4 us)
Async XLA Ops:
  6.5 1.7 copy-start
  6.5 59.8 %reduce-scatter.2.cloned.1.call-start = ((), (), s32[]{:S(2)}) async-start(), calls=%async_computation.5 | async-start | bytes 1966080 | tf_op jit(solution)/shard_map/reduce_scatter | solution.py:58
  10.1 59.2 %copy-start.2 = (f32[3,3,256]{2,1,0:T(4,128)S(1)}, f32[3,3,256]{2,1,0:T(4,128)}, u32[]{:S(2)}) copy-start(f32[3,3,256]{2,1,0:T(4,128)} %param.8) | copy-start | bytes 27652
  10.1 59.2 %copy-start.1 = (f32[256,128]{1,0:T(8,128)S(1)}, f32[256,128]{1,0:T(8,128)}, u32[]{:S(2)}) copy-start(f32[256,128]{1,0:T(8,128)} %param.9) | copy-start | bytes 393220
  67.1 3.0 %collective-permute-start = (f32[2,3,256]{2,0,1:T(2,128)S(1)}, f32[2,3,256]{2,0,1:T(2,128)S(1)}, u32[]{:S(2)}, u32[]{:S(2)}) collective-permute-start(f32[2,3,256]{2,0,1:T(2,128)S(1)} %slice.68), channel_id=1, source_target_pairs={{0,4},{4,8},{8,12},{12,16},{16,20},{20,24},{24,28},{28,32},{32,36}... | collective-permute-start | bytes 18440 | tf_op jit(solution)/shard_map/ppermute | solution.py:12
  72.5 39.3 %all-to-all-start = ((f32[128,1,512]{2,1,0:T(1,128)}), f32[128,1,512]{2,1,0:T(1,128)S(1)}, u32[]{:S(2)}, u32[]{:S(2)}) async-start(f32[128,1,512]{2,1,0:T(1,128)} %copy.12), calls=%async_computation.1 | async-start | bytes 524288 | tf_op jit(solution)/shard_map/all_to_all | solution.py:84
  185.2 41.3 %all-to-all-start.2 = ((f32[2,128,2,256]{3,2,0,1:T(2,128)}), f32[2,128,2,256]{3,2,0,1:T(2,128)S(1)}, u32[]{:S(2)}, u32[]{:S(2)}) async-start(f32[2,128,2,256]{3,2,0,1:T(2,128)} %maximum_bitcast_fusion), calls=%async_computation.3 | async-start | bytes 1048576 | tf_op jit(solution)/shard_map/all_to_all | solution.py:121
  196.2 68.9 %all-gather.2.cloned.1.call-start = ((), (), s32[]{:S(2)}) async-start(), calls=%async_computation.6 | async-start | bytes 2621440 | tf_op jit(solution)/shard_map/all_gather | solution.py:133
  226.7 27.9 %copy-start.3 = (f32[256]{0:T(256)S(1)}, f32[256]{0:T(256)}, u32[]{:S(2)}) copy-start(f32[256]{0:T(256)} %param.10) | copy-start | bytes 3076
  229.6 24.9 %all-to-all-start.3 = ((f32[128,1,256]{2,1,0:T(1,128)}), f32[128,1,256]{2,1,0:T(1,128)S(1)}, u32[]{:S(2)}, u32[]{:S(2)}) async-start(f32[128,1,256]{2,1,0:T(1,128)} %copy.17), calls=%async_computation.4 | async-start | bytes 262144 | tf_op jit(solution)/shard_map/all_to_all | solution.py:129
Sparse Core Ops, SparseCore 0:
  10.4 55.8 reduce-scatter.1
  199.3 35.3 all-gather.1
where the time goes:
time: 274 us
  waiting for transfers between devices  122 us (45%)
  blocking collectives  70.3 us (26%)
  starting transfers between devices  43 us (16%)
  matrix products  13.9 us (5%)
  between operations  13.8 us (5%)
  local copies, waits for them, and re-layouts  7.32 us (3%)
  other arithmetic  4.16 us (2%)
    all_to_all x1, blocking collectives, on_device(): lax.all_to_all(outgoing, 'seq', split_axis=1, concat_axis=1, tiled=True)  59.8 us
    reduce_scatter x1, waiting for transfers between devices, on_device(): lax.psum_scatter(partial_proj, 'fsdp', scatter_dimension=2, tiled=True)  56.2 us
    all_to_all x1, waiting for transfers between devices, on_device(): lax.all_to_all(returning, 'seq', split_axis=1, concat_axis=1, tiled=True)  29.6 us
    all_to_all x1, starting transfers between devices, on_device(): lax.all_to_all(stacked, 'seq', split_axis=0, concat_axis=0, tiled=True)  20.1 us
    all_to_all x1, waiting for transfers between devices, on_device(): lax.all_to_all(stacked, 'seq', split_axis=0, concat_axis=0, tiled=True)  19.2 us
    all_to_all x1, waiting for transfers between devices, on_device(): lax.all_to_all(outcome_time, 'seq', split_axis=0, concat_axis=0, tiled=True)  15.5 us
    all_to_all x1, starting transfers between devices, on_device(): lax.all_to_all(returning, 'seq', split_axis=1, concat_axis=1, tiled=True)  11 us
    all_gather x1, blocking collectives, on_device(): lax.all_gather(gated, 'fsdp', axis=1, tiled=True)  10.5 us
  transfers between devices with their start and end apart: 6, of which 5 were waited for; matrix products, arithmetic and copies ran while one was open for 1% of the time, Pallas kernels for 0%

commit v1 on v0

v1 whole, which is shorter than its diff:
```python
import jax
import jax.numpy as jnp
import numpy as np
from jax import lax
from jax.sharding import PartitionSpec as P

HIGH = lax.Precision.HIGHEST
PROJ_SCALE = 1024.0
TAP_SCALE = 32768.0


def encode(values, scale):
    root = jnp.sqrt(jnp.abs(values)) * scale
    return jnp.where(values < 0, -root, root).astype(jnp.float16)


def decode(code, scale):
    root = code.astype(jnp.float32) * (1.0 / scale)
    return root * jnp.abs(root)


def dot(left, right):
    return jnp.dot(left, right, precision=HIGH, preferred_element_type=jnp.float32)


def transform_tables(rows, cols):
    total = rows * cols
    a, b = np.arange(rows), np.arange(cols)
    first = np.exp(-2j * np.pi * np.outer(a, a) / rows - 0.5j * np.pi * a[None, :] / rows)
    twist = np.exp(-2j * np.pi * np.outer(a, b) / total - 0.5j * np.pi * b[None, :] / total)
    second = np.exp(-2j * np.pi * np.outer(b, b) / cols)
    return first, twist, second


def f32(table):
    return jnp.asarray(np.asarray(table, np.float32))


def causal_convolution(signal, taps):
    rows, channels, cols = signal.shape
    first, twist, second = transform_tables(rows, cols)
    data = jnp.concatenate([signal, taps], axis=1).reshape(rows, -1)
    spread = dot(f32(np.concatenate([first.real, first.imag])), data).reshape(2, rows, 2 * channels, cols)
    t_re, t_im = f32(twist.real)[:, None, :], f32(twist.imag)[:, None, :]
    re = spread[0] * t_re - spread[1] * t_im
    im = spread[0] * t_im + spread[1] * t_re
    forward = f32(np.block([[second.real, second.imag], [-second.imag, second.real]]))
    freq = dot(jnp.concatenate([re, im], axis=-1).reshape(-1, 2 * cols), forward)
    freq = freq.reshape(rows, 2, channels, 2, cols)
    s_re, s_im, h_re, h_im = freq[:, 0, :, 0], freq[:, 0, :, 1], freq[:, 1, :, 0], freq[:, 1, :, 1]
    both = jnp.concatenate([s_re * h_re - s_im * h_im, s_re * h_im + s_im * h_re], axis=-1)
    inverse = f32(np.block([[second.real, -second.imag], [second.imag, second.real]]))
    back = dot(both.reshape(-1, 2 * cols), inverse).reshape(rows, channels, 2, cols)
    re = back[:, :, 0] * t_re + back[:, :, 1] * t_im
    im = back[:, :, 1] * t_re - back[:, :, 0] * t_im
    last = f32(np.concatenate([first.real.T, first.imag.T], axis=1) / (rows * cols))
    stacked = jnp.concatenate([re, im], axis=0).reshape(2 * rows, -1)
    return dot(last, stacked).reshape(rows, channels, cols)


def delayed(blocks):
    carry = jnp.concatenate([jnp.zeros_like(blocks[:1, ..., -1:]), blocks[:-1, ..., -1:]], axis=0)
    return jnp.concatenate([carry, blocks[..., :-1]], axis=-1)


def on_device(tokens, w_in, short_w, long_filter, skip_gain, w_out):
    seq_count = lax.axis_size("seq")
    fsdp_count = lax.axis_size("fsdp")
    seq_index = lax.axis_index("seq")
    local_tok = tokens.shape[0]
    channels = long_filter.shape[0]
    own = channels // seq_count
    partial = jnp.einsum("dhc,td->hct", w_in, tokens, preferred_element_type=jnp.float32)
    sent = encode(partial, PROJ_SCALE).reshape(3, fsdp_count, channels, local_tok)
    parts = lax.all_to_all(sent.transpose(1, 0, 2, 3), "fsdp", 0, 0, tiled=True)
    projected = jnp.sum(decode(parts, PROJ_SCALE), axis=0)
    packed = jnp.concatenate([encode(projected, PROJ_SCALE), encode(long_filter, TAP_SCALE)[None]])
    packed = packed.reshape(4, seq_count, own, local_tok).transpose(1, 0, 2, 3)
    whole = lax.all_to_all(packed, "seq", 0, 0, tiled=True)
    now = decode(whole[:, :3], PROJ_SCALE)
    taps = decode(whole[:, 3], TAP_SCALE)
    short = lax.dynamic_slice_in_dim(short_w, seq_index * own, own, 2)[..., None]
    skip = lax.dynamic_slice_in_dim(skip_gain, seq_index * own, own, 0)[:, None]
    before = delayed(now)
    mixed = short[0] * now + short[1] * before + short[2] * delayed(before)
    query = mixed[:, 0]
    signal = mixed[:, 1] * mixed[:, 2]
    convolved = causal_convolution(signal, taps)
    gated = (query * (convolved + skip * signal)).astype(jnp.bfloat16)
    home = lax.all_to_all(gated, "seq", 0, 0, tiled=True).reshape(channels, local_tok)
    outcome = lax.dot_general(home, w_out, (((0,), (1,)), ((), ())), preferred_element_type=jnp.float32)
    outcome = outcome.reshape(local_tok, fsdp_count, -1).transpose(1, 0, 2).astype(jnp.bfloat16)
    shares = lax.all_to_all(outcome, "fsdp", 0, 0, tiled=True)
    return jnp.sum(shares.astype(jnp.float32), axis=0)


def solution(mesh):
    in_specs = (
        P("seq", "fsdp"),
        P("fsdp", None, None),
        P(None, None, "fsdp"),
        P("fsdp", "seq"),
        P("fsdp"),
        P(None, "fsdp"),
    )
    out_specs = P("seq", "fsdp")
    return jax.shard_map(
        on_device, mesh=mesh, in_specs=in_specs, out_specs=out_specs, check_vma=False
    )
```

time: 274 us -> 107 us (0.39)
  waiting for transfers between devices: 122 us -> 32.3 us
  blocking collectives: 70.3 us -> 33.8 us
  starting transfers between devices: 43 us -> 25.6 us
  between operations: 13.8 us -> 0.39 us
  matrix products: 13.9 us -> 4.38 us
    reduce_scatter x1 -> x0, waiting for transfers between devices: 56.2 us -> none  [on_device(): lax.psum_scatter(partial_proj, 'fsdp', scatter_dimension=2, tiled=True)]
    all_to_all x3 -> x2, waiting for transfers between devices: 64.2 us -> 32.3 us  [the longest x1 20.3 us: on_device(): whole = lax.all_to_all(packed, 'seq', 0, 0, tiled=True)]
    all_to_all x1 -> x2, blocking collectives: 59.8 us -> 33.8 us  [the longest x1 22.1 us: on_device(): lax.all_to_all(gated, 'seq', 0, 0, tiled=True).reshape(channels, local_tok)]
    all_to_all x3 -> x2, starting transfers between devices: 40.5 us -> 25.6 us  [the longest x1 15.2 us: on_device(): whole = lax.all_to_all(packed, 'seq', 0, 0, tiled=True)]
    all_gather x1 -> x0, blocking collectives: 10.5 us -> none  [on_device(): lax.all_gather(gated, 'fsdp', axis=1, tiled=True)]
    dot_general x14 -> x7, matrix products: 13.9 us -> 4.38 us  [the longest x5 2.16 us: dot(): jnp.dot(left, right, precision=HIGH, preferred_element_type=jnp.float32)]
  transfers between devices with their start and end apart: 6 -> 2, of which waited for: 5 -> 2; matrix products, arithmetic and copies ran while one was open for 1% -> 0% of each run, Pallas kernels for 0% -> 0%
where the time goes in v1:
time: 107 us
  blocking collectives  33.8 us (32%)
  waiting for transfers between devices  32.3 us (30%)
  starting transfers between devices  25.6 us (24%)
  other arithmetic  5.26 us (5%)
  local copies, waits for them, and re-layouts  5.18 us (5%)
  matrix products  4.38 us (4%)
    all_to_all x1, blocking collectives, on_device(): lax.all_to_all(gated, 'seq', 0, 0, tiled=True).reshape(channels, local_tok)  22.1 us
    all_to_all x1, waiting for transfers between devices, on_device(): whole = lax.all_to_all(packed, 'seq', 0, 0, tiled=True)  20.3 us
    all_to_all x1, starting transfers between devices, on_device(): whole = lax.all_to_all(packed, 'seq', 0, 0, tiled=True)  15.2 us
    all_to_all x1, waiting for transfers between devices, on_device(): parts = lax.all_to_all(sent.transpose(1, 0, 2, 3), 'fsdp', 0, 0, tiled=True)  12.1 us
    all_to_all x1, blocking collectives, on_device(): shares = lax.all_to_all(outcome, 'fsdp', 0, 0, tiled=True)  11.8 us
    all_to_all x1, starting transfers between devices, on_device(): parts = lax.all_to_all(sent.transpose(1, 0, 2, 3), 'fsdp', 0, 0, tiled=True)  10.3 us
    unnamed x28, local copies, waits for them, and re-layouts  2.25 us
    dot_general x5, matrix products, dot(): jnp.dot(left, right, precision=HIGH, preferred_element_type=jnp.float32)  2.16 us
  transfers between devices with their start and end apart: 2, of which 2 were waited for; matrix products, arithmetic and copies ran while one was open for 0% of the time, Pallas kernels for 0%

profile of v1, /device:TPU:1, one launch (start us, length us, event | category | flops | bytes accessed | tf_op | source)
XLA Modules:
  0.0 106.9 jit_solution(16612747156301869631)
XLA Ops:
  0.0 1.4 %copy-done = bf16[256,3,1024]{2,0,1:T(8,128)(2,1)S(1)} copy-done((bf16[256,3,1024]{2,0,1:T(8,128)(2,1)S(1)}, bf16[256,3,1024]{2,0,1:T(8,128)(2,1)}, u32[]{:S(2)}) %copy-start) | copy-done | bytes 1572888
  1.4 1.9 %fusion = f16[3,1024,128]{2,1,0:T(8,128)(2,1)S(1)} fusion(bf16[256,3,1024]{2,0,1:T(8,128)(2,1)S(1)} %copy-done, bf16[128,256]{1,0:T(8,128)(2,1)} %param.12), kind=kOutput, calls=%fused_computation.2 | convolution fusion | flops 203685888 | bytes 2424832 | tf_op jit(solution)/shard_map/dhc,td->hct/dot_general | solution.py:73
  3.3 1.1 %copy.145 = f16[3,4,256,128]{3,2,0,1:T(8,128)(2,1)} copy(f16[3,4,256,128]{3,2,1,0:T(8,128)(2,1)S(1)} %bitcast.130) | data formatting | bytes 1572864 | tf_op jit(solution)/shard_map/reshape | solution.py:74
  4.4 10.3 %all-to-all-start = ((f16[4,3,256,128]{3,2,1,0:T(8,128)(2,1)}), f16[4,3,256,128]{3,2,1,0:T(8,128)(2,1)S(1)}, u32[]{:S(2)}, u32[]{:S(2)}) async-start(f16[4,3,256,128]{3,2,1,0:T(8,128)(2,1)} %bitcast.117), calls=%async_computation | async-start | bytes 1572864 | tf_op jit(solution)/shard_map/all_to_all | solution.py:75
  14.8 0.1 fusion.15
  14.9 0.2 copy.95
  15.0 12.1 %all-to-all-done = f16[4,3,256,128]{3,2,1,0:T(8,128)(2,1)S(1)} async-done(((f16[4,3,256,128]{3,2,1,0:T(8,128)(2,1)}), f16[4,3,256,128]{3,2,1,0:T(8,128)(2,1)S(1)}, u32[]{:S(2)}, u32[]{:S(2)}) %all-to-all-start) | async-done | bytes 786464 | tf_op jit(solution)/shard_map/all_to_all | solution.py:75
  27.1 0.3 fusion.1
  27.4 0.1 sqrt_multiply_fusion
  27.5 0.1 broadcast_compare_fusion
  27.6 0.1 copy.92
  27.7 0.4 fusion.3
  28.1 1.1 maximum_bitcast_fusion.2
  29.2 15.2 %all-to-all-start.1 = ((f16[128,4,2,128]{3,1,2,0:T(4,128)(2,1)}), f16[128,4,2,128]{3,1,2,0:T(4,128)(2,1)S(1)}, u32[]{:S(2)}, u32[]{:S(2)}) async-start(f16[128,4,2,128]{3,1,2,0:T(4,128)(2,1)} %maximum_bitcast_fusion.2), calls=%async_computation.1 | async-start | bytes 524288 | tf_op jit(solution)/shard_map/all_to_all | solution.py:79
  44.5 0.1 dynamic_slice.7
  44.5 0.1 dynamic-slice_bitcast_fusion.2
  44.6 20.3 %all-to-all-done.1 = f16[128,4,2,128]{3,1,2,0:T(4,128)(2,1)S(1)} async-done(((f16[128,4,2,128]{3,1,2,0:T(4,128)(2,1)}), f16[128,4,2,128]{3,1,2,0:T(4,128)(2,1)S(1)}, u32[]{:S(2)}, u32[]{:S(2)}) %all-to-all-start.1) | async-done | bytes 262176 | tf_op jit(solution)/shard_map/all_to_all | solution.py:79
  64.9 0.3 abs_multiply_fusion.1
  65.1 0.9 fusion.29
  66.0 0.5 select_maximum_fusion.1
  66.5 0.0 copy-start.4
  66.5 1.2 %fusion.8 = f32[128,3,2,128]{3,2,0,1:T(2,128)S(1)} fusion(f32[127,3,2,1]{3,2,0,1:T(2,128)S(1)} %get-tuple-element.12, f32[128,3,2,127]{3,2,0,1:T(2,128)S(1)} %bitcast.128, f32[3,2]{1,0:T(4,128)S(1)} %get-tuple-element.17, f32[3,2]{1,0:T(4,128)S(1)} %get-tuple-element.16, f32[3,2]{1,0:T(4,128)S(1)} %get-tuple-element.15, ...), kind=kLoop, calls=%fused_computation.18 | loop fusion | flops 1376256 | bytes 1376280 | tf_op jit(solution)/shard_map/add | solution.py:85
  67.7 0.1 fusion.19
  67.8 0.2 fusion.18
  67.9 0.1 pad_maximum_fusion
  68.1 0.0 copy-start.10
  68.1 0.0 copy-start.11
  68.1 0.6 fusion.9
  68.7 0.0 copy-start.3
  68.7 0.2 squeeze.11
  68.9 0.2 squeeze.12
  69.1 0.1 multiply_subtract_fusion
  69.2 0.0 copy-start.2
  69.2 0.5 copy-done.3
  69.7 0.6 fusion.4
  70.3 0.0 copy-start.8
  70.3 0.0 copy-start.9
  70.4 0.4 fusion.12
  70.9 0.3 copy-done.8
  71.1 0.0 copy-done.9
  71.2 0.3 fusion.31
  71.5 0.3 convolution_add_fusion
  71.8 0.1 copy.114
  71.9 0.2 fusion.21
  72.1 22.1 %all_to_all.20 = bf16[128,2,128]{2,1,0:T(2,128)(2,1)S(1)} all-to-all(bf16[128,2,128]{2,1,0:T(2,128)(2,1)S(1)} %fusion.21), channel_id=1, replica_groups=mesh['seq'=128,'fsdp'=4] {'seq'}, dimensions={0} | all-to-all | bytes 131072 | tf_op jit(solution)/shard_map/all_to_all | solution.py:90
  94.2 0.3 fusion.2
  94.5 11.8 %all_to_all.21 = bf16[4,128,256]{2,1,0:T(8,128)(2,1)S(1)} all-to-all(bf16[4,128,256]{2,1,0:T(8,128)(2,1)S(1)} %fusion.2), channel_id=1, replica_groups=mesh['seq'=128,'fsdp'=4] {'fsdp'}, dimensions={0} | all-to-all | bytes 524288 | tf_op jit(solution)/shard_map/all_to_all | solution.py:93
  106.3 0.7 convert_reduce_fusion
  (23 shorter events, 0.2 us)
Async XLA Ops:
  0.0 1.4 %copy-start = (bf16[256,3,1024]{2,0,1:T(8,128)(2,1)S(1)}, bf16[256,3,1024]{2,0,1:T(8,128)(2,1)}, u32[]{:S(2)}) copy-start(bf16[256,3,1024]{2,0,1:T(8,128)(2,1)} %param.13) | copy-start | bytes 4718596
  3.3 11.4 %copy-start.5 = (f32[256,128]{1,0:T(8,128)S(1)}, f32[256,128]{1,0:T(8,128)}, u32[]{:S(2)}) copy-start(f32[256,128]{1,0:T(8,128)} %param.15) | copy-start | bytes 393220
  4.4 22.6 %all-to-all-start = ((f16[4,3,256,128]{3,2,1,0:T(8,128)(2,1)}), f16[4,3,256,128]{3,2,1,0:T(8,128)(2,1)S(1)}, u32[]{:S(2)}, u32[]{:S(2)}) async-start(f16[4,3,256,128]{3,2,1,0:T(8,128)(2,1)} %bitcast.117), calls=%async_computation | async-start | bytes 1572864 | tf_op jit(solution)/shard_map/all_to_all | solution.py:75
  27.3 17.1 %copy-start.13 = (f32[256]{0:T(256)S(1)}, f32[256]{0:T(256)}, u32[]{:S(2)}) copy-start(f32[256]{0:T(256)} %param.16) | copy-start | bytes 3076
  27.4 17.2 %copy-start.12 = (f32[3,3,256]{2,1,0:T(4,128)S(1)}, f32[3,3,256]{2,1,0:T(4,128)}, u32[]{:S(2)}) copy-start(f32[3,3,256]{2,1,0:T(4,128)} %param.14) | copy-start | bytes 27652
  29.2 35.7 %all-to-all-start.1 = ((f16[128,4,2,128]{3,1,2,0:T(4,128)(2,1)}), f16[128,4,2,128]{3,1,2,0:T(4,128)(2,1)S(1)}, u32[]{:S(2)}, u32[]{:S(2)}) async-start(f16[128,4,2,128]{3,1,2,0:T(4,128)(2,1)} %maximum_bitcast_fusion.2), calls=%async_computation.1 | async-start | bytes 524288 | tf_op jit(solution)/shard_map/all_to_all | solution.py:79
  66.5 1.6 %copy-start.4 = (f32[256,128]{1,0:T(8,128)S(1)}, f32[256,128]{1,0:T(8,128)}, u32[]{:S(2)}) copy-start(f32[256,128]{1,0:T(8,128)} %constant.12.clone) | copy-start | bytes 393220
  68.1 1.0 copy-start.10
  68.1 1.0 copy-start.11
  68.7 1.0 copy-start.3
  69.2 1.2 %copy-start.2 = (f32[2,128,256,1]{2,1,0,3:T(8,128)S(1)}, f32[2,128,256,1]{2,1,0,3:T(8,128)}, u32[]{:S(2)}) copy-start(f32[2,128,256,1]{2,1,0,3:T(8,128)} %constant.57) | copy-start | bytes 786436
  70.3 0.8 copy-start.8
  70.3 0.9 copy-start.9
  70.3 0.9 copy-start.7
  70.4 1.1 %copy-start.6 = (f32[128,128]{1,0:T(8,128)S(1)}, f32[128,128]{1,0:T(8,128)}, u32[]{:S(2)}) copy-start(f32[128,128]{1,0:T(8,128)} %constant.55) | copy-start | bytes 196612
  70.8 23.3 %copy-start.1 = (bf16[1024,256]{1,0:T(8,128)(2,1)S(1)}, bf16[1024,256]{1,0:T(8,128)(2,1)}, u32[]{:S(2)}) copy-start(bf16[1024,256]{1,0:T(8,128)(2,1)} %param.17) | copy-start | bytes 1572868

commit v2 on v1

v2 whole, which is shorter than its diff:
```python
import jax
import jax.numpy as jnp
import numpy as np
from jax import lax
from jax.experimental import pallas as pl
from jax.experimental.pallas import tpu as pltpu
from jax.sharding import PartitionSpec as P

PROJ_SCALE = 2.0**21
TAP_SCALE = 2.0**31
TINY = 1e-37
VMEM = pl.BlockSpec(memory_space=pltpu.VMEM)
SMEM = pl.BlockSpec(memory_space=pltpu.SMEM)
PARAMS = pltpu.CompilerParams(vmem_limit_bytes=32 * 1024 * 1024)


def encode(scaled):
    return ((scaled * scaled) * (scaled * jnp.abs(scaled))).astype(jnp.bfloat16)


def decode(code):
    wide = code.astype(jnp.float32)
    root = lax.rsqrt(lax.rsqrt(jnp.maximum(jnp.abs(wide), TINY)))
    return jnp.where(wide < 0, -root, root)


def project_kernel(tokens_ref, w_ref, out_ref):
    peers, _, _, channels = out_ref.shape
    for peer in range(peers):
        part = jnp.dot(
            tokens_ref[...], w_ref[0, :, peer * channels : (peer + 1) * channels], preferred_element_type=jnp.float32
        )
        out_ref[peer, 0] = encode(part * PROJ_SCALE)


def project(tokens, weights, peers):
    kinds, depth, wide = weights.shape
    rows, channels = tokens.shape[0], wide // peers
    return pl.pallas_call(
        project_kernel,
        grid=(kinds,),
        in_specs=[
            pl.BlockSpec((rows, depth), lambda kind: (0, 0)),
            pl.BlockSpec((1, depth, wide), lambda kind: (kind, 0, 0)),
        ],
        out_specs=pl.BlockSpec((peers, 1, rows, channels), lambda kind: (0, kind, 0, 0)),
        out_shape=jax.ShapeDtypeStruct((peers, kinds, rows, channels), jnp.bfloat16),
        compiler_params=PARAMS,
        name="project",
    )(tokens, weights)


def pack_kernel(parts_ref, taps_ref, out_ref, flat_ref, packed_ref):
    peers, kinds, _, channels = parts_ref.shape
    half = channels // 2
    for kind in range(kinds + 1):
        if kind < kinds:
            total = decode(parts_ref[0, kind])
            for peer in range(1, peers):
                total = total + decode(parts_ref[peer, kind])
            flat_ref[...] = total.T
        else:
            flat_ref[...] = taps_ref[...] * TAP_SCALE
        for j in range(2):
            packed_ref[pl.ds(2 * kind + j, half, stride=8), :] = flat_ref[pl.ds(j, half, stride=2), :]
    out_ref[...] = encode(packed_ref[...])


def pack(parts, taps):
    channels, rows = taps.shape
    return pl.pallas_call(
        pack_kernel,
        in_specs=[VMEM, VMEM],
        out_specs=VMEM,
        out_shape=jax.ShapeDtypeStruct((4 * channels, rows), jnp.bfloat16),
        scratch_shapes=[pltpu.VMEM((channels, rows), jnp.float32), pltpu.VMEM((4 * channels, rows), jnp.float32)],
        compiler_params=PARAMS,
        name="pack",
    )(parts, taps)


def split(values):
    high = values.astype(jnp.bfloat16)
    return high, (values - high.astype(jnp.float32)).astype(jnp.bfloat16)


def dot3(left, right):
    (a, b), (c, d) = left, right
    low = jnp.dot(a, d, preferred_element_type=jnp.float32) + jnp.dot(b, c, preferred_element_type=jnp.float32)
    return jnp.dot(a, c, preferred_element_type=jnp.float32) + low


def delayed(block, by):
    rows, cols = block.shape
    moved = pltpu.roll(block, by, 1)
    col = lax.broadcasted_iota(jnp.int32, (rows, cols), 1)
    row = lax.broadcasted_iota(jnp.int32, (rows, cols), 0)
    carried = jnp.where(row == 0, 0.0, pltpu.roll(moved, 1, 0))
    return jnp.where(col < by, carried, moved)


def convolve_kernel(code_ref, short_ref, skip_ref, first_ref, twist_ref, mid_ref, inv_ref, last_ref, out_ref, now_ref, mix_ref):
    rows, cols = twist_ref.shape[1:]
    now_ref[...] = decode(code_ref[...])

    def mixed(kind, j):
        r = 2 * kind + j
        block = now_ref[pl.ds(r, rows, stride=8), :] * (1.0 / PROJ_SCALE)
        return short_ref[0, r] * block + short_ref[1, r] * delayed(block, 1) + short_ref[2, r] * delayed(block, 2)

    signal = [mixed(1, j) * mixed(2, j) for j in range(2)]
    taps = [now_ref[pl.ds(6 + j, rows, stride=8), :] * (1.0 / TAP_SCALE) for j in range(2)]
    data = jnp.concatenate(signal + taps, axis=1)
    spread = dot3((first_ref[0], first_ref[1]), split(data))
    t_re, t_im = twist_ref[0], twist_ref[1]
    turned = []
    for k in range(4):
        re = spread[:rows, k * cols : (k + 1) * cols]
        im = spread[rows:, k * cols : (k + 1) * cols]
        turned.append(jnp.concatenate([re * t_re - im * t_im, re * t_im + im * t_re], axis=1))
    freq = dot3(split(jnp.concatenate(turned, axis=0)), (mid_ref[0], mid_ref[1]))
    both = []
    for j in range(2):
        s_re, s_im = freq[j * rows : (j + 1) * rows, :cols], freq[j * rows : (j + 1) * rows, cols:]
        h_re, h_im = freq[(2 + j) * rows : (3 + j) * rows, :cols], freq[(2 + j) * rows : (3 + j) * rows, cols:]
        both.append(jnp.concatenate([s_re * h_re - s_im * h_im, s_re * h_im + s_im * h_re], axis=1))
    back = dot3(split(jnp.concatenate(both, axis=0)), (inv_ref[0], inv_ref[1]))
    real, imag = [], []
    for j in range(2):
        re, im = back[j * rows : (j + 1) * rows, :cols], back[j * rows : (j + 1) * rows, cols:]
        real.append(re * t_re + im * t_im)
        imag.append(im * t_re - re * t_im)
    stacked = jnp.concatenate([jnp.concatenate(real, axis=1), jnp.concatenate(imag, axis=1)], axis=0)
    convolved = dot3((last_ref[0], last_ref[1]), split(stacked))
    for j in range(2):
        gated = mixed(0, j) * (convolved[:, j * cols : (j + 1) * cols] + skip_ref[0, j] * signal[j])
        mix_ref[pl.ds(j, rows, stride=2), :] = gated
    out_ref[...] = mix_ref[...].astype(jnp.bfloat16)


def tables(rows, cols):
    total = rows * cols
    a, b = np.arange(rows), np.arange(cols)
    first = np.exp(-2j * np.pi * np.outer(a, a) / rows - 0.5j * np.pi * a[None, :] / rows)
    twist = np.exp(-2j * np.pi * np.outer(a, b) / total - 0.5j * np.pi * b[None, :] / total)
    second = np.exp(-2j * np.pi * np.outer(b, b) / cols)

    def halves(table):
        table = table.astype(np.float32)
        high = table.astype(jnp.bfloat16)
        return jnp.asarray(np.stack([high, (table - high.astype(np.float32)).astype(jnp.bfloat16)]))

    return (
        halves(np.concatenate([first.real, first.imag])),
        jnp.asarray(np.stack([twist.real, twist.imag]).astype(np.float32)),
        halves(np.block([[second.real, second.imag], [-second.imag, second.real]])),
        halves(np.block([[second.real, -second.imag], [second.imag, second.real]])),
        halves(np.concatenate([first.real.T, first.imag.T], axis=1) / total),
    )


def convolve(code, short, skip, rows, cols):
    return pl.pallas_call(
        convolve_kernel,
        in_specs=[VMEM, SMEM, SMEM] + [VMEM] * 5,
        out_specs=VMEM,
        out_shape=jax.ShapeDtypeStruct((2 * rows, cols), jnp.bfloat16),
        scratch_shapes=[pltpu.VMEM((8 * rows, cols), jnp.float32), pltpu.VMEM((2 * rows, cols), jnp.float32)],
        compiler_params=PARAMS,
        name="convolve",
    )(code, short, skip, *tables(rows, cols))


def output_kernel(index_ref, gated_ref, *refs):
    *w_refs, out_ref = refs
    channels = w_refs[0].shape[1]
    total = 0.0
    for step, w_ref in enumerate(w_refs):
        start = pl.multiple_of((index_ref[0] ^ step) * channels, channels)
        total = total + jnp.dot(w_ref[...], gated_ref[pl.ds(start, channels), :], preferred_element_type=jnp.float32)
    out_ref[...] = total.T


def output(index, gated, columns):
    return pl.pallas_call(
        output_kernel,
        in_specs=[SMEM, VMEM] + [VMEM] * len(columns),
        out_specs=VMEM,
        out_shape=jax.ShapeDtypeStruct((gated.shape[1], columns[0].shape[0]), jnp.float32),
        compiler_params=PARAMS,
        name="output",
    )(index, gated, *columns)


def exchanged(shares, axis):
    index = lax.axis_index(axis)
    peers = shares.shape[0]
    pieces = [lax.dynamic_index_in_dim(shares, index ^ step, 0, keepdims=False) for step in range(peers)]
    return pieces[:1] + [
        lax.ppermute(pieces[step], axis, [(i, i ^ step) for i in range(peers)]) for step in range(1, peers)
    ]


def on_device(tokens, w_in, short_w, long_filter, skip_gain, w_out):
    seq_count = lax.axis_size("seq")
    fsdp_count = lax.axis_size("fsdp")
    seq_index = lax.axis_index("seq")
    fsdp_index = lax.axis_index("fsdp")
    channels, local_tok = long_filter.shape
    partial = project(tokens, w_in.transpose(1, 0, 2), fsdp_count)
    parts = lax.all_to_all(partial, "fsdp", 0, 0, tiled=True)
    packed = pack(parts, long_filter).reshape(seq_count, -1, local_tok)
    whole = lax.all_to_all(packed, "seq", 0, 0, tiled=True).reshape(-1, local_tok)
    columns = exchanged(w_out.reshape(fsdp_count, -1, channels), "fsdp")
    short = lax.dynamic_slice_in_dim(short_w, seq_index * 2, 2, 2).reshape(3, 6)
    skip = lax.dynamic_slice_in_dim(skip_gain, seq_index * 2, 2, 0).reshape(1, 2)
    gated = convolve(whole, short, skip, seq_count, local_tok)
    home = lax.all_to_all(gated.reshape(seq_count, 2, local_tok), "seq", 0, 0, tiled=True)
    gathered = lax.all_gather(home.reshape(channels, local_tok), "fsdp", axis=0, tiled=True)
    return output(fsdp_index.reshape(1), gathered, columns)


def solution(mesh):
    in_specs = (
        P("seq", "fsdp"),
        P("fsdp", None, None),
        P(None, None, "fsdp"),
        P("fsdp", "seq"),
        P("fsdp"),
        P(None, "fsdp"),
    )
    out_specs = P("seq", "fsdp")
    return jax.shard_map(
        on_device, mesh=mesh, in_specs=in_specs, out_specs=out_specs, check_vma=False
    )
```

time: 107 us -> 99.3 us (0.928)
  starting transfers between devices: 25.6 us -> 35.2 us
  waiting for transfers between devices: 32.3 us -> 23.1 us
  Pallas kernels: 0 us -> 6.13 us
  other arithmetic: 5.26 us -> 0 us
  matrix products: 4.38 us -> 0 us
  local copies, waits for them, and re-layouts: 5.18 us -> 2.6 us
  blocking collectives: 33.8 us -> 31.7 us
    all_to_all x2 -> x1, blocking collectives: 33.8 us -> 21.5 us  [on_device(): parts = lax.all_to_all(partial, 'fsdp', 0, 0, tiled=True)]
    ppermute x0 -> x3, starting transfers between devices: none -> 10.7 us  [exchanged(): lax.ppermute(pieces[step], axis, [(i, i ^ step) for i in range(peers)])]
    all_gather x0 -> x1, blocking collectives: none -> 10.2 us  [on_device(): lax.all_gather(home.reshape(channels, local_tok), 'fsdp', axis=0, tiled=T...]
    all_to_all x2, waiting for transfers between devices: 32.3 us -> 23.1 us  [the longest x1 19.7 us: on_device(): lax.all_to_all(packed, 'seq', 0, 0, tiled=True).reshape(-1, local_tok)]
    pallas_call x0 -> x4, Pallas kernels: none -> 6.13 us  [the longest x1 2.91 us: convolve(): pl.pallas_call(convolve_kernel, in_specs=[VMEM, SMEM, SMEM] + [VMEM] * 5,...]
    dot_general x7 -> x0, matrix products: 4.38 us -> none  [the longest x5 2.16 us: dot(): jnp.dot(left, right, precision=HIGH, preferred_element_type=jnp.float32)]
    add x2 -> x0, other arithmetic: 1.19 us -> none  [the longest x1 1.16 us: on_device(): mixed = short[0] * now + short[1] * before + short[2] * delayed(before)]
    all_to_all x2, starting transfers between devices: 25.6 us -> 24.5 us  [the longest x1 16.1 us: on_device(): lax.all_to_all(packed, 'seq', 0, 0, tiled=True).reshape(-1, local_tok)]
  transfers between devices with their start and end apart: 2 -> 5, of which waited for: 2 -> 2; matrix products, arithmetic and copies ran while one was open for 0% -> 0% of each run, Pallas kernels for 0% -> 0%
where the time goes in v2:
time: 99.3 us; the launch traced here: 98.9 us
  starting transfers between devices  35.2 us (35%)
  blocking collectives  31.7 us (32%)
  waiting for transfers between devices  23.1 us (23%)
  Pallas kernels  6.13 us (6%)
  local copies, waits for them, and re-layouts  2.6 us (3%)
    all_to_all x1, blocking collectives, on_device(): parts = lax.all_to_all(partial, 'fsdp', 0, 0, tiled=True)  21.5 us
    all_to_all x1, waiting for transfers between devices, on_device(): lax.all_to_all(packed, 'seq', 0, 0, tiled=True).reshape(-1, local_tok)  19.7 us
    all_to_all x1, starting transfers between devices, on_device(): lax.all_to_all(packed, 'seq', 0, 0, tiled=True).reshape(-1, local_tok)  16.1 us
    ppermute x3, starting transfers between devices, exchanged(): lax.ppermute(pieces[step], axis, [(i, i ^ step) for i in range(peers)])  10.7 us
    all_gather x1, blocking collectives, on_device(): lax.all_gather(home.reshape(channels, local_tok), 'fsdp', axis=0, tiled=T...  10.2 us
    all_to_all x1, starting transfers between devices, on_device(): lax.all_to_all(gated.reshape(seq_count, 2, local_tok), 'seq', 0, 0, tiled...  8.41 us
    all_to_all x1, waiting for transfers between devices, on_device(): lax.all_to_all(gated.reshape(seq_count, 2, local_tok), 'seq', 0, 0, tiled...  3.38 us
    pallas_call x1, Pallas kernels, convolve(): pl.pallas_call(convolve_kernel, in_specs=[VMEM, SMEM, SMEM] + [VMEM] * 5,...  2.91 us
  transfers between devices with their start and end apart: 5, of which 2 were waited for; matrix products, arithmetic and copies ran while one was open for 0% of the time, Pallas kernels for 0%

profile of v2, /device:TPU:1, one launch (start us, length us, event | category | flops | bytes accessed | tf_op | source)
XLA Modules:
  0.0 98.9 jit_solution(11266610170205307927)
XLA Ops:
  0.0 0.0 copy-start
  0.0 0.0 copy-start.1
  0.0 1.4 %copy-done.1 = bf16[256,3,1024]{2,0,1:T(8,128)(2,1)S(1)} copy-done((bf16[256,3,1024]{2,0,1:T(8,128)(2,1)S(1)}, bf16[256,3,1024]{2,0,1:T(8,128)(2,1)}, u32[]{:S(2)}) %copy-start.1) | copy-done | bytes 1572888
  1.4 0.0 copy-start.8
  1.4 0.8 copy-done.8
  2.3 0.0 copy-start.4
  2.3 0.9 project.1
  3.1 0.0 copy-start.10
  3.1 0.0 copy-start.2
  3.2 0.0 copy-start.3
  3.2 0.0 copy-start.5
  3.2 0.0 copy-start.6
  3.2 0.0 copy-start.7
  3.2 21.5 %all_to_all.15.parts_ref = bf16[4,3,128,256]{3,2,1,0:T(8,128)(2,1)S(1)} all-to-all(bf16[4,3,128,256]{3,2,1,0:T(8,128)(2,1)S(1)} %project.1), channel_id=1, replica_groups=mesh['seq'=128,'fsdp'=4] {'fsdp'}, dimensions={0} | all-to-all | bytes 1572864 | tf_op jit(solution)/shard_map/all_to_all | solution.py:211
  24.8 0.0 copy-done.4
  24.8 0.0 copy-start.9
  24.8 1.3 %pack.1 = bf16[1024,128]{1,0:T(8,128)(2,1)} custom-call(bf16[4,3,128,256]{3,2,1,0:T(8,128)(2,1)S(1)} %all_to_all.15.parts_ref, f32[256,128]{1,0:T(8,128)S(1)} %copy-done.4), custom_call_target="tpu_custom_call" | custom-call | tf_op jit(solution)/shard_map/pack/pallas_call | solution.py:71
  26.1 16.1 %all-to-all-start.1 = ((bf16[128,8,128]{2,1,0:T(8,128)(2,1)}), bf16[128,8,128]{2,1,0:T(8,128)(2,1)S(1)}, u32[]{:S(2)}, u32[]{:S(2)}) async-start(bf16[128,8,128]{2,1,0:T(8,128)(2,1)} %bitcast.2), calls=%async_computation.1 | async-start | bytes 524288 | tf_op jit(solution)/shard_map/all_to_all | solution.py:213
  42.2 0.0 copy-done
  42.2 0.1 constant_dynamic-slice_fusion
  42.3 0.1 reshape.32.short_ref
  42.4 0.0 copy-done.10
  42.4 0.1 dynamic-slice_bitcast_fusion.4.skip_ref
  42.5 19.7 %all-to-all-done.1 = bf16[128,8,128]{2,1,0:T(8,128)(2,1)S(1)} async-done(((bf16[128,8,128]{2,1,0:T(8,128)(2,1)}), bf16[128,8,128]{2,1,0:T(8,128)(2,1)S(1)}, u32[]{:S(2)}, u32[]{:S(2)}) %all-to-all-start.1) | async-done | bytes 262176 | tf_op jit(solution)/shard_map/all_to_all | solution.py:213
  62.2 0.0 copy-done.2
  62.2 0.0 copy-done.3
  62.2 0.0 copy-done.5
  62.2 0.0 copy-done.6
  62.2 0.0 copy-done.7
  62.2 2.9 %convolve.1 = bf16[256,128]{1,0:T(8,128)(2,1)} custom-call(bf16[1024,128]{1,0:T(8,128)(2,1)S(1)} %bitcast.18, f32[3,6]{1,0:T(4,128)S(1)} %reshape.32.short_ref, f32[1,2]{1,0:T(1,128)S(1)} %dynamic-slice_bitcast_fusion.4.skip_ref, bf16[2,256,128]{2,1,0:T(8,128)(2,1)S(1)} %copy-done.5, f32[2,128,128]{2,1,0:T(8,128)S(1)} %copy-done.6, ...), custom_call_target="tpu_custom_call" | custom-call | tf_op jit(solution)/shard_map/convolve/pallas_call | solution.py:163
  65.1 8.4 %all-to-all-start.2 = ((bf16[128,2,128]{2,1,0:T(2,128)(2,1)}), bf16[128,2,128]{2,1,0:T(2,128)(2,1)S(1)}, u32[]{:S(2)}, u32[]{:S(2)}) async-start(bf16[128,2,128]{2,1,0:T(2,128)(2,1)} %bitcast.5), calls=%async_computation.2 | async-start | bytes 131072 | tf_op jit(solution)/shard_map/all_to_all | solution.py:218
  73.5 0.0 copy-done.9
  73.6 3.7 %collective-permute-start = (bf16[256,256]{1,0:T(8,128)(2,1)S(1)}, bf16[256,256]{1,0:T(8,128)(2,1)S(1)}, u32[]{:S(2)}, u32[]{:S(2)}) collective-permute-start(bf16[256,256]{1,0:T(8,128)(2,1)S(1)} %get-tuple-element.7), channel_id=1, source_target_pairs={{0,1},{1,0},{2,3},{3,2},{4,5},{5,4},{6,7},{7,6},{8,9},{9,8},{10,11... | collective-permute-start | bytes 393224 | tf_op jit(solution)/shard_map/ppermute | solution.py:200
  77.3 3.2 %collective-permute-start.1 = (bf16[256,256]{1,0:T(8,128)(2,1)S(1)}, bf16[256,256]{1,0:T(8,128)(2,1)S(1)}, u32[]{:S(2)}, u32[]{:S(2)}) collective-permute-start(bf16[256,256]{1,0:T(8,128)(2,1)S(1)} %get-tuple-element.6), channel_id=1, source_target_pairs={{0,2},{1,3},{2,0},{3,1},{4,6},{5,7},{6,4},{7,5},{8,10},{9,11},{10,... | collective-permute-start | bytes 393224 | tf_op jit(solution)/shard_map/ppermute | solution.py:200
  80.6 3.8 %collective-permute-start.2 = (bf16[256,256]{1,0:T(8,128)(2,1)S(1)}, bf16[256,256]{1,0:T(8,128)(2,1)S(1)}, u32[]{:S(2)}, u32[]{:S(2)}) collective-permute-start(bf16[256,256]{1,0:T(8,128)(2,1)S(1)} %get-tuple-element.5), channel_id=1, source_target_pairs={{0,3},{1,2},{2,1},{3,0},{4,7},{5,6},{6,5},{7,4},{8,11},{9,10},{10,... | collective-permute-start | bytes 393224 | tf_op jit(solution)/shard_map/ppermute | solution.py:200
  84.3 3.4 %all-to-all-done.2 = bf16[128,2,128]{2,1,0:T(2,128)(2,1)S(1)} async-done(((bf16[128,2,128]{2,1,0:T(2,128)(2,1)}), bf16[128,2,128]{2,1,0:T(2,128)(2,1)S(1)}, u32[]{:S(2)}, u32[]{:S(2)}) %all-to-all-start.2) | async-done | bytes 65568 | tf_op jit(solution)/shard_map/all_to_all | solution.py:218
  87.7 10.2 %all_gather.3.gated_ref = bf16[1024,128]{1,0:T(8,128)(2,1)S(1)} all-gather(bf16[256,128]{1,0:T(8,128)(2,1)S(1)} %bitcast.20), channel_id=1, replica_groups=mesh['seq'=128,'fsdp'=4] {'fsdp'}, dimensions={0}, use_global_device_ids=true | all-gather | bytes 327680 | tf_op jit(solution)/shard_map/all_gather | solution.py:219
  97.9 0.0 collective-permute-done.refs_1_
  97.9 0.0 collective-permute-done.1.refs_2_
  97.9 0.0 collective-permute-done.2.refs_3_
  97.9 1.0 %output.1 = f32[128,256]{1,0:T(8,128)} custom-call(s32[1]{0:T(128)} %bitcast.index_ref, bf16[1024,128]{1,0:T(8,128)(2,1)S(1)} %all_gather.3.gated_ref, bf16[256,256]{1,0:T(8,128)(2,1)S(1)} %get-tuple-element.8.refs_0_, bf16[256,256]{1,0:T(8,128)(2,1)S(1)} %collective-permute-done.refs_1_, bf16[256,256]{1,0:T(8,128)(2,1)S(1)} %collective-permute-done.1.refs_2_, ...), custom_call_target="tpu_custom_call" | custom-call | tf_op jit(solution)/shard_map/output/pallas_call | solution.py:185
  (1 shorter events, 0.0 us)
Async XLA Ops:
  0.0 42.2 %copy-start = (f32[3,3,256]{2,1,0:T(4,128)S(1)}, f32[3,3,256]{2,1,0:T(4,128)}, u32[]{:S(2)}) copy-start(f32[3,3,256]{2,1,0:T(4,128)} %param.13) | copy-start | bytes 27652
  0.0 1.4 %copy-start.1 = (bf16[256,3,1024]{2,0,1:T(8,128)(2,1)S(1)}, bf16[256,3,1024]{2,0,1:T(8,128)(2,1)}, u32[]{:S(2)}) copy-start(bf16[256,3,1024]{2,0,1:T(8,128)(2,1)} %param.12) | copy-start | bytes 4718596
  1.4 0.8 copy-start.8
  2.3 22.5 %copy-start.4 = (f32[256,128]{1,0:T(8,128)S(1)}, f32[256,128]{1,0:T(8,128)}, u32[]{:S(2)}) copy-start(f32[256,128]{1,0:T(8,128)} %taps_ref.1) | copy-start | bytes 393220
  3.1 39.2 %copy-start.10 = (f32[256]{0:T(256)S(1)}, f32[256]{0:T(256)}, u32[]{:S(2)}) copy-start(f32[256]{0:T(256)} %param.15) | copy-start | bytes 3076
  3.1 59.0 %copy-start.2 = (bf16[2,256,256]{2,1,0:T(8,128)(2,1)S(1)}, bf16[2,256,256]{2,1,0:T(8,128)(2,1)}, u32[]{:S(2)}) copy-start(bf16[2,256,256]{2,1,0:T(8,128)(2,1)} %constant.42.clone.mid_ref) | copy-start | bytes 786436
  3.2 59.0 %copy-start.3 = (bf16[2,256,256]{2,1,0:T(8,128)(2,1)S(1)}, bf16[2,256,256]{2,1,0:T(8,128)(2,1)}, u32[]{:S(2)}) copy-start(bf16[2,256,256]{2,1,0:T(8,128)(2,1)} %constant.43.clone.inv_ref) | copy-start | bytes 786436
  3.2 59.0 %copy-start.5 = (bf16[2,256,128]{2,1,0:T(8,128)(2,1)S(1)}, bf16[2,256,128]{2,1,0:T(8,128)(2,1)}, u32[]{:S(2)}) copy-start(bf16[2,256,128]{2,1,0:T(8,128)(2,1)} %constant.40.clone.first_ref) | copy-start | bytes 393220
  3.2 59.0 %copy-start.6 = (f32[2,128,128]{2,1,0:T(8,128)S(1)}, f32[2,128,128]{2,1,0:T(8,128)}, u32[]{:S(2)}) copy-start(f32[2,128,128]{2,1,0:T(8,128)} %constant.41.clone.twist_ref) | copy-start | bytes 393220
  3.2 59.0 %copy-start.7 = (bf16[2,128,256]{2,1,0:T(8,128)(2,1)S(1)}, bf16[2,128,256]{2,1,0:T(8,128)(2,1)}, u32[]{:S(2)}) copy-start(bf16[2,128,256]{2,1,0:T(8,128)(2,1)} %constant.44.clone.last_ref) | copy-start | bytes 393220
  24.8 48.8 %copy-start.9 = (bf16[1024,256]{1,0:T(8,128)(2,1)S(1)}, bf16[1024,256]{1,0:T(8,128)(2,1)}, u32[]{:S(2)}) copy-start(bf16[1024,256]{1,0:T(8,128)(2,1)} %param.16) | copy-start | bytes 1572868
  26.1 36.1 %all-to-all-start.1 = ((bf16[128,8,128]{2,1,0:T(8,128)(2,1)}), bf16[128,8,128]{2,1,0:T(8,128)(2,1)S(1)}, u32[]{:S(2)}, u32[]{:S(2)}) async-start(bf16[128,8,128]{2,1,0:T(8,128)(2,1)} %bitcast.2), calls=%async_computation.1 | async-start | bytes 524288 | tf_op jit(solution)/shard_map/all_to_all | solution.py:213
  65.1 22.6 %all-to-all-start.2 = ((bf16[128,2,128]{2,1,0:T(2,128)(2,1)}), bf16[128,2,128]{2,1,0:T(2,128)(2,1)S(1)}, u32[]{:S(2)}, u32[]{:S(2)}) async-start(bf16[128,2,128]{2,1,0:T(2,128)(2,1)} %bitcast.5), calls=%async_computation.2 | async-start | bytes 131072 | tf_op jit(solution)/shard_map/all_to_all | solution.py:218
  73.6 24.3 %collective-permute-start = (bf16[256,256]{1,0:T(8,128)(2,1)S(1)}, bf16[256,256]{1,0:T(8,128)(2,1)S(1)}, u32[]{:S(2)}, u32[]{:S(2)}) collective-permute-start(bf16[256,256]{1,0:T(8,128)(2,1)S(1)} %get-tuple-element.7), channel_id=1, source_target_pairs={{0,1},{1,0},{2,3},{3,2},{4,5},{5,4},{6,7},{7,6},{8,9},{9,8},{10,11... | collective-permute-start | bytes 393224 | tf_op jit(solution)/shard_map/ppermute | solution.py:200
  77.3 20.5 %collective-permute-start.1 = (bf16[256,256]{1,0:T(8,128)(2,1)S(1)}, bf16[256,256]{1,0:T(8,128)(2,1)S(1)}, u32[]{:S(2)}, u32[]{:S(2)}) collective-permute-start(bf16[256,256]{1,0:T(8,128)(2,1)S(1)} %get-tuple-element.6), channel_id=1, source_target_pairs={{0,2},{1,3},{2,0},{3,1},{4,6},{5,7},{6,4},{7,5},{8,10},{9,11},{10,... | collective-permute-start | bytes 393224 | tf_op jit(solution)/shard_map/ppermute | solution.py:200
  80.6 17.3 %collective-permute-start.2 = (bf16[256,256]{1,0:T(8,128)(2,1)S(1)}, bf16[256,256]{1,0:T(8,128)(2,1)S(1)}, u32[]{:S(2)}, u32[]{:S(2)}) collective-permute-start(bf16[256,256]{1,0:T(8,128)(2,1)S(1)} %get-tuple-element.5), channel_id=1, source_target_pairs={{0,3},{1,2},{2,1},{3,0},{4,7},{5,6},{6,5},{7,4},{8,11},{9,10},{10,... | collective-permute-start | bytes 393224 | tf_op jit(solution)/shard_map/ppermute | solution.py:200

commit v3 on v2

--- a/solution.py
+++ b/solution.py
@@ -30,7 +30,7 @@
         part = jnp.dot(
             tokens_ref[...], w_ref[0, :, peer * channels : (peer + 1) * channels], preferred_element_type=jnp.float32
         )
-        out_ref[peer, 0] = encode(part * PROJ_SCALE)
+        out_ref[peer, 0] = encode(part)
 
 
 def project(tokens, weights, peers):
@@ -102,11 +102,14 @@
 def convolve_kernel(code_ref, short_ref, skip_ref, first_ref, twist_ref, mid_ref, inv_ref, last_ref, out_ref, now_ref, mix_ref):
     rows, cols = twist_ref.shape[1:]
     now_ref[...] = decode(code_ref[...])
+    shift = short_ref.shape[2] - 2 * lax.axis_index("seq")
+    short = [pltpu.roll(short_ref[tap], shift, 1) for tap in range(3)]
+    skip = pltpu.roll(skip_ref[...], shift, 1)
 
     def mixed(kind, j):
-        r = 2 * kind + j
-        block = now_ref[pl.ds(r, rows, stride=8), :] * (1.0 / PROJ_SCALE)
-        return short_ref[0, r] * block + short_ref[1, r] * delayed(block, 1) + short_ref[2, r] * delayed(block, 2)
+        block = now_ref[pl.ds(2 * kind + j, rows, stride=8), :] * (1.0 / PROJ_SCALE)
+        weights = [short[tap][kind : kind + 1, j : j + 1] for tap in range(3)]
+        return weights[0] * block + weights[1] * delayed(block, 1) + weights[2] * delayed(block, 2)
 
     signal = [mixed(1, j) * mixed(2, j) for j in range(2)]
     taps = [now_ref[pl.ds(6 + j, rows, stride=8), :] * (1.0 / TAP_SCALE) for j in range(2)]
@@ -133,7 +136,7 @@
     stacked = jnp.concatenate([jnp.concatenate(real, axis=1), jnp.concatenate(imag, axis=1)], axis=0)
     convolved = dot3((last_ref[0], last_ref[1]), split(stacked))
     for j in range(2):
-        gated = mixed(0, j) * (convolved[:, j * cols : (j + 1) * cols] + skip_ref[0, j] * signal[j])
+        gated = mixed(0, j) * (convolved[:, j * cols : (j + 1) * cols] + skip[:, j : j + 1] * signal[j])
         mix_ref[pl.ds(j, rows, stride=2), :] = gated
     out_ref[...] = mix_ref[...].astype(jnp.bfloat16)
 
@@ -162,7 +165,7 @@
 def convolve(code, short, skip, rows, cols):
     return pl.pallas_call(
         convolve_kernel,
-        in_specs=[VMEM, SMEM, SMEM] + [VMEM] * 5,
+        in_specs=[VMEM] * 8,
         out_specs=VMEM,
         out_shape=jax.ShapeDtypeStruct((2 * rows, cols), jnp.bfloat16),
         scratch_shapes=[pltpu.VMEM((8 * rows, cols), jnp.float32), pltpu.VMEM((2 * rows, cols), jnp.float32)],
@@ -171,25 +174,26 @@
     )(code, short, skip, *tables(rows, cols))
 
 
-def output_kernel(index_ref, gated_ref, *refs):
+def output_kernel(gated_ref, *refs):
     *w_refs, out_ref = refs
+    index = lax.axis_index("fsdp")
     channels = w_refs[0].shape[1]
     total = 0.0
     for step, w_ref in enumerate(w_refs):
-        start = pl.multiple_of((index_ref[0] ^ step) * channels, channels)
+        start = pl.multiple_of((index ^ step) * channels, channels)
         total = total + jnp.dot(w_ref[...], gated_ref[pl.ds(start, channels), :], preferred_element_type=jnp.float32)
     out_ref[...] = total.T
 
 
-def output(index, gated, columns):
+def output(gated, columns):
     return pl.pallas_call(
         output_kernel,
-        in_specs=[SMEM, VMEM] + [VMEM] * len(columns),
+        in_specs=[VMEM] + [VMEM] * len(columns),
         out_specs=VMEM,
         out_shape=jax.ShapeDtypeStruct((gated.shape[1], columns[0].shape[0]), jnp.float32),
         compiler_params=PARAMS,
         name="output",
-    )(index, gated, *columns)
+    )(gated, *columns)
 
 
 def exchanged(shares, axis):
@@ -204,20 +208,18 @@
 def on_device(tokens, w_in, short_w, long_filter, skip_gain, w_out):
     seq_count = lax.axis_size("seq")
     fsdp_count = lax.axis_size("fsdp")
-    seq_index = lax.axis_index("seq")
-    fsdp_index = lax.axis_index("fsdp")
     channels, local_tok = long_filter.shape
-    partial = project(tokens, w_in.transpose(1, 0, 2), fsdp_count)
+    scaled = tokens * jnp.bfloat16(PROJ_SCALE)
+    partial = project(scaled, w_in.transpose(1, 0, 2), fsdp_count)
     parts = lax.all_to_all(partial, "fsdp", 0, 0, tiled=True)
     packed = pack(parts, long_filter).reshape(seq_count, -1, local_tok)
     whole = lax.all_to_all(packed, "seq", 0, 0, tiled=True).reshape(-1, local_tok)
+    gated = convolve(whole, short_w, skip_gain.reshape(1, -1), seq_count, local_tok)
+    gated, w_out = lax.optimization_barrier((gated, w_out))
     columns = exchanged(w_out.reshape(fsdp_count, -1, channels), "fsdp")
-    short = lax.dynamic_slice_in_dim(short_w, seq_index * 2, 2, 2).reshape(3, 6)
-    skip = lax.dynamic_slice_in_dim(skip_gain, seq_index * 2, 2, 0).reshape(1, 2)
-    gated = convolve(whole, short, skip, seq_count, local_tok)
     home = lax.all_to_all(gated.reshape(seq_count, 2, local_tok), "seq", 0, 0, tiled=True)
     gathered = lax.all_gather(home.reshape(channels, local_tok), "fsdp", axis=0, tiled=True)
-    return output(fsdp_index.reshape(1), gathered, columns)
+    return output(gathered, columns)
 
 
 def solution(mesh):

time: 99.3 us -> 97.8 us (0.985)
  blocking collectives: 31.7 us -> 67.6 us
  waiting for transfers between devices: 23.1 us -> 3.38 us
  starting transfers between devices: 35.2 us -> 19.1 us
  Pallas kernels: 6.13 us -> 4.81 us
  local copies, waits for them, and re-layouts: 2.6 us -> 1.5 us
    all_to_all x0 -> x1, blocking collectives: none -> 35.9 us  [on_device(): lax.all_to_all(packed, 'seq', 0, 0, tiled=True).reshape(-1, local_tok)]
    all_to_all x1 -> x0, waiting for transfers between devices: 19.7 us -> none  [on_device(): lax.all_to_all(packed, 'seq', 0, 0, tiled=True).reshape(-1, local_tok)]
    all_to_all x1 -> x0, starting transfers between devices: 16.1 us -> none  [on_device(): lax.all_to_all(packed, 'seq', 0, 0, tiled=True).reshape(-1, local_tok)]
    unnamed x22 -> x20, local copies, waits for them, and re-layouts: 2.31 us -> 1.46 us
  transfers between devices with their start and end apart: 5 -> 4, of which waited for: 2 -> 1; matrix products, arithmetic and copies ran while one was open for 0% -> 0% of each run, Pallas kernels for 0% -> 0%
where the time goes in v3:
time: 97.8 us; the launch traced here: 97.4 us
  blocking collectives  67.6 us (69%)
  starting transfers between devices  19.1 us (20%)
  Pallas kernels  4.81 us (5%)
  waiting for transfers between devices  3.38 us (3%)
  local copies, waits for them, and re-layouts  1.5 us (2%)
    all_to_all x1, blocking collectives, on_device(): lax.all_to_all(packed, 'seq', 0, 0, tiled=True).reshape(-1, local_tok)  35.9 us
    all_to_all x1, blocking collectives, on_device(): parts = lax.all_to_all(partial, 'fsdp', 0, 0, tiled=True)  21.5 us
    ppermute x3, starting transfers between devices, exchanged(): lax.ppermute(pieces[step], axis, [(i, i ^ step) for i in range(peers)])  10.7 us
    all_gather x1, blocking collectives, on_device(): lax.all_gather(home.reshape(channels, local_tok), 'fsdp', axis=0, tiled=T...  10.2 us
    all_to_all x1, starting transfers between devices, on_device(): lax.all_to_all(gated.reshape(seq_count, 2, local_tok), 'seq', 0, 0, tiled...  8.4 us
    all_to_all x1, waiting for transfers between devices, on_device(): lax.all_to_all(gated.reshape(seq_count, 2, local_tok), 'seq', 0, 0, tiled...  3.37 us
    pallas_call x1, Pallas kernels, convolve(): pl.pallas_call(convolve_kernel, in_specs=[VMEM] * 8, out_specs=VMEM, out_...  2.36 us
  transfers between devices with their start and end apart: 4, of which 1 were waited for; matrix products, arithmetic and copies ran while one was open for 0% of the time, Pallas kernels for 0%

profile of v3, /device:TPU:1, one launch (start us, length us, event | category | flops | bytes accessed | tf_op | source)
XLA Modules:
  0.0 97.4 jit_solution(10907134163579875746)
XLA Ops:
  0.0 0.8 broadcast_multiply_fusion.tokens_ref
  0.8 0.0 copy-start
  0.9 1.4 %copy-done = bf16[256,3,1024]{2,0,1:T(8,128)(2,1)S(1)} copy-done((bf16[256,3,1024]{2,0,1:T(8,128)(2,1)S(1)}, bf16[256,3,1024]{2,0,1:T(8,128)(2,1)}, u32[]{:S(2)}) %copy-start) | copy-done | bytes 1572888
  2.3 0.0 copy-start.3
  2.3 0.8 project.1
  3.1 0.0 copy-start.1
  3.1 0.0 copy-start.2
  3.1 0.0 copy-start.4
  3.1 0.0 copy-start.5
  3.1 0.0 copy-start.6
  3.1 0.0 copy-start.7
  3.2 0.0 copy-start.8
  3.2 21.5 %all_to_all.15.parts_ref = bf16[4,3,128,256]{3,2,1,0:T(8,128)(2,1)S(1)} all-to-all(bf16[4,3,128,256]{3,2,1,0:T(8,128)(2,1)S(1)} %project.1), channel_id=1, replica_groups=mesh['seq'=128,'fsdp'=4] {'fsdp'}, dimensions={0} | all-to-all | bytes 1572864 | tf_op jit(solution)/shard_map/all_to_all | solution.py:214
  24.7 0.0 copy-done.3
  24.7 0.0 copy-start.9
  24.7 0.6 pack.1
  25.3 35.9 %all_to_all.16 = bf16[128,8,128]{2,1,0:T(8,128)(2,1)S(1)} all-to-all(bf16[128,8,128]{2,1,0:T(8,128)(2,1)S(1)} %bitcast.17), channel_id=1, replica_groups=mesh['seq'=128,'fsdp'=4] {'seq'}, dimensions={0} | all-to-all | bytes 524288 | tf_op jit(solution)/shard_map/all_to_all | solution.py:216
  61.2 0.0 copy-done.1
  61.2 0.0 copy-done.2
  61.2 0.0 copy-done.4
  61.2 0.0 copy-done.5
  61.2 0.0 copy-done.6
  61.2 0.0 copy-done.7
  61.2 0.0 copy-done.8
  61.3 2.4 %convolve.1 = bf16[256,128]{1,0:T(8,128)(2,1)} custom-call(bf16[1024,128]{1,0:T(8,128)(2,1)S(1)} %bitcast.16, f32[3,3,256]{2,1,0:T(4,128)S(1)} %copy-done.7, f32[1,256]{1,0:T(1,128)S(1)} %bitcast.18, bf16[2,256,128]{2,1,0:T(8,128)(2,1)S(1)} %copy-done.4, f32[2,128,128]{2,1,0:T(8,128)S(1)} %copy-done.5, bf16[2,256,256]{2,1,0:T(8,128)(2,1)S(1)} %copy-done.1, ...), custom_call_target="tpu_custom_call" | custom-call | tf_op jit(solution)/shard_map/convolve/pallas_call | solution.py:166
  63.6 8.4 %all-to-all-start.2 = ((bf16[128,2,128]{2,1,0:T(2,128)(2,1)}), bf16[128,2,128]{2,1,0:T(2,128)(2,1)S(1)}, u32[]{:S(2)}, u32[]{:S(2)}) async-start(bf16[128,2,128]{2,1,0:T(2,128)(2,1)} %bitcast.4), calls=%async_computation.2 | async-start | bytes 131072 | tf_op jit(solution)/shard_map/all_to_all | solution.py:220
  72.0 0.0 copy-done.9
  72.1 3.7 %collective-permute-start = (bf16[256,256]{1,0:T(8,128)(2,1)S(1)}, bf16[256,256]{1,0:T(8,128)(2,1)S(1)}, u32[]{:S(2)}, u32[]{:S(2)}) collective-permute-start(bf16[256,256]{1,0:T(8,128)(2,1)S(1)} %get-tuple-element.11), channel_id=1, source_target_pairs={{0,1},{1,0},{2,3},{3,2},{4,5},{5,4},{6,7},{7,6},{8,9},{9,8},{10,11... | collective-permute-start | bytes 393224 | tf_op jit(solution)/shard_map/ppermute | solution.py:204
  75.9 3.2 %collective-permute-start.1 = (bf16[256,256]{1,0:T(8,128)(2,1)S(1)}, bf16[256,256]{1,0:T(8,128)(2,1)S(1)}, u32[]{:S(2)}, u32[]{:S(2)}) collective-permute-start(bf16[256,256]{1,0:T(8,128)(2,1)S(1)} %get-tuple-element.10), channel_id=1, source_target_pairs={{0,2},{1,3},{2,0},{3,1},{4,6},{5,7},{6,4},{7,5},{8,10},{9,11},{10,... | collective-permute-start | bytes 393224 | tf_op jit(solution)/shard_map/ppermute | solution.py:204
  79.1 3.8 %collective-permute-start.2 = (bf16[256,256]{1,0:T(8,128)(2,1)S(1)}, bf16[256,256]{1,0:T(8,128)(2,1)S(1)}, u32[]{:S(2)}, u32[]{:S(2)}) collective-permute-start(bf16[256,256]{1,0:T(8,128)(2,1)S(1)} %get-tuple-element.9), channel_id=1, source_target_pairs={{0,3},{1,2},{2,1},{3,0},{4,7},{5,6},{6,5},{7,4},{8,11},{9,10},{10,... | collective-permute-start | bytes 393224 | tf_op jit(solution)/shard_map/ppermute | solution.py:204
  82.8 3.4 %all-to-all-done.2 = bf16[128,2,128]{2,1,0:T(2,128)(2,1)S(1)} async-done(((bf16[128,2,128]{2,1,0:T(2,128)(2,1)}), bf16[128,2,128]{2,1,0:T(2,128)(2,1)S(1)}, u32[]{:S(2)}, u32[]{:S(2)}) %all-to-all-start.2) | async-done | bytes 65568 | tf_op jit(solution)/shard_map/all_to_all | solution.py:220
  86.2 10.2 %all_gather.3.gated_ref = bf16[1024,128]{1,0:T(8,128)(2,1)S(1)} all-gather(bf16[256,128]{1,0:T(8,128)(2,1)S(1)} %bitcast.20), channel_id=1, replica_groups=mesh['seq'=128,'fsdp'=4] {'fsdp'}, dimensions={0}, use_global_device_ids=true | all-gather | bytes 327680 | tf_op jit(solution)/shard_map/all_gather | solution.py:221
  96.4 0.0 collective-permute-done.refs_1_
  96.4 0.0 collective-permute-done.1.refs_2_
  96.4 0.0 collective-permute-done.2.refs_3_
  96.4 1.0 %output.1 = f32[128,256]{1,0:T(8,128)} custom-call(bf16[1024,128]{1,0:T(8,128)(2,1)S(1)} %all_gather.3.gated_ref, bf16[256,256]{1,0:T(8,128)(2,1)S(1)} %get-tuple-element.12.refs_0_, bf16[256,256]{1,0:T(8,128)(2,1)S(1)} %collective-permute-done.refs_1_, bf16[256,256]{1,0:T(8,128)(2,1)S(1)} %collective-permute-done.1.refs_2_, ...), custom_call_target="tpu_custom_call" | custom-call | tf_op jit(solution)/shard_map/output/pallas_call | solution.py:189
  (1 shorter events, 0.0 us)
Async XLA Ops:
  0.8 1.4 %copy-start = (bf16[256,3,1024]{2,0,1:T(8,128)(2,1)S(1)}, bf16[256,3,1024]{2,0,1:T(8,128)(2,1)}, u32[]{:S(2)}) copy-start(bf16[256,3,1024]{2,0,1:T(8,128)(2,1)} %param.12) | copy-start | bytes 4718596
  2.3 22.5 %copy-start.3 = (f32[256,128]{1,0:T(8,128)S(1)}, f32[256,128]{1,0:T(8,128)}, u32[]{:S(2)}) copy-start(f32[256,128]{1,0:T(8,128)} %taps_ref.1) | copy-start | bytes 393220
  3.1 58.1 %copy-start.1 = (bf16[2,256,256]{2,1,0:T(8,128)(2,1)S(1)}, bf16[2,256,256]{2,1,0:T(8,128)(2,1)}, u32[]{:S(2)}) copy-start(bf16[2,256,256]{2,1,0:T(8,128)(2,1)} %constant.36.clone.mid_ref) | copy-start | bytes 786436
  3.1 58.1 %copy-start.2 = (bf16[2,256,256]{2,1,0:T(8,128)(2,1)S(1)}, bf16[2,256,256]{2,1,0:T(8,128)(2,1)}, u32[]{:S(2)}) copy-start(bf16[2,256,256]{2,1,0:T(8,128)(2,1)} %constant.37.clone.inv_ref) | copy-start | bytes 786436
  3.1 58.1 %copy-start.4 = (bf16[2,256,128]{2,1,0:T(8,128)(2,1)S(1)}, bf16[2,256,128]{2,1,0:T(8,128)(2,1)}, u32[]{:S(2)}) copy-start(bf16[2,256,128]{2,1,0:T(8,128)(2,1)} %constant.34.clone.first_ref) | copy-start | bytes 393220
  3.1 58.1 %copy-start.5 = (f32[2,128,128]{2,1,0:T(8,128)S(1)}, f32[2,128,128]{2,1,0:T(8,128)}, u32[]{:S(2)}) copy-start(f32[2,128,128]{2,1,0:T(8,128)} %constant.35.clone.twist_ref) | copy-start | bytes 393220
  3.1 58.1 %copy-start.6 = (bf16[2,128,256]{2,1,0:T(8,128)(2,1)S(1)}, bf16[2,128,256]{2,1,0:T(8,128)(2,1)}, u32[]{:S(2)}) copy-start(bf16[2,128,256]{2,1,0:T(8,128)(2,1)} %constant.38.clone.last_ref) | copy-start | bytes 393220
  3.1 58.1 %copy-start.7 = (f32[3,3,256]{2,1,0:T(4,128)S(1)}, f32[3,3,256]{2,1,0:T(4,128)}, u32[]{:S(2)}) copy-start(f32[3,3,256]{2,1,0:T(4,128)} %short_ref.1) | copy-start | bytes 27652
  3.2 58.1 %copy-start.8 = (f32[256]{0:T(256)S(1)}, f32[256]{0:T(256)}, u32[]{:S(2)}) copy-start(f32[256]{0:T(256)} %param.15) | copy-start | bytes 3076
  24.7 47.3 %copy-start.9 = (bf16[1024,256]{1,0:T(8,128)(2,1)S(1)}, bf16[1024,256]{1,0:T(8,128)(2,1)}, u32[]{:S(2)}) copy-start(bf16[1024,256]{1,0:T(8,128)(2,1)} %param.16) | copy-start | bytes 1572868
  63.6 22.6 %all-to-all-start.2 = ((bf16[128,2,128]{2,1,0:T(2,128)(2,1)}), bf16[128,2,128]{2,1,0:T(2,128)(2,1)S(1)}, u32[]{:S(2)}, u32[]{:S(2)}) async-start(bf16[128,2,128]{2,1,0:T(2,128)(2,1)} %bitcast.4), calls=%async_computation.2 | async-start | bytes 131072 | tf_op jit(solution)/shard_map/all_to_all | solution.py:220
  72.1 24.3 %collective-permute-start = (bf16[256,256]{1,0:T(8,128)(2,1)S(1)}, bf16[256,256]{1,0:T(8,128)(2,1)S(1)}, u32[]{:S(2)}, u32[]{:S(2)}) collective-permute-start(bf16[256,256]{1,0:T(8,128)(2,1)S(1)} %get-tuple-element.11), channel_id=1, source_target_pairs={{0,1},{1,0},{2,3},{3,2},{4,5},{5,4},{6,7},{7,6},{8,9},{9,8},{10,11... | collective-permute-start | bytes 393224 | tf_op jit(solution)/shard_map/ppermute | solution.py:204
  75.9 20.5 %collective-permute-start.1 = (bf16[256,256]{1,0:T(8,128)(2,1)S(1)}, bf16[256,256]{1,0:T(8,128)(2,1)S(1)}, u32[]{:S(2)}, u32[]{:S(2)}) collective-permute-start(bf16[256,256]{1,0:T(8,128)(2,1)S(1)} %get-tuple-element.10), channel_id=1, source_target_pairs={{0,2},{1,3},{2,0},{3,1},{4,6},{5,7},{6,4},{7,5},{8,10},{9,11},{10,... | collective-permute-start | bytes 393224 | tf_op jit(solution)/shard_map/ppermute | solution.py:204
  79.1 17.3 %collective-permute-start.2 = (bf16[256,256]{1,0:T(8,128)(2,1)S(1)}, bf16[256,256]{1,0:T(8,128)(2,1)S(1)}, u32[]{:S(2)}, u32[]{:S(2)}) collective-permute-start(bf16[256,256]{1,0:T(8,128)(2,1)S(1)} %get-tuple-element.9), channel_id=1, source_target_pairs={{0,3},{1,2},{2,1},{3,0},{4,7},{5,6},{6,5},{7,4},{8,11},{9,10},{10,... | collective-permute-start | bytes 393224 | tf_op jit(solution)/shard_map/ppermute | solution.py:204

commit v4 on v3

--- a/solution.py
+++ b/solution.py
@@ -24,27 +24,29 @@
     return jnp.where(wide < 0, -root, root)
 
 
-def project_kernel(tokens_ref, w_ref, out_ref):
-    peers, _, _, channels = out_ref.shape
-    for peer in range(peers):
-        part = jnp.dot(
-            tokens_ref[...], w_ref[0, :, peer * channels : (peer + 1) * channels], preferred_element_type=jnp.float32
-        )
-        out_ref[peer, 0] = encode(part)
+def project_kernel(tokens_ref, w_ref, query_ref, out_ref):
+    peers, kinds, _, channels = out_ref.shape
+    for kind in range(kinds + 1):
+        for peer in range(peers):
+            columns = w_ref[kind, :, peer * channels : (peer + 1) * channels]
+            part = encode(jnp.dot(tokens_ref[...], columns, preferred_element_type=jnp.float32))
+            if kind == 0:
+                query_ref[peer] = part
+            else:
+                out_ref[peer, kind - 1] = part
 
 
 def project(tokens, weights, peers):
-    kinds, depth, wide = weights.shape
+    kinds, _, wide = weights.shape
     rows, channels = tokens.shape[0], wide // peers
     return pl.pallas_call(
         project_kernel,
-        grid=(kinds,),
-        in_specs=[
-            pl.BlockSpec((rows, depth), lambda kind: (0, 0)),
-            pl.BlockSpec((1, depth, wide), lambda kind: (kind, 0, 0)),
+        in_specs=[VMEM, VMEM],
+        out_specs=[VMEM, VMEM],
+        out_shape=[
+            jax.ShapeDtypeStruct((peers, rows, channels), jnp.bfloat16),
+            jax.ShapeDtypeStruct((peers, kinds - 1, rows, channels), jnp.bfloat16),
         ],
-        out_specs=pl.BlockSpec((peers, 1, rows, channels), lambda kind: (0, kind, 0, 0)),
-        out_shape=jax.ShapeDtypeStruct((peers, kinds, rows, channels), jnp.bfloat16),
         compiler_params=PARAMS,
         name="project",
     )(tokens, weights)
@@ -63,6 +65,8 @@
             flat_ref[...] = taps_ref[...] * TAP_SCALE
         for j in range(2):
             packed_ref[pl.ds(2 * kind + j, half, stride=8), :] = flat_ref[pl.ds(j, half, stride=2), :]
+    for j in range(2 * kinds + 2, 8):
+        packed_ref[pl.ds(j, half, stride=8), :] = jnp.zeros((half, packed_ref.shape[1]), jnp.float32)
     out_ref[...] = encode(packed_ref[...])
 
 
@@ -108,11 +112,11 @@
 
     def mixed(kind, j):
         block = now_ref[pl.ds(2 * kind + j, rows, stride=8), :] * (1.0 / PROJ_SCALE)
-        weights = [short[tap][kind : kind + 1, j : j + 1] for tap in range(3)]
+        weights = [short[tap][kind + 1 : kind + 2, j : j + 1] for tap in range(3)]
         return weights[0] * block + weights[1] * delayed(block, 1) + weights[2] * delayed(block, 2)
 
-    signal = [mixed(1, j) * mixed(2, j) for j in range(2)]
-    taps = [now_ref[pl.ds(6 + j, rows, stride=8), :] * (1.0 / TAP_SCALE) for j in range(2)]
+    signal = [mixed(0, j) * mixed(1, j) for j in range(2)]
+    taps = [now_ref[pl.ds(4 + j, rows, stride=8), :] * (1.0 / TAP_SCALE) for j in range(2)]
     data = jnp.concatenate(signal + taps, axis=1)
     spread = dot3((first_ref[0], first_ref[1]), split(data))
     t_re, t_im = twist_ref[0], twist_ref[1]
@@ -136,9 +140,8 @@
     stacked = jnp.concatenate([jnp.concatenate(real, axis=1), jnp.concatenate(imag, axis=1)], axis=0)
     convolved = dot3((last_ref[0], last_ref[1]), split(stacked))
     for j in range(2):
-        gated = mixed(0, j) * (convolved[:, j * cols : (j + 1) * cols] + skip[:, j : j + 1] * signal[j])
-        mix_ref[pl.ds(j, rows, stride=2), :] = gated
-    out_ref[...] = mix_ref[...].astype(jnp.bfloat16)
+        mix_ref[pl.ds(j, rows, stride=2), :] = convolved[:, j * cols : (j + 1) * cols] + skip[:, j : j + 1] * signal[j]
+    out_ref[...] = (mix_ref[...] * jnp.abs(mix_ref[...])).astype(jnp.bfloat16)
 
 
 def tables(rows, cols):
@@ -174,35 +177,91 @@
     )(code, short, skip, *tables(rows, cols))
 
 
+def sum_query_kernel(*refs):
+    *piece_refs, out_ref, edge_ref = refs
+    rows = out_ref.shape[0]
+    total = decode(piece_refs[0][:rows])
+    for piece_ref in piece_refs[1:]:
+        total = total + decode(piece_ref[:rows])
+    out_ref[...] = total * (1.0 / PROJ_SCALE)
+    edge_ref[...] = out_ref[rows - 8 :]
+
+
+def sum_query(pieces, rows):
+    channels = pieces[0].shape[1]
+    return pl.pallas_call(
+        sum_query_kernel,
+        in_specs=[VMEM] * len(pieces),
+        out_specs=[VMEM, VMEM],
+        out_shape=[
+            jax.ShapeDtypeStruct((rows, channels), jnp.float32),
+            jax.ShapeDtypeStruct((8, channels), jnp.float32),
+        ],
+        compiler_params=PARAMS,
+        name="sum_query",
+    )(*pieces)
+
+
+def mix_query_kernel(edge_ref, query_ref, short_ref, out_ref):
+    rows = query_ref.shape[0]
+    wide = jnp.concatenate([edge_ref[...], query_ref[...]], axis=0)
+    total = short_ref[0, 0:1] * query_ref[...]
+    for tap in range(1, 3):
+        total = total + short_ref[tap, 0:1] * pltpu.roll(wide, tap, 0)[8 : 8 + rows]
+    out_ref[...] = total.T
+
+
+def mix_query(edge, query, short):
+    return pl.pallas_call(
+        mix_query_kernel,
+        in_specs=[VMEM] * 3,
+        out_specs=VMEM,
+        out_shape=jax.ShapeDtypeStruct(query.shape[::-1], jnp.float32),
+        compiler_params=PARAMS,
+        name="mix_query",
+    )(edge, query, short)
+
+
+def gate_kernel(code_ref, query_ref, out_ref):
+    wide = code_ref[...].astype(jnp.float32)
+    out_ref[...] = (query_ref[...] * (wide * lax.rsqrt(jnp.maximum(jnp.abs(wide), TINY)))).astype(jnp.bfloat16)
+
+
+def gate(code, query):
+    return pl.pallas_call(
+        gate_kernel,
+        in_specs=[VMEM] * 2,
+        out_specs=VMEM,
+        out_shape=jax.ShapeDtypeStruct(query.shape, jnp.bfloat16),
+        compiler_params=PARAMS,
+        name="gate",
+    )(code, query)
+
+
 def output_kernel(gated_ref, *refs):
     *w_refs, out_ref = refs
     index = lax.axis_index("fsdp")
-    channels = w_refs[0].shape[1]
+    features, channels = out_ref.shape[1], w_refs[0].shape[1]
     total = 0.0
     for step, w_ref in enumerate(w_refs):
         start = pl.multiple_of((index ^ step) * channels, channels)
-        total = total + jnp.dot(w_ref[...], gated_ref[pl.ds(start, channels), :], preferred_element_type=jnp.float32)
+        total = total + jnp.dot(w_ref[w_ref.shape[0] - features :], gated_ref[pl.ds(start, channels), :], preferred_element_type=jnp.float32)
     out_ref[...] = total.T
 
 
-def output(gated, columns):
+def output(gated, pieces, features):
     return pl.pallas_call(
         output_kernel,
-        in_specs=[VMEM] + [VMEM] * len(columns),
-        out_specs=VMEM,
-        out_shape=jax.ShapeDtypeStruct((gated.shape[1], columns[0].shape[0]), jnp.float32),
+        in_specs=[VMEM] + [VMEM] * len(pieces),
+        out_specs=VMEM,
+        out_shape=jax.ShapeDtypeStruct((gated.shape[1], features), jnp.float32),
         compiler_params=PARAMS,
         name="output",
-    )(gated, *columns)
-
-
-def exchanged(shares, axis):
-    index = lax.axis_index(axis)
-    peers = shares.shape[0]
-    pieces = [lax.dynamic_index_in_dim(shares, index ^ step, 0, keepdims=False) for step in range(peers)]
-    return pieces[:1] + [
-        lax.ppermute(pieces[step], axis, [(i, i ^ step) for i in range(peers)]) for step in range(1, peers)
-    ]
+    )(gated, *pieces)
+
+
+def exchanged(piece, axis, step):
+    return lax.ppermute(piece, axis, [(i, i ^ step) for i in range(lax.axis_size(axis))])
 
 
 def on_device(tokens, w_in, short_w, long_filter, skip_gain, w_out):
@@ -210,16 +269,27 @@
     fsdp_count = lax.axis_size("fsdp")
     channels, local_tok = long_filter.shape
     scaled = tokens * jnp.bfloat16(PROJ_SCALE)
-    partial = project(scaled, w_in.transpose(1, 0, 2), fsdp_count)
+    query_parts, partial = project(scaled, w_in.transpose(1, 0, 2), fsdp_count)
     parts = lax.all_to_all(partial, "fsdp", 0, 0, tiled=True)
+    parts, query_parts, w_out = lax.optimization_barrier((parts, query_parts, w_out))
+    features = w_out.shape[0] // fsdp_count
+    fsdp_index = lax.axis_index("fsdp")
+    shares = [lax.dynamic_index_in_dim(query_parts, fsdp_index ^ step, 0, keepdims=False) for step in range(4)]
+    rows = [lax.dynamic_slice_in_dim(w_out, (fsdp_index ^ step) * features, features, 0) for step in range(4)]
+    pieces = [shares[0], exchanged(jnp.concatenate([shares[1], rows[1]], axis=0), "fsdp", 1)]
+    pieces += [exchanged(shares[step], "fsdp", step) for step in range(2, 4)]
     packed = pack(parts, long_filter).reshape(seq_count, -1, local_tok)
     whole = lax.all_to_all(packed, "seq", 0, 0, tiled=True).reshape(-1, local_tok)
-    gated = convolve(whole, short_w, skip_gain.reshape(1, -1), seq_count, local_tok)
-    gated, w_out = lax.optimization_barrier((gated, w_out))
-    columns = exchanged(w_out.reshape(fsdp_count, -1, channels), "fsdp")
-    home = lax.all_to_all(gated.reshape(seq_count, 2, local_tok), "seq", 0, 0, tiled=True)
-    gathered = lax.all_gather(home.reshape(channels, local_tok), "fsdp", axis=0, tiled=True)
-    return output(gathered, columns)
+    coded = convolve(whole, short_w, skip_gain.reshape(1, -1), seq_count, local_tok)
+    coded, pieces, rows = lax.optimization_barrier((coded, pieces, rows))
+    query, edge = sum_query(pieces, local_tok)
+    edge = lax.ppermute(edge, "seq", [(i, i + 1) for i in range(seq_count - 1)])
+    query = mix_query(edge, query, short_w)
+    columns = [rows[0], pieces[1]] + [exchanged(rows[step], "fsdp", step) for step in range(2, 4)]
+    home = lax.all_to_all(coded.reshape(seq_count, 2, local_tok), "seq", 0, 0, tiled=True)
+    gated = gate(home.reshape(channels, local_tok), query)
+    gathered = lax.all_gather(gated, "fsdp", axis=0, tiled=True)
+    return output(gathered, columns, features)
 
 
 def solution(mesh):

time: 97.8 us -> 95.5 us (0.976)
  blocking collectives: 67.6 us -> 28.9 us
  starting transfers between devices: 19.1 us -> 46.2 us
  waiting for transfers between devices: 3.38 us -> 12 us
    all_to_all x1 -> x0, blocking collectives: 35.9 us -> none  [on_device(): lax.all_to_all(packed, 'seq', 0, 0, tiled=True).reshape(-1, local_tok)]
    all_to_all x1 -> x2, starting transfers between devices: 8.4 us -> 24.5 us  [the longest x1 16.1 us: on_device(): lax.all_to_all(packed, 'seq', 0, 0, tiled=True).reshape(-1, local_tok)]
    ppermute x3 -> x6, starting transfers between devices: 10.7 us -> 21.6 us  [the longest x5 19 us: exchanged(): lax.ppermute(piece, axis, [(i, i ^ step) for i in range(lax.axis_size(axi...]
    all_to_all x1 -> x2, waiting for transfers between devices: 3.37 us -> 11.2 us  [the longest x1 9.6 us: on_device(): lax.all_to_all(packed, 'seq', 0, 0, tiled=True).reshape(-1, local_tok)]
    all_to_all x1, blocking collectives: 21.5 us -> 18.7 us  [on_device(): parts = lax.all_to_all(partial, 'fsdp', 0, 0, tiled=True)]
  transfers between devices with their start and end apart: 4 -> 8, of which waited for: 1 -> 3; matrix products, arithmetic and copies ran while one was open for 0% -> 0% of each run, Pallas kernels for 0% -> 3%
where the time goes in v4:
time: 95.5 us; the launch traced here: 95 us
  starting transfers between devices  46.2 us (48%)
  blocking collectives  28.9 us (30%)
  waiting for transfers between devices  12 us (13%)
  Pallas kernels  5.31 us (6%)
  local copies, waits for them, and re-layouts  1.53 us (2%)
    ppermute x5, starting transfers between devices, exchanged(): lax.ppermute(piece, axis, [(i, i ^ step) for i in range(lax.axis_size(axi...  19 us
    all_to_all x1, blocking collectives, on_device(): parts = lax.all_to_all(partial, 'fsdp', 0, 0, tiled=True)  18.7 us
    all_to_all x1, starting transfers between devices, on_device(): lax.all_to_all(packed, 'seq', 0, 0, tiled=True).reshape(-1, local_tok)  16.1 us
    all_gather x1, blocking collectives, on_device(): gathered = lax.all_gather(gated, 'fsdp', axis=0, tiled=True)  10.2 us
    all_to_all x1, waiting for transfers between devices, on_device(): lax.all_to_all(packed, 'seq', 0, 0, tiled=True).reshape(-1, local_tok)  9.6 us
    all_to_all x1, starting transfers between devices, on_device(): lax.all_to_all(coded.reshape(seq_count, 2, local_tok), 'seq', 0, 0, tiled...  8.41 us
    ppermute x1, starting transfers between devices, on_device(): edge = lax.ppermute(edge, 'seq', [(i, i + 1) for i in range(seq_count - 1)])  2.67 us
    pallas_call x1, Pallas kernels, convolve(): pl.pallas_call(convolve_kernel, in_specs=[VMEM] * 8, out_specs=VMEM, out_...  2.33 us
  transfers between devices with their start and end apart: 8, of which 3 were waited for; matrix products, arithmetic and copies ran while one was open for 0% of the time, Pallas kernels for 3%

profile of v4, /device:TPU:1, one launch (start us, length us, event | category | flops | bytes accessed | tf_op | source)
XLA Modules:
  0.0 95.0 jit_solution(12102298350139745425)
XLA Ops:
  0.0 0.0 copy-start.3
  0.0 0.9 broadcast_multiply_fusion.tokens_ref
  0.9 0.0 copy-start
  0.9 1.4 %copy-done = bf16[256,3,1024]{2,0,1:T(8,128)(2,1)S(1)} copy-done((bf16[256,3,1024]{2,0,1:T(8,128)(2,1)S(1)}, bf16[256,3,1024]{2,0,1:T(8,128)(2,1)}, u32[]{:S(2)}) %copy-start) | copy-done | bytes 1572888
  2.3 0.4 project.1
  2.7 0.0 copy-start.9
  2.7 18.7 %all_to_all.15.parts_ref = bf16[4,2,128,256]{3,2,1,0:T(8,128)(2,1)S(1)} all-to-all(bf16[4,2,128,256]{3,2,1,0:T(8,128)(2,1)S(1)} %get-tuple-element.20), channel_id=1, replica_groups=mesh['seq'=128,'fsdp'=4] {'fsdp'}, dimensions={0} | all-to-all | bytes 1048576 | tf_op jit(solution)/shard_map/all_to_all | solution.py:273
  21.5 0.0 copy-done.3
  21.5 0.0 copy-start.1
  21.5 0.0 copy-start.2
  21.5 0.0 copy-start.4
  21.5 0.0 copy-start.5
  21.5 0.0 copy-start.6
  21.5 0.0 copy-start.7
  21.5 0.0 copy-start.8
  21.5 1.2 %pack.1 = bf16[1024,128]{1,0:T(8,128)(2,1)} custom-call(bf16[4,2,128,256]{3,2,1,0:T(8,128)(2,1)S(1)} %all_to_all.15.parts_ref, f32[256,128]{1,0:T(8,128)S(1)} %copy-done.3), custom_call_target="tpu_custom_call" | custom-call | tf_op jit(solution)/shard_map/pack/pallas_call | solution.py:75
  22.7 16.1 %all-to-all-start.1 = ((bf16[128,8,128]{2,1,0:T(8,128)(2,1)}), bf16[128,8,128]{2,1,0:T(8,128)(2,1)S(1)}, u32[]{:S(2)}, u32[]{:S(2)}) async-start(bf16[128,8,128]{2,1,0:T(8,128)(2,1)} %bitcast.1), calls=%async_computation.1 | async-start | bytes 524288 | tf_op jit(solution)/shard_map/all_to_all | solution.py:282
  38.9 0.0 copy-done.9
  39.0 3.2 %collective-permute-start = (bf16[384,256]{1,0:T(8,128)(2,1)S(1)}, bf16[384,256]{1,0:T(8,128)(2,1)S(1)}, u32[]{:S(2)}, u32[]{:S(2)}) collective-permute-start(bf16[384,256]{1,0:T(8,128)(2,1)S(1)} %pad_maximum_fusion), channel_id=1, source_target_pairs={{0,1},{1,0},{2,3},{3,2},{4,5},{5,4},{6,7},{7,6},{8,9},{9,8},{10,11... | collective-permute-start | bytes 589832 | tf_op jit(solution)/shard_map/ppermute | solution.py:264
  42.2 2.6 %collective-permute-start.1 = (bf16[128,256]{1,0:T(8,128)(2,1)S(1)}, bf16[128,256]{1,0:T(8,128)(2,1)S(1)}, u32[]{:S(2)}, u32[]{:S(2)}) collective-permute-start(bf16[128,256]{1,0:T(8,128)(2,1)S(1)} %get-tuple-element.40), channel_id=1, source_target_pairs={{0,2},{1,3},{2,0},{3,1},{4,6},{5,7},{6,4},{7,5},{8,10},{9,11},{10,... | collective-permute-start | bytes 196616 | tf_op jit(solution)/shard_map/ppermute | solution.py:264
  44.8 4.4 %collective-permute-start.2 = (bf16[128,256]{1,0:T(8,128)(2,1)S(1)}, bf16[128,256]{1,0:T(8,128)(2,1)S(1)}, u32[]{:S(2)}, u32[]{:S(2)}) collective-permute-start(bf16[128,256]{1,0:T(8,128)(2,1)S(1)} %get-tuple-element.39), channel_id=1, source_target_pairs={{0,3},{1,2},{2,1},{3,0},{4,7},{5,6},{6,5},{7,4},{8,11},{9,10},{10,... | collective-permute-start | bytes 196616 | tf_op jit(solution)/shard_map/ppermute | solution.py:264
  49.2 9.6 %all-to-all-done.1 = bf16[128,8,128]{2,1,0:T(8,128)(2,1)S(1)} async-done(((bf16[128,8,128]{2,1,0:T(8,128)(2,1)}), bf16[128,8,128]{2,1,0:T(8,128)(2,1)S(1)}, u32[]{:S(2)}, u32[]{:S(2)}) %all-to-all-start.1) | async-done | bytes 262176 | tf_op jit(solution)/shard_map/all_to_all | solution.py:282
  58.8 0.0 copy-done.1
  58.8 0.0 copy-done.2
  58.8 0.0 copy-done.4
  58.8 0.0 copy-done.5
  58.8 0.0 copy-done.6
  58.8 0.0 copy-done.7
  58.8 0.0 copy-done.8
  58.9 2.3 %convolve.1 = bf16[256,128]{1,0:T(8,128)(2,1)} custom-call(bf16[1024,128]{1,0:T(8,128)(2,1)S(1)} %bitcast.15, f32[3,3,256]{2,1,0:T(4,128)S(1)} %copy-done.7, f32[1,256]{1,0:T(1,128)S(1)} %bitcast.17, bf16[2,256,128]{2,1,0:T(8,128)(2,1)S(1)} %copy-done.4, f32[2,128,128]{2,1,0:T(8,128)S(1)} %copy-done.5, bf16[2,256,256]{2,1,0:T(8,128)(2,1)S(1)} %copy-done.1, ...), custom_call_target="tpu_custom_call" | custom-call | tf_op jit(solution)/shard_map/convolve/pallas_call | solution.py:169
  61.2 0.0 collective-permute-done.1.refs_2_
  61.2 0.0 collective-permute-done.2.refs_3_
  61.2 0.0 collective-permute-done.refs_1_
  61.2 8.4 %all-to-all-start.2 = ((bf16[128,2,128]{2,1,0:T(2,128)(2,1)}), bf16[128,2,128]{2,1,0:T(2,128)(2,1)S(1)}, u32[]{:S(2)}, u32[]{:S(2)}) async-start(bf16[128,2,128]{2,1,0:T(2,128)(2,1)} %bitcast.8), calls=%async_computation.2 | async-start | bytes 131072 | tf_op jit(solution)/shard_map/all_to_all | solution.py:289
  69.6 4.3 %collective-permute-start.4 = (bf16[256,256]{1,0:T(8,128)(2,1)S(1)}, bf16[256,256]{1,0:T(8,128)(2,1)S(1)}, u32[]{:S(2)}, u32[]{:S(2)}) collective-permute-start(bf16[256,256]{1,0:T(8,128)(2,1)S(1)} %get-tuple-element.33), channel_id=1, source_target_pairs={{0,2},{1,3},{2,0},{3,1},{4,6},{5,7},{6,4},{7,5},{8,10},{9,11},{10,... | collective-permute-start | bytes 393224 | tf_op jit(solution)/shard_map/ppermute | solution.py:264
  73.9 4.5 %collective-permute-start.5 = (bf16[256,256]{1,0:T(8,128)(2,1)S(1)}, bf16[256,256]{1,0:T(8,128)(2,1)S(1)}, u32[]{:S(2)}, u32[]{:S(2)}) collective-permute-start(bf16[256,256]{1,0:T(8,128)(2,1)S(1)} %get-tuple-element.34), channel_id=1, source_target_pairs={{0,3},{1,2},{2,1},{3,0},{4,7},{5,6},{6,5},{7,4},{8,11},{9,10},{10,... | collective-permute-start | bytes 393224 | tf_op jit(solution)/shard_map/ppermute | solution.py:264
  78.4 0.2 sum_query.1
  78.6 2.7 %collective-permute-start.3 = (f32[8,256]{1,0:T(8,128)S(1)}, f32[8,256]{1,0:T(8,128)S(1)}, u32[]{:S(2)}, u32[]{:S(2)}) collective-permute-start(f32[8,256]{1,0:T(8,128)S(1)} %get-tuple-element.30), channel_id=1, source_target_pairs={{0,4},{4,8},{8,12},{12,16},{16,20},{20,24},{24,28},{28,32},{32,36}... | collective-permute-start | bytes 24584 | tf_op jit(solution)/shard_map/ppermute | solution.py:286
  81.3 0.8 collective-permute-done.3.edge_ref
  82.1 0.1 mix_query.1.query_ref
  82.2 1.6 %all-to-all-done.2 = bf16[128,2,128]{2,1,0:T(2,128)(2,1)S(1)} async-done(((bf16[128,2,128]{2,1,0:T(2,128)(2,1)}), bf16[128,2,128]{2,1,0:T(2,128)(2,1)S(1)}, u32[]{:S(2)}, u32[]{:S(2)}) %all-to-all-start.2) | async-done | bytes 65568 | tf_op jit(solution)/shard_map/all_to_all | solution.py:289
  83.8 10.2 %all_gather.3.gated_ref = bf16[1024,128]{1,0:T(8,128)(2,1)S(1)} all-gather(bf16[256,128]{1,0:T(8,128)(2,1)S(1)} %gate.1), channel_id=1, replica_groups=mesh['seq'=128,'fsdp'=4] {'fsdp'}, dimensions={0}, use_global_device_ids=true | all-gather | bytes 327680 | tf_op jit(solution)/shard_map/all_gather | solution.py:291
  94.0 0.0 collective-permute-done.4.refs_2_
  94.0 0.0 collective-permute-done.5.refs_3_
  94.0 1.0 %output.1 = f32[128,256]{1,0:T(8,128)} custom-call(bf16[1024,128]{1,0:T(8,128)(2,1)S(1)} %all_gather.3.gated_ref, bf16[256,256]{1,0:T(8,128)(2,1)S(1)} %get-tuple-element.32.refs_0_, bf16[384,256]{1,0:T(8,128)(2,1)S(1)} %collective-permute-done.refs_1_, bf16[256,256]{1,0:T(8,128)(2,1)S(1)} %collective-permute-done.4.refs_2_, ...), custom_call_target="tpu_custom_call" | custom-call | tf_op jit(solution)/shard_map/output/pallas_call | solution.py:253
  (4 shorter events, 0.1 us)
Async XLA Ops:
  0.0 21.5 %copy-start.3 = (f32[256,128]{1,0:T(8,128)S(1)}, f32[256,128]{1,0:T(8,128)}, u32[]{:S(2)}) copy-start(f32[256,128]{1,0:T(8,128)} %taps_ref.1) | copy-start | bytes 393220
  0.9 1.4 %copy-start = (bf16[256,3,1024]{2,0,1:T(8,128)(2,1)S(1)}, bf16[256,3,1024]{2,0,1:T(8,128)(2,1)}, u32[]{:S(2)}) copy-start(bf16[256,3,1024]{2,0,1:T(8,128)(2,1)} %param.12) | copy-start | bytes 4718596
  2.7 36.2 %copy-start.9 = (bf16[1024,256]{1,0:T(8,128)(2,1)S(1)}, bf16[1024,256]{1,0:T(8,128)(2,1)}, u32[]{:S(2)}) copy-start(bf16[1024,256]{1,0:T(8,128)(2,1)} %param.16) | copy-start | bytes 1572868
  21.5 37.4 %copy-start.1 = (bf16[2,256,256]{2,1,0:T(8,128)(2,1)S(1)}, bf16[2,256,256]{2,1,0:T(8,128)(2,1)}, u32[]{:S(2)}) copy-start(bf16[2,256,256]{2,1,0:T(8,128)(2,1)} %constant.41.clone.mid_ref) | copy-start | bytes 786436
  21.5 37.4 %copy-start.2 = (bf16[2,256,256]{2,1,0:T(8,128)(2,1)S(1)}, bf16[2,256,256]{2,1,0:T(8,128)(2,1)}, u32[]{:S(2)}) copy-start(bf16[2,256,256]{2,1,0:T(8,128)(2,1)} %constant.42.clone.inv_ref) | copy-start | bytes 786436
  21.5 37.4 %copy-start.4 = (bf16[2,256,128]{2,1,0:T(8,128)(2,1)S(1)}, bf16[2,256,128]{2,1,0:T(8,128)(2,1)}, u32[]{:S(2)}) copy-start(bf16[2,256,128]{2,1,0:T(8,128)(2,1)} %constant.39.clone.first_ref) | copy-start | bytes 393220
  21.5 37.4 %copy-start.5 = (f32[2,128,128]{2,1,0:T(8,128)S(1)}, f32[2,128,128]{2,1,0:T(8,128)}, u32[]{:S(2)}) copy-start(f32[2,128,128]{2,1,0:T(8,128)} %constant.40.clone.twist_ref) | copy-start | bytes 393220
  21.5 37.3 %copy-start.6 = (bf16[2,128,256]{2,1,0:T(8,128)(2,1)S(1)}, bf16[2,128,256]{2,1,0:T(8,128)(2,1)}, u32[]{:S(2)}) copy-start(bf16[2,128,256]{2,1,0:T(8,128)(2,1)} %constant.43.clone.last_ref) | copy-start | bytes 393220
  21.5 37.3 %copy-start.7 = (f32[3,3,256]{2,1,0:T(4,128)S(1)}, f32[3,3,256]{2,1,0:T(4,128)}, u32[]{:S(2)}) copy-start(f32[3,3,256]{2,1,0:T(4,128)} %short_ref.3) | copy-start | bytes 27652
  21.5 37.3 %copy-start.8 = (f32[256]{0:T(256)S(1)}, f32[256]{0:T(256)}, u32[]{:S(2)}) copy-start(f32[256]{0:T(256)} %param.15) | copy-start | bytes 3076
  22.7 36.1 %all-to-all-start.1 = ((bf16[128,8,128]{2,1,0:T(8,128)(2,1)}), bf16[128,8,128]{2,1,0:T(8,128)(2,1)S(1)}, u32[]{:S(2)}, u32[]{:S(2)}) async-start(bf16[128,8,128]{2,1,0:T(8,128)(2,1)} %bitcast.1), calls=%async_computation.1 | async-start | bytes 524288 | tf_op jit(solution)/shard_map/all_to_all | solution.py:282
  39.0 22.2 %collective-permute-start = (bf16[384,256]{1,0:T(8,128)(2,1)S(1)}, bf16[384,256]{1,0:T(8,128)(2,1)S(1)}, u32[]{:S(2)}, u32[]{:S(2)}) collective-permute-start(bf16[384,256]{1,0:T(8,128)(2,1)S(1)} %pad_maximum_fusion), channel_id=1, source_target_pairs={{0,1},{1,0},{2,3},{3,2},{4,5},{5,4},{6,7},{7,6},{8,9},{9,8},{10,11... | collective-permute-start | bytes 589832 | tf_op jit(solution)/shard_map/ppermute | solution.py:264
  42.2 19.0 %collective-permute-start.1 = (bf16[128,256]{1,0:T(8,128)(2,1)S(1)}, bf16[128,256]{1,0:T(8,128)(2,1)S(1)}, u32[]{:S(2)}, u32[]{:S(2)}) collective-permute-start(bf16[128,256]{1,0:T(8,128)(2,1)S(1)} %get-tuple-element.40), channel_id=1, source_target_pairs={{0,2},{1,3},{2,0},{3,1},{4,6},{5,7},{6,4},{7,5},{8,10},{9,11},{10,... | collective-permute-start | bytes 196616 | tf_op jit(solution)/shard_map/ppermute | solution.py:264
  44.8 16.4 %collective-permute-start.2 = (bf16[128,256]{1,0:T(8,128)(2,1)S(1)}, bf16[128,256]{1,0:T(8,128)(2,1)S(1)}, u32[]{:S(2)}, u32[]{:S(2)}) collective-permute-start(bf16[128,256]{1,0:T(8,128)(2,1)S(1)} %get-tuple-element.39), channel_id=1, source_target_pairs={{0,3},{1,2},{2,1},{3,0},{4,7},{5,6},{6,5},{7,4},{8,11},{9,10},{10,... | collective-permute-start | bytes 196616 | tf_op jit(solution)/shard_map/ppermute | solution.py:264
  61.2 22.6 %all-to-all-start.2 = ((bf16[128,2,128]{2,1,0:T(2,128)(2,1)}), bf16[128,2,128]{2,1,0:T(2,128)(2,1)S(1)}, u32[]{:S(2)}, u32[]{:S(2)}) async-start(bf16[128,2,128]{2,1,0:T(2,128)(2,1)} %bitcast.8), calls=%async_computation.2 | async-start | bytes 131072 | tf_op jit(solution)/shard_map/all_to_all | solution.py:289
  69.6 24.4 %collective-permute-start.4 = (bf16[256,256]{1,0:T(8,128)(2,1)S(1)}, bf16[256,256]{1,0:T(8,128)(2,1)S(1)}, u32[]{:S(2)}, u32[]{:S(2)}) collective-permute-start(bf16[256,256]{1,0:T(8,128)(2,1)S(1)} %get-tuple-element.33), channel_id=1, source_target_pairs={{0,2},{1,3},{2,0},{3,1},{4,6},{5,7},{6,4},{7,5},{8,10},{9,11},{10,... | collective-permute-start | bytes 393224 | tf_op jit(solution)/shard_map/ppermute | solution.py:264
  73.9 20.2 %collective-permute-start.5 = (bf16[256,256]{1,0:T(8,128)(2,1)S(1)}, bf16[256,256]{1,0:T(8,128)(2,1)S(1)}, u32[]{:S(2)}, u32[]{:S(2)}) collective-permute-start(bf16[256,256]{1,0:T(8,128)(2,1)S(1)} %get-tuple-element.34), channel_id=1, source_target_pairs={{0,3},{1,2},{2,1},{3,0},{4,7},{5,6},{6,5},{7,4},{8,11},{9,10},{10,... | collective-permute-start | bytes 393224 | tf_op jit(solution)/shard_map/ppermute | solution.py:264
  78.6 3.5 %collective-permute-start.3 = (f32[8,256]{1,0:T(8,128)S(1)}, f32[8,256]{1,0:T(8,128)S(1)}, u32[]{:S(2)}, u32[]{:S(2)}) collective-permute-start(f32[8,256]{1,0:T(8,128)S(1)} %get-tuple-element.30), channel_id=1, source_target_pairs={{0,4},{4,8},{8,12},{12,16},{16,20},{20,24},{24,28},{28,32},{32,36}... | collective-permute-start | bytes 24584 | tf_op jit(solution)/shard_map/ppermute | solution.py:286

commit v5 on v4

--- a/solution.py
+++ b/solution.py
@@ -1,3 +1,5 @@
+import functools
+
 import jax
 import jax.numpy as jnp
 import numpy as np
@@ -24,37 +26,80 @@
     return jnp.where(wide < 0, -root, root)
 
 
-def project_kernel(tokens_ref, w_ref, query_ref, out_ref):
+def project_kernel(first, tokens_hbm, w_hbm, out_ref, tokens_ref, w_ref, sems):
     peers, kinds, _, channels = out_ref.shape
-    for kind in range(kinds + 1):
+    parts = (sems.shape[0] - 1) // kinds
+    depth = w_ref.shape[1] // parts
+
+    def piece(kind, part):
+        cut = pl.ds(part * depth, depth)
+        return pltpu.make_async_copy(w_hbm.at[first + kind, cut], w_ref.at[kind, cut], sems.at[kind * parts + part])
+
+    tokens_copy = pltpu.make_async_copy(tokens_hbm, tokens_ref, sems.at[kinds * parts])
+    tokens_copy.start()
+    for kind in range(kinds):
+        for part in range(parts):
+            piece(kind, part).start()
+    tokens_copy.wait()
+    scaled = tokens_ref[...] * jnp.bfloat16(PROJ_SCALE)
+    for kind in range(kinds):
+        for part in range(parts):
+            piece(kind, part).wait()
         for peer in range(peers):
             columns = w_ref[kind, :, peer * channels : (peer + 1) * channels]
-            part = encode(jnp.dot(tokens_ref[...], columns, preferred_element_type=jnp.float32))
-            if kind == 0:
-                query_ref[peer] = part
-            else:
-                out_ref[peer, kind - 1] = part
-
-
-def project(tokens, weights, peers):
-    kinds, _, wide = weights.shape
+            out_ref[peer, kind] = encode(jnp.dot(scaled, columns, preferred_element_type=jnp.float32))
+
+
+def project(tokens, weights, first, kinds, peers):
+    _, depth, wide = weights.shape
     rows, channels = tokens.shape[0], wide // peers
     return pl.pallas_call(
-        project_kernel,
-        in_specs=[VMEM, VMEM],
-        out_specs=[VMEM, VMEM],
+        functools.partial(project_kernel, first),
+        in_specs=[pl.BlockSpec(memory_space=pltpu.HBM)] * 2,
+        out_specs=VMEM,
+        out_shape=jax.ShapeDtypeStruct((peers, kinds, rows, channels), jnp.bfloat16),
+        scratch_shapes=[
+            pltpu.VMEM(tokens.shape, tokens.dtype),
+            pltpu.VMEM((kinds, depth, wide), weights.dtype),
+            pltpu.SemaphoreType.DMA((4 * kinds + 1,)),
+        ],
+        compiler_params=PARAMS,
+        name="project",
+    )(pltpu.with_memory_space_constraint(tokens, pltpu.HBM), pltpu.with_memory_space_constraint(weights, pltpu.HBM))
+
+
+def project_query_kernel(tokens_ref, w_ref, w_out_ref, own_ref, bundle_ref):
+    peers, rows, channels = own_ref.shape
+    features = w_out_ref.shape[0] // peers
+    mate = 1 - lax.rem(lax.axis_index("fsdp"), 2)
+    scaled = tokens_ref[...] * jnp.bfloat16(PROJ_SCALE)
+    for peer in range(peers):
+        columns = w_ref[0, :, peer * channels : (peer + 1) * channels]
+        own_ref[peer] = encode(jnp.dot(scaled, columns, preferred_element_type=jnp.float32))
+    for chip in range(peers // 2):
+        start = pl.multiple_of((2 * chip + mate) * features, features)
+        bundle_ref[chip * rows : (chip + 1) * rows] = own_ref[2 * chip + mate]
+        bundle_ref[2 * rows + chip * features : 2 * rows + (chip + 1) * features] = w_out_ref[pl.ds(start, features), :]
+
+
+def project_query(tokens, weights, w_out, peers):
+    rows, channels = tokens.shape[0], weights.shape[2] // peers
+    return pl.pallas_call(
+        project_query_kernel,
+        in_specs=[VMEM] * 3,
+        out_specs=[VMEM] * 2,
         out_shape=[
             jax.ShapeDtypeStruct((peers, rows, channels), jnp.bfloat16),
-            jax.ShapeDtypeStruct((peers, kinds - 1, rows, channels), jnp.bfloat16),
-        ],
-        compiler_params=PARAMS,
-        name="project",
-    )(tokens, weights)
+            jax.ShapeDtypeStruct((2 * rows + w_out.shape[0] // 2, channels), jnp.bfloat16),
+        ],
+        compiler_params=PARAMS,
+        name="project_query",
+    )(tokens, weights, w_out)
 
 
 def pack_kernel(parts_ref, taps_ref, out_ref, flat_ref, packed_ref):
     peers, kinds, _, channels = parts_ref.shape
-    half = channels // 2
+    half, chunk = channels // 2, 2 * kinds + 2
     for kind in range(kinds + 1):
         if kind < kinds:
             total = decode(parts_ref[0, kind])
@@ -64,20 +109,22 @@
         else:
             flat_ref[...] = taps_ref[...] * TAP_SCALE
         for j in range(2):
-            packed_ref[pl.ds(2 * kind + j, half, stride=8), :] = flat_ref[pl.ds(j, half, stride=2), :]
-    for j in range(2 * kinds + 2, 8):
-        packed_ref[pl.ds(j, half, stride=8), :] = jnp.zeros((half, packed_ref.shape[1]), jnp.float32)
+            packed_ref[pl.ds(2 * kind + j, half, stride=chunk), :] = flat_ref[pl.ds(j, half, stride=2), :]
     out_ref[...] = encode(packed_ref[...])
 
 
 def pack(parts, taps):
     channels, rows = taps.shape
+    kinds = parts.shape[1] + 1
     return pl.pallas_call(
         pack_kernel,
         in_specs=[VMEM, VMEM],
         out_specs=VMEM,
-        out_shape=jax.ShapeDtypeStruct((4 * channels, rows), jnp.bfloat16),
-        scratch_shapes=[pltpu.VMEM((channels, rows), jnp.float32), pltpu.VMEM((4 * channels, rows), jnp.float32)],
+        out_shape=jax.ShapeDtypeStruct((kinds * channels, rows), jnp.bfloat16),
+        scratch_shapes=[
+            pltpu.VMEM((channels, rows), jnp.float32),
+            pltpu.VMEM((kinds * channels, rows), jnp.float32),
+        ],
         compiler_params=PARAMS,
         name="pack",
     )(parts, taps)
@@ -111,12 +158,12 @@
     skip = pltpu.roll(skip_ref[...], shift, 1)
 
     def mixed(kind, j):
-        block = now_ref[pl.ds(2 * kind + j, rows, stride=8), :] * (1.0 / PROJ_SCALE)
+        block = now_ref[pl.ds(2 * kind + j, rows, stride=6), :] * (1.0 / PROJ_SCALE)
         weights = [short[tap][kind + 1 : kind + 2, j : j + 1] for tap in range(3)]
         return weights[0] * block + weights[1] * delayed(block, 1) + weights[2] * delayed(block, 2)
 
     signal = [mixed(0, j) * mixed(1, j) for j in range(2)]
-    taps = [now_ref[pl.ds(4 + j, rows, stride=8), :] * (1.0 / TAP_SCALE) for j in range(2)]
+    taps = [now_ref[pl.ds(4 + j, rows, stride=6), :] * (1.0 / TAP_SCALE) for j in range(2)]
     data = jnp.concatenate(signal + taps, axis=1)
     spread = dot3((first_ref[0], first_ref[1]), split(data))
     t_re, t_im = twist_ref[0], twist_ref[1]
@@ -171,35 +218,64 @@
         in_specs=[VMEM] * 8,
         out_specs=VMEM,
         out_shape=jax.ShapeDtypeStruct((2 * rows, cols), jnp.bfloat16),
-        scratch_shapes=[pltpu.VMEM((8 * rows, cols), jnp.float32), pltpu.VMEM((2 * rows, cols), jnp.float32)],
+        scratch_shapes=[pltpu.VMEM((6 * rows, cols), jnp.float32), pltpu.VMEM((2 * rows, cols), jnp.float32)],
         compiler_params=PARAMS,
         name="convolve",
     )(code, short, skip, *tables(rows, cols))
 
 
-def sum_query_kernel(*refs):
-    *piece_refs, out_ref, edge_ref = refs
-    rows = out_ref.shape[0]
-    total = decode(piece_refs[0][:rows])
-    for piece_ref in piece_refs[1:]:
-        total = total + decode(piece_ref[:rows])
-    out_ref[...] = total * (1.0 / PROJ_SCALE)
-    edge_ref[...] = out_ref[rows - 8 :]
-
-
-def sum_query(pieces, rows):
-    channels = pieces[0].shape[1]
-    return pl.pallas_call(
-        sum_query_kernel,
-        in_specs=[VMEM] * len(pieces),
+def pair_query_kernel(own_ref, from_mate_ref, keep_ref, send_ref):
+    index = lax.axis_index("fsdp")
+    rows = keep_ref.shape[0]
+
+    def total(peer):
+        start = pl.multiple_of(lax.div(peer, 2) * rows, rows)
+        return decode(own_ref[peer]) + decode(from_mate_ref[pl.ds(start, rows), :])
+
+    keep_ref[...] = total(index)
+    send_ref[...] = encode(total(index ^ 2))
+
+
+def pair_query(own, from_mate):
+    _, rows, channels = own.shape
+    return pl.pallas_call(
+        pair_query_kernel,
+        in_specs=[VMEM, VMEM],
         out_specs=[VMEM, VMEM],
         out_shape=[
             jax.ShapeDtypeStruct((rows, channels), jnp.float32),
+            jax.ShapeDtypeStruct((rows, channels), jnp.bfloat16),
+        ],
+        compiler_params=PARAMS,
+        name="pair_query",
+    )(own, from_mate)
+
+
+def sum_query_kernel(keep_ref, code_ref, w_out_ref, from_mate_ref, out_ref, edge_ref, far_ref):
+    rows, features = out_ref.shape[0], far_ref.shape[0] // 2
+    index = lax.axis_index("fsdp")
+    out_ref[...] = (keep_ref[...] + decode(code_ref[...])) * (1.0 / PROJ_SCALE)
+    edge_ref[...] = out_ref[rows - 8 :]
+    start = pl.multiple_of((index ^ 2) * features, features)
+    far_ref[:features] = w_out_ref[pl.ds(start, features), :]
+    start = pl.multiple_of(2 * rows + (1 - lax.div(index, 2)) * features, features)
+    far_ref[features:] = from_mate_ref[pl.ds(start, features), :]
+
+
+def sum_query(keep, code, w_out, from_mate):
+    rows, channels = keep.shape
+    return pl.pallas_call(
+        sum_query_kernel,
+        in_specs=[VMEM] * 4,
+        out_specs=[VMEM] * 3,
+        out_shape=[
+            jax.ShapeDtypeStruct((rows, channels), jnp.float32),
             jax.ShapeDtypeStruct((8, channels), jnp.float32),
+            jax.ShapeDtypeStruct((w_out.shape[0] // 2, channels), jnp.bfloat16),
         ],
         compiler_params=PARAMS,
         name="sum_query",
-    )(*pieces)
+    )(keep, code, w_out, from_mate)
 
 
 def mix_query_kernel(edge_ref, query_ref, short_ref, out_ref):
@@ -238,26 +314,34 @@
     )(code, query)
 
 
-def output_kernel(gated_ref, *refs):
-    *w_refs, out_ref = refs
+def output_kernel(gated_ref, w_out_ref, from_mate_ref, far_ref, out_ref):
     index = lax.axis_index("fsdp")
-    features, channels = out_ref.shape[1], w_refs[0].shape[1]
+    rows, features = out_ref.shape
+    channels = gated_ref.shape[0] // 4
+    own = pl.multiple_of(index * features, features)
+    mate = pl.multiple_of(2 * rows + lax.div(index, 2) * features, features)
+    columns = [
+        w_out_ref[pl.ds(own, features), :],
+        from_mate_ref[pl.ds(mate, features), :],
+        far_ref[:features],
+        far_ref[features:],
+    ]
     total = 0.0
-    for step, w_ref in enumerate(w_refs):
+    for step, column in enumerate(columns):
         start = pl.multiple_of((index ^ step) * channels, channels)
-        total = total + jnp.dot(w_ref[w_ref.shape[0] - features :], gated_ref[pl.ds(start, channels), :], preferred_element_type=jnp.float32)
+        total = total + jnp.dot(column, gated_ref[pl.ds(start, channels), :], preferred_element_type=jnp.float32)
     out_ref[...] = total.T
 
 
-def output(gated, pieces, features):
+def output(gated, w_out, from_mate, far):
     return pl.pallas_call(
         output_kernel,
-        in_specs=[VMEM] + [VMEM] * len(pieces),
-        out_specs=VMEM,
-        out_shape=jax.ShapeDtypeStruct((gated.shape[1], features), jnp.float32),
+        in_specs=[VMEM] * 4,
+        out_specs=VMEM,
+        out_shape=jax.ShapeDtypeStruct((gated.shape[1], far.shape[0] // 2), jnp.float32),
         compiler_params=PARAMS,
         name="output",
-    )(gated, *pieces)
+    )(gated, w_out, from_mate, far)
 
 
 def exchanged(piece, axis, step):
@@ -268,28 +352,27 @@
     seq_count = lax.axis_size("seq")
     fsdp_count = lax.axis_size("fsdp")
     channels, local_tok = long_filter.shape
-    scaled = tokens * jnp.bfloat16(PROJ_SCALE)
-    query_parts, partial = project(scaled, w_in.transpose(1, 0, 2), fsdp_count)
+    weights = w_in.transpose(1, 0, 2)
+    partial = project(tokens, weights, 1, 2, fsdp_count)
     parts = lax.all_to_all(partial, "fsdp", 0, 0, tiled=True)
-    parts, query_parts, w_out = lax.optimization_barrier((parts, query_parts, w_out))
-    features = w_out.shape[0] // fsdp_count
-    fsdp_index = lax.axis_index("fsdp")
-    shares = [lax.dynamic_index_in_dim(query_parts, fsdp_index ^ step, 0, keepdims=False) for step in range(4)]
-    rows = [lax.dynamic_slice_in_dim(w_out, (fsdp_index ^ step) * features, features, 0) for step in range(4)]
-    pieces = [shares[0], exchanged(jnp.concatenate([shares[1], rows[1]], axis=0), "fsdp", 1)]
-    pieces += [exchanged(shares[step], "fsdp", step) for step in range(2, 4)]
-    packed = pack(parts, long_filter).reshape(seq_count, -1, local_tok)
-    whole = lax.all_to_all(packed, "seq", 0, 0, tiled=True).reshape(-1, local_tok)
+    parts, tokens, w_out = lax.optimization_barrier((parts, tokens, w_out))
+    query_parts, bundle = project_query(tokens, weights, w_out, fsdp_count)
+    from_mate = exchanged(bundle, "fsdp", 1)
+    keep, send = pair_query(query_parts, from_mate)
+    other_chip = exchanged(send, "fsdp", 2)
+    packed = pack(parts, long_filter).reshape(seq_count, 3, 2, local_tok).transpose(0, 2, 1, 3)
+    whole = lax.all_to_all(packed.reshape(seq_count, 2, -1), "seq", 0, 0, tiled=True)
+    whole = whole.reshape(seq_count, 2, 3, local_tok).transpose(0, 2, 1, 3).reshape(-1, local_tok)
     coded = convolve(whole, short_w, skip_gain.reshape(1, -1), seq_count, local_tok)
-    coded, pieces, rows = lax.optimization_barrier((coded, pieces, rows))
-    query, edge = sum_query(pieces, local_tok)
+    coded, other_chip, from_mate = lax.optimization_barrier((coded, other_chip, from_mate))
+    query, edge, far = sum_query(keep, other_chip, w_out, from_mate)
     edge = lax.ppermute(edge, "seq", [(i, i + 1) for i in range(seq_count - 1)])
     query = mix_query(edge, query, short_w)
-    columns = [rows[0], pieces[1]] + [exchanged(rows[step], "fsdp", step) for step in range(2, 4)]
+    far = exchanged(far, "fsdp", 2)
     home = lax.all_to_all(coded.reshape(seq_count, 2, local_tok), "seq", 0, 0, tiled=True)
     gated = gate(home.reshape(channels, local_tok), query)
     gathered = lax.all_gather(gated, "fsdp", axis=0, tiled=True)
-    return output(gathered, columns, features)
+    return output(gathered, w_out, from_mate, far)
 
 
 def solution(mesh):

time: 95.5 us -> 92.1 us (0.964)
  starting transfers between devices: 46.2 us -> 35.8 us
  waiting for transfers between devices: 12 us -> 19.9 us
  Pallas kernels: 5.31 us -> 6.8 us
  local copies, waits for them, and re-layouts: 1.53 us -> 0.06 us
    ppermute x5 -> x3, starting transfers between devices: 19 us -> 9.07 us  [exchanged(): lax.ppermute(piece, axis, [(i, i ^ step) for i in range(lax.axis_size(axi...]
    all_to_all x1, waiting for transfers between devices: 1.6 us -> 6.14 us  [on_device(): lax.all_to_all(coded.reshape(seq_count, 2, local_tok), 'seq', 0, 0, tiled...]
    ppermute x1, waiting for transfers between devices: 0.78 us -> 2.72 us  [on_device(): edge = lax.ppermute(edge, 'seq', [(i, i + 1) for i in range(seq_count - 1)])]
    pallas_call x3 -> x5, Pallas kernels: 1.64 us -> 3.28 us  [the longest x1 1.74 us: project(): pl.pallas_call(functools.partial(project_kernel, first), in_specs=[pl.Blo...]
    unnamed x20 -> x22, local copies, waits for them, and re-layouts: 1.45 us -> 0.06 us
    ppermute x5 -> x3, waiting for transfers between devices: 0.01 us -> 1.33 us  [exchanged(): lax.ppermute(piece, axis, [(i, i ^ step) for i in range(lax.axis_size(axi...]
  transfers between devices with their start and end apart: 8 -> 6, of which waited for: 3 -> 4; matrix products, arithmetic and copies ran while one was open for 0% -> 0% of each run, Pallas kernels for 3% -> 3%
where the time goes in v5:
time: 92.1 us; the launch traced here: 91.7 us
  starting transfers between devices  35.8 us (39%)
  blocking collectives  28.9 us (31%)
  waiting for transfers between devices  19.9 us (22%)
  Pallas kernels  6.8 us (7%)
    all_to_all x1, blocking collectives, on_device(): parts = lax.all_to_all(partial, 'fsdp', 0, 0, tiled=True)  18.7 us
    all_to_all x1, starting transfers between devices, on_device(): lax.all_to_all(packed.reshape(seq_count, 2, -1), 'seq', 0, 0, tiled=True)  16.3 us
    all_gather x1, blocking collectives, on_device(): gathered = lax.all_gather(gated, 'fsdp', axis=0, tiled=True)  10.2 us
    all_to_all x1, waiting for transfers between devices, on_device(): lax.all_to_all(packed.reshape(seq_count, 2, -1), 'seq', 0, 0, tiled=True)  9.75 us
    ppermute x3, starting transfers between devices, exchanged(): lax.ppermute(piece, axis, [(i, i ^ step) for i in range(lax.axis_size(axi...  9.07 us
    all_to_all x1, starting transfers between devices, on_device(): lax.all_to_all(coded.reshape(seq_count, 2, local_tok), 'seq', 0, 0, tiled...  8.65 us
    all_to_all x1, waiting for transfers between devices, on_device(): lax.all_to_all(coded.reshape(seq_count, 2, local_tok), 'seq', 0, 0, tiled...  6.14 us
    ppermute x1, waiting for transfers between devices, on_device(): edge = lax.ppermute(edge, 'seq', [(i, i + 1) for i in range(seq_count - 1)])  2.72 us
  transfers between devices with their start and end apart: 6, of which 4 were waited for; matrix products, arithmetic and copies ran while one was open for 0% of the time, Pallas kernels for 3%

profile of v5, /device:TPU:1, one launch (start us, length us, event | category | flops | bytes accessed | tf_op | source)
XLA Modules:
  0.0 91.7 jit_solution(9379929320352896583)
XLA Ops:
  0.0 0.0 copy-start.5
  0.0 1.7 %project.1 = bf16[4,2,128,256]{3,2,1,0:T(8,128)(2,1)S(1)} custom-call(bf16[128,256]{1,0:T(8,128)(2,1)} %tokens_ref, bf16[3,256,1024]{2,1,0:T(8,128)(2,1)} %bitcast.14), custom_call_target="tpu_custom_call" | custom-call | tf_op jit(solution)/shard_map/project/pallas_call | solution.py:56
  1.8 0.0 copy-start
  1.8 0.0 copy-start.1
  1.8 0.0 copy-start.2
  1.8 18.7 %all_to_all.15.parts_ref = bf16[4,2,128,256]{3,2,1,0:T(8,128)(2,1)S(1)} all-to-all(bf16[4,2,128,256]{3,2,1,0:T(8,128)(2,1)S(1)} %project.1), channel_id=1, replica_groups=mesh['seq'=128,'fsdp'=4] {'fsdp'}, dimensions={0} | all-to-all | bytes 1048576 | tf_op jit(solution)/shard_map/all_to_all | solution.py:357
  20.5 0.0 copy-done.5
  20.5 1.1 %pack.1 = bf16[768,128]{1,0:T(8,128)(2,1)} custom-call(bf16[4,2,128,256]{3,2,1,0:T(8,128)(2,1)S(1)} %all_to_all.15.parts_ref, f32[256,128]{1,0:T(8,128)S(1)} %copy-done.5), custom_call_target="tpu_custom_call" | custom-call | tf_op jit(solution)/shard_map/pack/pallas_call | solution.py:119
  21.6 0.0 copy-start.3
  21.6 0.0 copy-start.4
  21.6 0.0 copy-start.6
  21.6 0.0 copy-start.7
  21.6 0.0 copy-start.8
  21.6 0.0 copy-start.9
  21.6 0.0 copy-start.10
  21.7 16.3 %all-to-all-start.1 = ((bf16[128,2,384]{2,1,0:T(2,128)(2,1)}), bf16[128,2,384]{2,1,0:T(2,128)(2,1)S(1)}, u32[]{:S(2)}, u32[]{:S(2)}) async-start(bf16[128,2,384]{2,1,0:T(2,128)(2,1)} %bitcast.3), calls=%async_computation.1 | async-start | bytes 393216 | tf_op jit(solution)/shard_map/all_to_all | solution.py:364
  37.9 0.0 copy-done
  37.9 0.0 copy-done.1
  37.9 0.0 copy-done.2
  37.9 0.3 project_query.1
  38.2 3.2 %collective-permute-start = (bf16[768,256]{1,0:T(8,128)(2,1)S(1)}, bf16[768,256]{1,0:T(8,128)(2,1)S(1)}, u32[]{:S(2)}, u32[]{:S(2)}) collective-permute-start(bf16[768,256]{1,0:T(8,128)(2,1)S(1)} %get-tuple-element.22), channel_id=1, source_target_pairs={{0,1},{1,0},{2,3},{3,2},{4,5},{5,4},{6,7},{7,6},{8,9},{9,8},{10,11... | collective-permute-start | bytes 1179656 | tf_op jit(solution)/shard_map/ppermute | solution.py:348
  41.5 1.3 %collective-permute-done.from_mate_ref = bf16[768,256]{1,0:T(8,128)(2,1)S(1)} collective-permute-done((bf16[768,256]{1,0:T(8,128)(2,1)S(1)}, bf16[768,256]{1,0:T(8,128)(2,1)S(1)}, u32[]{:S(2)}, u32[]{:S(2)}) %collective-permute-start) | collective-permute-done | bytes 393248 | tf_op jit(solution)/shard_map/ppermute | solution.py:348
  42.8 0.2 pair_query.1
  43.0 2.6 %collective-permute-start.1 = (bf16[128,256]{1,0:T(8,128)(2,1)S(1)}, bf16[128,256]{1,0:T(8,128)(2,1)S(1)}, u32[]{:S(2)}, u32[]{:S(2)}) collective-permute-start(bf16[128,256]{1,0:T(8,128)(2,1)S(1)} %get-tuple-element.23), channel_id=1, source_target_pairs={{0,2},{1,3},{2,0},{3,1},{4,6},{5,7},{6,4},{7,5},{8,10},{9,11},{10,... | collective-permute-start | bytes 196616 | tf_op jit(solution)/shard_map/ppermute | solution.py:348
  45.6 9.7 %all-to-all-done.1 = bf16[128,2,384]{2,1,0:T(2,128)(2,1)S(1)} async-done(((bf16[128,2,384]{2,1,0:T(2,128)(2,1)}), bf16[128,2,384]{2,1,0:T(2,128)(2,1)S(1)}, u32[]{:S(2)}, u32[]{:S(2)}) %all-to-all-start.1) | async-done | bytes 196640 | tf_op jit(solution)/shard_map/all_to_all | solution.py:364
  55.3 0.0 copy-done.3
  55.3 0.0 copy-done.4
  55.3 0.0 copy-done.6
  55.3 0.0 copy-done.7
  55.3 0.0 copy-done.8
  55.4 0.0 copy-done.9
  55.4 0.0 copy-done.10
  55.4 2.3 %convolve.1 = bf16[256,128]{1,0:T(8,128)(2,1)} custom-call(bf16[768,128]{1,0:T(8,128)(2,1)S(1)} %bitcast.16, f32[3,3,256]{2,1,0:T(4,128)S(1)} %copy-done.9, f32[1,256]{1,0:T(1,128)S(1)} %bitcast.18, bf16[2,256,128]{2,1,0:T(8,128)(2,1)S(1)} %copy-done.8, f32[2,128,128]{2,1,0:T(8,128)S(1)} %copy-done.7, bf16[2,256,256]{2,1,0:T(8,128)(2,1)S(1)} %copy-done.4, ...), custom_call_target="tpu_custom_call" | custom-call | tf_op jit(solution)/shard_map/convolve/pallas_call | solution.py:216
  57.6 0.0 collective-permute-done.1.code_ref
  57.7 8.7 %all-to-all-start.2 = ((bf16[128,2,128]{2,1,0:T(2,128)(2,1)}), bf16[128,2,128]{2,1,0:T(2,128)(2,1)S(1)}, u32[]{:S(2)}, u32[]{:S(2)}) async-start(bf16[128,2,128]{2,1,0:T(2,128)(2,1)} %bitcast.8), calls=%async_computation.2 | async-start | bytes 131072 | tf_op jit(solution)/shard_map/all_to_all | solution.py:372
  66.3 0.1 sum_query.1
  66.4 3.2 %collective-permute-start.3 = (bf16[512,256]{1,0:T(8,128)(2,1)S(1)}, bf16[512,256]{1,0:T(8,128)(2,1)S(1)}, u32[]{:S(2)}, u32[]{:S(2)}) collective-permute-start(bf16[512,256]{1,0:T(8,128)(2,1)S(1)} %get-tuple-element.30), channel_id=1, source_target_pairs={{0,2},{1,3},{2,0},{3,1},{4,6},{5,7},{6,4},{7,5},{8,10},{9,11},{10,... | collective-permute-start | bytes 786440 | tf_op jit(solution)/shard_map/ppermute | solution.py:348
  69.6 1.9 %collective-permute-start.2 = (f32[8,256]{1,0:T(8,128)S(1)}, f32[8,256]{1,0:T(8,128)S(1)}, u32[]{:S(2)}, u32[]{:S(2)}) collective-permute-start(f32[8,256]{1,0:T(8,128)S(1)} %get-tuple-element.28), channel_id=1, source_target_pairs={{0,4},{4,8},{8,12},{12,16},{16,20},{20,24},{24,28},{28,32},{32,36}... | collective-permute-start | bytes 24584 | tf_op jit(solution)/shard_map/ppermute | solution.py:369
  71.5 2.7 %collective-permute-done.2.edge_ref = f32[8,256]{1,0:T(8,128)S(1)} collective-permute-done((f32[8,256]{1,0:T(8,128)S(1)}, f32[8,256]{1,0:T(8,128)S(1)}, u32[]{:S(2)}, u32[]{:S(2)}) %collective-permute-start.2) | collective-permute-done | bytes 8224 | tf_op jit(solution)/shard_map/ppermute | solution.py:369
  74.2 0.1 mix_query.1.query_ref
  74.3 6.1 %all-to-all-done.2 = bf16[128,2,128]{2,1,0:T(2,128)(2,1)S(1)} async-done(((bf16[128,2,128]{2,1,0:T(2,128)(2,1)}), bf16[128,2,128]{2,1,0:T(2,128)(2,1)S(1)}, u32[]{:S(2)}, u32[]{:S(2)}) %all-to-all-start.2) | async-done | bytes 65568 | tf_op jit(solution)/shard_map/all_to_all | solution.py:372
  80.5 10.2 %all_gather.3.gated_ref = bf16[1024,128]{1,0:T(8,128)(2,1)S(1)} all-gather(bf16[256,128]{1,0:T(8,128)(2,1)S(1)} %gate.1), channel_id=1, replica_groups=mesh['seq'=128,'fsdp'=4] {'fsdp'}, dimensions={0}, use_global_device_ids=true | all-gather | bytes 327680 | tf_op jit(solution)/shard_map/all_gather | solution.py:374
  90.7 0.0 collective-permute-done.3.far_ref
  90.7 1.0 %output.1 = f32[128,256]{1,0:T(8,128)} custom-call(bf16[1024,128]{1,0:T(8,128)(2,1)S(1)} %all_gather.3.gated_ref, bf16[1024,256]{1,0:T(8,128)(2,1)S(1)} %copy-done.1, bf16[768,256]{1,0:T(8,128)(2,1)S(1)} %collective-permute-done.from_mate_ref, bf16[512,256]{1,0:T(8,128)(2,1)S(1)} %collective-permute-done.3.far_ref), custom_call_target="tpu_custom_call" | custom-call | tf_op jit(solution)/shard_map/output/pallas_call | solution.py:337
  (1 shorter events, 0.0 us)
Async XLA Ops:
  0.0 20.5 %copy-start.5 = (f32[256,128]{1,0:T(8,128)S(1)}, f32[256,128]{1,0:T(8,128)}, u32[]{:S(2)}) copy-start(f32[256,128]{1,0:T(8,128)} %taps_ref.1) | copy-start | bytes 393220
  1.8 36.2 %copy-start = (bf16[256,3,1024]{2,0,1:T(8,128)(2,1)S(1)}, bf16[256,3,1024]{2,0,1:T(8,128)(2,1)}, u32[]{:S(2)}) copy-start(bf16[256,3,1024]{2,0,1:T(8,128)(2,1)} %param.12) | copy-start | bytes 4718596
  1.8 36.2 %copy-start.1 = (bf16[1024,256]{1,0:T(8,128)(2,1)S(1)}, bf16[1024,256]{1,0:T(8,128)(2,1)}, u32[]{:S(2)}) copy-start(bf16[1024,256]{1,0:T(8,128)(2,1)} %w_out_ref.2) | copy-start | bytes 1572868
  1.8 36.2 %copy-start.2 = (bf16[128,256]{1,0:T(8,128)(2,1)S(1)}, bf16[128,256]{1,0:T(8,128)(2,1)}, u32[]{:S(2)}) copy-start(bf16[128,256]{1,0:T(8,128)(2,1)} %tokens_ref) | copy-start | bytes 196612
  21.6 33.7 %copy-start.3 = (bf16[2,256,256]{2,1,0:T(8,128)(2,1)S(1)}, bf16[2,256,256]{2,1,0:T(8,128)(2,1)}, u32[]{:S(2)}) copy-start(bf16[2,256,256]{2,1,0:T(8,128)(2,1)} %constant.13.clone.inv_ref) | copy-start | bytes 786436
  21.6 33.7 %copy-start.4 = (bf16[2,256,256]{2,1,0:T(8,128)(2,1)S(1)}, bf16[2,256,256]{2,1,0:T(8,128)(2,1)}, u32[]{:S(2)}) copy-start(bf16[2,256,256]{2,1,0:T(8,128)(2,1)} %constant.12.clone.mid_ref) | copy-start | bytes 786436
  21.6 33.7 %copy-start.6 = (bf16[2,128,256]{2,1,0:T(8,128)(2,1)S(1)}, bf16[2,128,256]{2,1,0:T(8,128)(2,1)}, u32[]{:S(2)}) copy-start(bf16[2,128,256]{2,1,0:T(8,128)(2,1)} %constant.14.clone.last_ref) | copy-start | bytes 393220
  21.6 33.7 %copy-start.7 = (f32[2,128,128]{2,1,0:T(8,128)S(1)}, f32[2,128,128]{2,1,0:T(8,128)}, u32[]{:S(2)}) copy-start(f32[2,128,128]{2,1,0:T(8,128)} %constant.11.clone.twist_ref) | copy-start | bytes 393220
  21.6 33.7 %copy-start.8 = (bf16[2,256,128]{2,1,0:T(8,128)(2,1)S(1)}, bf16[2,256,128]{2,1,0:T(8,128)(2,1)}, u32[]{:S(2)}) copy-start(bf16[2,256,128]{2,1,0:T(8,128)(2,1)} %constant.10.clone.first_ref) | copy-start | bytes 393220
  21.6 33.7 %copy-start.9 = (f32[3,3,256]{2,1,0:T(4,128)S(1)}, f32[3,3,256]{2,1,0:T(4,128)}, u32[]{:S(2)}) copy-start(f32[3,3,256]{2,1,0:T(4,128)} %short_ref.3) | copy-start | bytes 27652
  21.6 33.7 %copy-start.10 = (f32[256]{0:T(256)S(1)}, f32[256]{0:T(256)}, u32[]{:S(2)}) copy-start(f32[256]{0:T(256)} %param.15) | copy-start | bytes 3076
  21.7 33.7 %all-to-all-start.1 = ((bf16[128,2,384]{2,1,0:T(2,128)(2,1)}), bf16[128,2,384]{2,1,0:T(2,128)(2,1)S(1)}, u32[]{:S(2)}, u32[]{:S(2)}) async-start(bf16[128,2,384]{2,1,0:T(2,128)(2,1)} %bitcast.3), calls=%async_computation.1 | async-start | bytes 393216 | tf_op jit(solution)/shard_map/all_to_all | solution.py:364
  38.2 4.6 %collective-permute-start = (bf16[768,256]{1,0:T(8,128)(2,1)S(1)}, bf16[768,256]{1,0:T(8,128)(2,1)S(1)}, u32[]{:S(2)}, u32[]{:S(2)}) collective-permute-start(bf16[768,256]{1,0:T(8,128)(2,1)S(1)} %get-tuple-element.22), channel_id=1, source_target_pairs={{0,1},{1,0},{2,3},{3,2},{4,5},{5,4},{6,7},{7,6},{8,9},{9,8},{10,11... | collective-permute-start | bytes 1179656 | tf_op jit(solution)/shard_map/ppermute | solution.py:348
  43.0 14.7 %collective-permute-start.1 = (bf16[128,256]{1,0:T(8,128)(2,1)S(1)}, bf16[128,256]{1,0:T(8,128)(2,1)S(1)}, u32[]{:S(2)}, u32[]{:S(2)}) collective-permute-start(bf16[128,256]{1,0:T(8,128)(2,1)S(1)} %get-tuple-element.23), channel_id=1, source_target_pairs={{0,2},{1,3},{2,0},{3,1},{4,6},{5,7},{6,4},{7,5},{8,10},{9,11},{10,... | collective-permute-start | bytes 196616 | tf_op jit(solution)/shard_map/ppermute | solution.py:348
  57.7 22.8 %all-to-all-start.2 = ((bf16[128,2,128]{2,1,0:T(2,128)(2,1)}), bf16[128,2,128]{2,1,0:T(2,128)(2,1)S(1)}, u32[]{:S(2)}, u32[]{:S(2)}) async-start(bf16[128,2,128]{2,1,0:T(2,128)(2,1)} %bitcast.8), calls=%async_computation.2 | async-start | bytes 131072 | tf_op jit(solution)/shard_map/all_to_all | solution.py:372
  66.4 24.3 %collective-permute-start.3 = (bf16[512,256]{1,0:T(8,128)(2,1)S(1)}, bf16[512,256]{1,0:T(8,128)(2,1)S(1)}, u32[]{:S(2)}, u32[]{:S(2)}) collective-permute-start(bf16[512,256]{1,0:T(8,128)(2,1)S(1)} %get-tuple-element.30), channel_id=1, source_target_pairs={{0,2},{1,3},{2,0},{3,1},{4,6},{5,7},{6,4},{7,5},{8,10},{9,11},{10,... | collective-permute-start | bytes 786440 | tf_op jit(solution)/shard_map/ppermute | solution.py:348
  69.6 4.6 %collective-permute-start.2 = (f32[8,256]{1,0:T(8,128)S(1)}, f32[8,256]{1,0:T(8,128)S(1)}, u32[]{:S(2)}, u32[]{:S(2)}) collective-permute-start(f32[8,256]{1,0:T(8,128)S(1)} %get-tuple-element.28), channel_id=1, source_target_pairs={{0,4},{4,8},{8,12},{12,16},{16,20},{20,24},{24,28},{28,32},{32,36}... | collective-permute-start | bytes 24584 | tf_op jit(solution)/shard_map/ppermute | solution.py:369

commit v6 on v5

--- a/solution.py
+++ b/solution.py
@@ -61,7 +61,7 @@
         scratch_shapes=[
             pltpu.VMEM(tokens.shape, tokens.dtype),
             pltpu.VMEM((kinds, depth, wide), weights.dtype),
-            pltpu.SemaphoreType.DMA((4 * kinds + 1,)),
+            pltpu.SemaphoreType.DMA((kinds + 1,)),
         ],
         compiler_params=PARAMS,
         name="project",
@@ -135,10 +135,14 @@
     return high, (values - high.astype(jnp.float32)).astype(jnp.bfloat16)
 
 
-def dot3(left, right):
-    (a, b), (c, d) = left, right
-    low = jnp.dot(a, d, preferred_element_type=jnp.float32) + jnp.dot(b, c, preferred_element_type=jnp.float32)
-    return jnp.dot(a, c, preferred_element_type=jnp.float32) + low
+def dot_right(values, table):
+    high, low = split(values)
+    return jnp.dot(jnp.concatenate([high, low, high], axis=1), table, preferred_element_type=jnp.float32)
+
+
+def dot_left(table, values):
+    high, low = split(values)
+    return jnp.dot(table, jnp.concatenate([high, high, low], axis=0), preferred_element_type=jnp.float32)
 
 
 def delayed(block, by):
@@ -150,44 +154,49 @@
     return jnp.where(col < by, carried, moved)
 
 
-def convolve_kernel(code_ref, short_ref, skip_ref, first_ref, twist_ref, mid_ref, inv_ref, last_ref, out_ref, now_ref, mix_ref):
+def convolve_kernel(turn, code_ref, short_ref, skip_ref, first_ref, twist_ref, mid_ref, inv_ref, last_ref, out_ref, now_ref, mix_ref):
     rows, cols = twist_ref.shape[1:]
     now_ref[...] = decode(code_ref[...])
-    shift = short_ref.shape[2] - 2 * lax.axis_index("seq")
+    pair = lax.rem(lax.axis_index("seq") + rows - turn, rows)
+    shift = short_ref.shape[2] - 2 * pair
     short = [pltpu.roll(short_ref[tap], shift, 1) for tap in range(3)]
     skip = pltpu.roll(skip_ref[...], shift, 1)
 
+    def turned_back(row):
+        return jnp.roll(now_ref[pl.ds(row, rows, stride=6), :], turn, axis=0)
+
     def mixed(kind, j):
-        block = now_ref[pl.ds(2 * kind + j, rows, stride=6), :] * (1.0 / PROJ_SCALE)
+        block = turned_back(2 * kind + j) * (1.0 / PROJ_SCALE)
         weights = [short[tap][kind + 1 : kind + 2, j : j + 1] for tap in range(3)]
         return weights[0] * block + weights[1] * delayed(block, 1) + weights[2] * delayed(block, 2)
 
     signal = [mixed(0, j) * mixed(1, j) for j in range(2)]
-    taps = [now_ref[pl.ds(4 + j, rows, stride=6), :] * (1.0 / TAP_SCALE) for j in range(2)]
+    taps = [turned_back(4 + j) * (1.0 / TAP_SCALE) for j in range(2)]
     data = jnp.concatenate(signal + taps, axis=1)
-    spread = dot3((first_ref[0], first_ref[1]), split(data))
+    spread = dot_left(first_ref[...], data)
     t_re, t_im = twist_ref[0], twist_ref[1]
     turned = []
     for k in range(4):
         re = spread[:rows, k * cols : (k + 1) * cols]
         im = spread[rows:, k * cols : (k + 1) * cols]
         turned.append(jnp.concatenate([re * t_re - im * t_im, re * t_im + im * t_re], axis=1))
-    freq = dot3(split(jnp.concatenate(turned, axis=0)), (mid_ref[0], mid_ref[1]))
+    freq = dot_right(jnp.concatenate(turned, axis=0), mid_ref[...])
     both = []
     for j in range(2):
         s_re, s_im = freq[j * rows : (j + 1) * rows, :cols], freq[j * rows : (j + 1) * rows, cols:]
         h_re, h_im = freq[(2 + j) * rows : (3 + j) * rows, :cols], freq[(2 + j) * rows : (3 + j) * rows, cols:]
         both.append(jnp.concatenate([s_re * h_re - s_im * h_im, s_re * h_im + s_im * h_re], axis=1))
-    back = dot3(split(jnp.concatenate(both, axis=0)), (inv_ref[0], inv_ref[1]))
+    back = dot_right(jnp.concatenate(both, axis=0), inv_ref[...])
     real, imag = [], []
     for j in range(2):
         re, im = back[j * rows : (j + 1) * rows, :cols], back[j * rows : (j + 1) * rows, cols:]
         real.append(re * t_re + im * t_im)
         imag.append(im * t_re - re * t_im)
     stacked = jnp.concatenate([jnp.concatenate(real, axis=1), jnp.concatenate(imag, axis=1)], axis=0)
-    convolved = dot3((last_ref[0], last_ref[1]), split(stacked))
+    convolved = dot_left(last_ref[...], stacked)
     for j in range(2):
-        mix_ref[pl.ds(j, rows, stride=2), :] = convolved[:, j * cols : (j + 1) * cols] + skip[:, j : j + 1] * signal[j]
+        outcome = convolved[:, j * cols : (j + 1) * cols] + skip[:, j : j + 1] * signal[j]
+        mix_ref[pl.ds(j, rows, stride=2), :] = jnp.roll(outcome, -turn, axis=0)
     out_ref[...] = (mix_ref[...] * jnp.abs(mix_ref[...])).astype(jnp.bfloat16)
 
 
@@ -201,20 +210,28 @@
     def halves(table):
         table = table.astype(np.float32)
         high = table.astype(jnp.bfloat16)
-        return jnp.asarray(np.stack([high, (table - high.astype(np.float32)).astype(jnp.bfloat16)]))
+        return high, (table - high.astype(np.float32)).astype(jnp.bfloat16)
+
+    def at_left(table):
+        high, low = halves(table)
+        return jnp.asarray(np.concatenate([high, low, high], axis=1))
+
+    def at_right(table):
+        high, low = halves(table)
+        return jnp.asarray(np.concatenate([high, high, low], axis=0))
 
     return (
-        halves(np.concatenate([first.real, first.imag])),
+        at_left(np.concatenate([first.real, first.imag])),
         jnp.asarray(np.stack([twist.real, twist.imag]).astype(np.float32)),
-        halves(np.block([[second.real, second.imag], [-second.imag, second.real]])),
-        halves(np.block([[second.real, -second.imag], [second.imag, second.real]])),
-        halves(np.concatenate([first.real.T, first.imag.T], axis=1) / total),
+        at_right(np.block([[second.real, second.imag], [-second.imag, second.real]])),
+        at_right(np.block([[second.real, -second.imag], [second.imag, second.real]])),
+        at_left(np.concatenate([first.real.T, first.imag.T], axis=1) / total),
     )
 
 
-def convolve(code, short, skip, rows, cols):
-    return pl.pallas_call(
-        convolve_kernel,
+def convolve(code, short, skip, rows, cols, turn):
+    return pl.pallas_call(
+        functools.partial(convolve_kernel, turn),
         in_specs=[VMEM] * 8,
         out_specs=VMEM,
         out_shape=jax.ShapeDtypeStruct((2 * rows, cols), jnp.bfloat16),
@@ -352,6 +369,8 @@
     seq_count = lax.axis_size("seq")
     fsdp_count = lax.axis_size("fsdp")
     channels, local_tok = long_filter.shape
+    turn = 88
+    group = [[(i + turn) % seq_count for i in range(seq_count)]]
     weights = w_in.transpose(1, 0, 2)
     partial = project(tokens, weights, 1, 2, fsdp_count)
     parts = lax.all_to_all(partial, "fsdp", 0, 0, tiled=True)
@@ -361,15 +380,15 @@
     keep, send = pair_query(query_parts, from_mate)
     other_chip = exchanged(send, "fsdp", 2)
     packed = pack(parts, long_filter).reshape(seq_count, 3, 2, local_tok).transpose(0, 2, 1, 3)
-    whole = lax.all_to_all(packed.reshape(seq_count, 2, -1), "seq", 0, 0, tiled=True)
+    whole = lax.all_to_all(packed.reshape(seq_count, 2, -1), "seq", 0, 0, tiled=True, axis_index_groups=group)
     whole = whole.reshape(seq_count, 2, 3, local_tok).transpose(0, 2, 1, 3).reshape(-1, local_tok)
-    coded = convolve(whole, short_w, skip_gain.reshape(1, -1), seq_count, local_tok)
+    coded = convolve(whole, short_w, skip_gain.reshape(1, -1), seq_count, local_tok, turn)
     coded, other_chip, from_mate = lax.optimization_barrier((coded, other_chip, from_mate))
     query, edge, far = sum_query(keep, other_chip, w_out, from_mate)
     edge = lax.ppermute(edge, "seq", [(i, i + 1) for i in range(seq_count - 1)])
     query = mix_query(edge, query, short_w)
     far = exchanged(far, "fsdp", 2)
-    home = lax.all_to_all(coded.reshape(seq_count, 2, local_tok), "seq", 0, 0, tiled=True)
+    home = lax.all_to_all(coded.reshape(seq_count, 2, local_tok), "seq", 0, 0, tiled=True, axis_index_groups=group)
     gated = gate(home.reshape(channels, local_tok), query)
     gathered = lax.all_gather(gated, "fsdp", axis=0, tiled=True)
     return output(gathered, w_out, from_mate, far)

time: 92.1 us -> 87.6 us (0.951); the launches traced: 91.7 us -> 86 us
  waiting for transfers between devices: 19.9 us -> 7.22 us
  starting transfers between devices: 35.8 us -> 41.9 us
    all_to_all x1, waiting for transfers between devices: 6.14 us -> 0.01 us  [on_device(): lax.all_to_all(coded.reshape(seq_count, 2, local_tok), 'seq', 0, 0, tiled...]
    all_to_all x1, waiting for transfers between devices: 9.75 us -> 4.25 us  [on_device(): lax.all_to_all(packed.reshape(seq_count, 2, -1), 'seq', 0, 0, tiled=True,...]
    all_to_all x1, starting transfers between devices: 8.65 us -> 13.1 us  [on_device(): lax.all_to_all(coded.reshape(seq_count, 2, local_tok), 'seq', 0, 0, tiled...]
    ppermute x1, waiting for transfers between devices: 2.72 us -> 1.63 us  [on_device(): edge = lax.ppermute(edge, 'seq', [(i, i + 1) for i in range(seq_count - 1)])]
  transfers between devices with their start and end apart: 6 -> 6, of which waited for: 4 -> 3; matrix products, arithmetic and copies ran while one was open for 0% -> 0% of each run, Pallas kernels for 3% -> 3%
where the time goes in v6:
time: 87.6 us; the launch traced here: 86 us
  starting transfers between devices  41.9 us (48%)
  blocking collectives  29.1 us (33%)
  waiting for transfers between devices  7.22 us (8%)
  Pallas kernels  6.63 us (8%)
  local copies, waits for them, and re-layouts  0.95 us (1%)
    all_to_all x1, blocking collectives, on_device(): parts = lax.all_to_all(partial, 'fsdp', 0, 0, tiled=True)  18.7 us
    all_to_all x1, starting transfers between devices, on_device(): lax.all_to_all(packed.reshape(seq_count, 2, -1), 'seq', 0, 0, tiled=True,...  16.4 us
    all_to_all x1, starting transfers between devices, on_device(): lax.all_to_all(coded.reshape(seq_count, 2, local_tok), 'seq', 0, 0, tiled...  13.1 us
    all_gather x1, blocking collectives, on_device(): gathered = lax.all_gather(gated, 'fsdp', axis=0, tiled=True)  10.4 us
    ppermute x3, starting transfers between devices, exchanged(): lax.ppermute(piece, axis, [(i, i ^ step) for i in range(lax.axis_size(axi...  9.94 us
    all_to_all x1, waiting for transfers between devices, on_device(): lax.all_to_all(packed.reshape(seq_count, 2, -1), 'seq', 0, 0, tiled=True,...  4.25 us
    ppermute x1, starting transfers between devices, on_device(): edge = lax.ppermute(edge, 'seq', [(i, i + 1) for i in range(seq_count - 1)])  2.49 us
    pallas_call x1, Pallas kernels, convolve(): pl.pallas_call(functools.partial(convolve_kernel, turn), in_specs=[VMEM]...  2.21 us
  transfers between devices with their start and end apart: 6, of which 3 were waited for; matrix products, arithmetic and copies ran while one was open for 0% of the time, Pallas kernels for 3%

profile of v6, /device:TPU:1, one launch (start us, length us, event | category | flops | bytes accessed | tf_op | source)
XLA Modules:
  0.0 86.0 jit_solution(9280045466423406382)
XLA Ops:
  0.0 0.0 copy-start.7
  0.0 1.6 %project.1 = bf16[4,2,128,256]{3,2,1,0:T(8,128)(2,1)S(1)} custom-call(bf16[128,256]{1,0:T(8,128)(2,1)} %tokens_ref, bf16[3,256,1024]{2,1,0:T(8,128)(2,1)} %bitcast.14), custom_call_target="tpu_custom_call" | custom-call | tf_op jit(solution)/shard_map/project/pallas_call | solution.py:56
  1.6 0.0 copy-start
  1.7 0.0 copy-start.1
  1.7 0.0 copy-start.4
  1.7 18.7 %all_to_all.15.parts_ref = bf16[4,2,128,256]{3,2,1,0:T(8,128)(2,1)S(1)} all-to-all(bf16[4,2,128,256]{3,2,1,0:T(8,128)(2,1)S(1)} %project.1), channel_id=1, replica_groups=mesh['seq'=128,'fsdp'=4] {'fsdp'}, dimensions={0} | all-to-all | bytes 1048576 | tf_op jit(solution)/shard_map/all_to_all | solution.py:376
  20.4 0.0 copy-done.7
  20.4 1.1 %pack.1 = bf16[768,128]{1,0:T(8,128)(2,1)} custom-call(bf16[4,2,128,256]{3,2,1,0:T(8,128)(2,1)S(1)} %all_to_all.15.parts_ref, f32[256,128]{1,0:T(8,128)S(1)} %copy-done.7), custom_call_target="tpu_custom_call" | custom-call | tf_op jit(solution)/shard_map/pack/pallas_call | solution.py:119
  21.5 0.0 copy-start.2
  21.5 0.0 copy-start.3
  21.5 0.0 copy-start.5
  21.5 0.0 copy-start.6
  21.5 0.0 copy-start.9
  21.5 0.0 copy-start.10
  21.5 16.4 %all-to-all-start.1 = ((bf16[128,2,384]{2,1,0:T(2,128)(2,1)}), bf16[128,2,384]{2,1,0:T(2,128)(2,1)S(1)}, u32[]{:S(2)}, u32[]{:S(2)}) async-start(bf16[128,2,384]{2,1,0:T(2,128)(2,1)} %bitcast.3), calls=%async_computation.1 | async-start | bytes 393216 | tf_op jit(solution)/shard_map/all_to_all | solution.py:383
  38.0 0.0 copy-done
  38.0 0.0 copy-done.1
  38.0 0.0 copy-done.4
  38.0 0.3 project_query.1
  38.3 3.5 %collective-permute-start = (bf16[768,256]{1,0:T(8,128)(2,1)S(1)}, bf16[768,256]{1,0:T(8,128)(2,1)S(1)}, u32[]{:S(2)}, u32[]{:S(2)}) collective-permute-start(bf16[768,256]{1,0:T(8,128)(2,1)S(1)} %get-tuple-element.22), channel_id=1, source_target_pairs={{0,1},{1,0},{2,3},{3,2},{4,5},{5,4},{6,7},{7,6},{8,9},{9,8},{10,11... | collective-permute-start | bytes 1179656 | tf_op jit(solution)/shard_map/ppermute | solution.py:365
  41.8 1.3 %collective-permute-done.from_mate_ref = bf16[768,256]{1,0:T(8,128)(2,1)S(1)} collective-permute-done((bf16[768,256]{1,0:T(8,128)(2,1)S(1)}, bf16[768,256]{1,0:T(8,128)(2,1)S(1)}, u32[]{:S(2)}, u32[]{:S(2)}) %collective-permute-start) | collective-permute-done | bytes 393248 | tf_op jit(solution)/shard_map/ppermute | solution.py:365
  43.1 0.2 pair_query.1
  43.3 2.6 %collective-permute-start.1 = (bf16[128,256]{1,0:T(8,128)(2,1)S(1)}, bf16[128,256]{1,0:T(8,128)(2,1)S(1)}, u32[]{:S(2)}, u32[]{:S(2)}) collective-permute-start(bf16[128,256]{1,0:T(8,128)(2,1)S(1)} %get-tuple-element.23), channel_id=1, source_target_pairs={{0,2},{1,3},{2,0},{3,1},{4,6},{5,7},{6,4},{7,5},{8,10},{9,11},{10,... | collective-permute-start | bytes 196616 | tf_op jit(solution)/shard_map/ppermute | solution.py:365
  45.9 4.3 %all-to-all-done.1 = bf16[128,2,384]{2,1,0:T(2,128)(2,1)S(1)} async-done(((bf16[128,2,384]{2,1,0:T(2,128)(2,1)}), bf16[128,2,384]{2,1,0:T(2,128)(2,1)S(1)}, u32[]{:S(2)}, u32[]{:S(2)}) %all-to-all-start.1) | async-done | bytes 196640 | tf_op jit(solution)/shard_map/all_to_all | solution.py:383
  50.2 0.0 copy-done.2
  50.2 0.0 copy-done.3
  50.2 0.0 copy-done.5
  50.2 0.0 copy-done.6
  50.2 0.0 copy-done.9
  50.2 0.0 copy-done.10
  50.2 0.0 copy-start.8
  50.2 0.9 %copy-done.8 = f32[2,128,128]{2,1,0:T(8,128)S(1)} copy-done((f32[2,128,128]{2,1,0:T(8,128)S(1)}, f32[2,128,128]{2,1,0:T(8,128)}, u32[]{:S(2)}) %copy-start.8) | copy-done | bytes 131096
  51.1 2.2 %convolve.1 = bf16[256,128]{1,0:T(8,128)(2,1)} custom-call(bf16[768,128]{1,0:T(8,128)(2,1)S(1)} %bitcast.16, f32[3,3,256]{2,1,0:T(4,128)S(1)} %copy-done.9, f32[1,256]{1,0:T(1,128)S(1)} %bitcast.18, bf16[256,384]{1,0:T(8,128)(2,1)S(1)} %copy-done.6, f32[2,128,128]{2,1,0:T(8,128)S(1)} %copy-done.8, bf16[768,256]{1,0:T(8,128)(2,1)S(1)} %copy-done.3, ...), custom_call_target="tpu_custom_call" | custom-call | tf_op jit(solution)/shard_map/convolve/pallas_call | solution.py:233
  53.3 0.0 collective-permute-done.1.code_ref
  53.3 13.1 %all-to-all-start.2 = ((bf16[128,2,128]{2,1,0:T(2,128)(2,1)}), bf16[128,2,128]{2,1,0:T(2,128)(2,1)S(1)}, u32[]{:S(2)}, u32[]{:S(2)}) async-start(bf16[128,2,128]{2,1,0:T(2,128)(2,1)} %bitcast.8), calls=%async_computation.2 | async-start | bytes 131072 | tf_op jit(solution)/shard_map/all_to_all | solution.py:391
  66.4 0.1 sum_query.1
  66.5 3.8 %collective-permute-start.3 = (bf16[512,256]{1,0:T(8,128)(2,1)S(1)}, bf16[512,256]{1,0:T(8,128)(2,1)S(1)}, u32[]{:S(2)}, u32[]{:S(2)}) collective-permute-start(bf16[512,256]{1,0:T(8,128)(2,1)S(1)} %get-tuple-element.30), channel_id=1, source_target_pairs={{0,2},{1,3},{2,0},{3,1},{4,6},{5,7},{6,4},{7,5},{8,10},{9,11},{10,... | collective-permute-start | bytes 786440 | tf_op jit(solution)/shard_map/ppermute | solution.py:365
  70.3 2.5 %collective-permute-start.2 = (f32[8,256]{1,0:T(8,128)S(1)}, f32[8,256]{1,0:T(8,128)S(1)}, u32[]{:S(2)}, u32[]{:S(2)}) collective-permute-start(f32[8,256]{1,0:T(8,128)S(1)} %get-tuple-element.28), channel_id=1, source_target_pairs={{0,4},{4,8},{8,12},{12,16},{16,20},{20,24},{24,28},{28,32},{32,36}... | collective-permute-start | bytes 24584 | tf_op jit(solution)/shard_map/ppermute | solution.py:388
  72.8 1.6 %collective-permute-done.2.edge_ref = f32[8,256]{1,0:T(8,128)S(1)} collective-permute-done((f32[8,256]{1,0:T(8,128)S(1)}, f32[8,256]{1,0:T(8,128)S(1)}, u32[]{:S(2)}, u32[]{:S(2)}) %collective-permute-start.2) | collective-permute-done | bytes 8224 | tf_op jit(solution)/shard_map/ppermute | solution.py:388
  74.4 0.1 mix_query.1.query_ref
  74.6 0.0 all-to-all-done.2
  74.6 10.4 %all_gather.3.gated_ref = bf16[1024,128]{1,0:T(8,128)(2,1)S(1)} all-gather(bf16[256,128]{1,0:T(8,128)(2,1)S(1)} %gate.1), channel_id=1, replica_groups=mesh['seq'=128,'fsdp'=4] {'fsdp'}, dimensions={0}, use_global_device_ids=true | all-gather | bytes 327680 | tf_op jit(solution)/shard_map/all_gather | solution.py:393
  85.0 0.0 collective-permute-done.3.far_ref
  85.0 1.0 %output.1 = f32[128,256]{1,0:T(8,128)} custom-call(bf16[1024,128]{1,0:T(8,128)(2,1)S(1)} %all_gather.3.gated_ref, bf16[1024,256]{1,0:T(8,128)(2,1)S(1)} %copy-done.1, bf16[768,256]{1,0:T(8,128)(2,1)S(1)} %collective-permute-done.from_mate_ref, bf16[512,256]{1,0:T(8,128)(2,1)S(1)} %collective-permute-done.3.far_ref), custom_call_target="tpu_custom_call" | custom-call | tf_op jit(solution)/shard_map/output/pallas_call | solution.py:354
  (1 shorter events, 0.0 us)
Async XLA Ops:
  0.0 20.4 %copy-start.7 = (f32[256,128]{1,0:T(8,128)S(1)}, f32[256,128]{1,0:T(8,128)}, u32[]{:S(2)}) copy-start(f32[256,128]{1,0:T(8,128)} %taps_ref.1) | copy-start | bytes 393220
  1.6 36.3 %copy-start = (bf16[256,3,1024]{2,0,1:T(8,128)(2,1)S(1)}, bf16[256,3,1024]{2,0,1:T(8,128)(2,1)}, u32[]{:S(2)}) copy-start(bf16[256,3,1024]{2,0,1:T(8,128)(2,1)} %param.12) | copy-start | bytes 4718596
  1.7 36.3 %copy-start.1 = (bf16[1024,256]{1,0:T(8,128)(2,1)S(1)}, bf16[1024,256]{1,0:T(8,128)(2,1)}, u32[]{:S(2)}) copy-start(bf16[1024,256]{1,0:T(8,128)(2,1)} %w_out_ref.2) | copy-start | bytes 1572868
  1.7 36.3 %copy-start.4 = (bf16[128,256]{1,0:T(8,128)(2,1)S(1)}, bf16[128,256]{1,0:T(8,128)(2,1)}, u32[]{:S(2)}) copy-start(bf16[128,256]{1,0:T(8,128)(2,1)} %tokens_ref) | copy-start | bytes 196612
  21.5 28.7 %copy-start.2 = (bf16[768,256]{1,0:T(8,128)(2,1)S(1)}, bf16[768,256]{1,0:T(8,128)(2,1)}, u32[]{:S(2)}) copy-start(bf16[768,256]{1,0:T(8,128)(2,1)} %constant.13.clone.inv_ref) | copy-start | bytes 1179652
  21.5 28.7 %copy-start.3 = (bf16[768,256]{1,0:T(8,128)(2,1)S(1)}, bf16[768,256]{1,0:T(8,128)(2,1)}, u32[]{:S(2)}) copy-start(bf16[768,256]{1,0:T(8,128)(2,1)} %constant.12.clone.mid_ref) | copy-start | bytes 1179652
  21.5 28.7 %copy-start.5 = (bf16[128,768]{1,0:T(8,128)(2,1)S(1)}, bf16[128,768]{1,0:T(8,128)(2,1)}, u32[]{:S(2)}) copy-start(bf16[128,768]{1,0:T(8,128)(2,1)} %constant.14.clone.last_ref) | copy-start | bytes 589828
  21.5 28.7 %copy-start.6 = (bf16[256,384]{1,0:T(8,128)(2,1)S(1)}, bf16[256,384]{1,0:T(8,128)(2,1)}, u32[]{:S(2)}) copy-start(bf16[256,384]{1,0:T(8,128)(2,1)} %constant.10.clone.first_ref) | copy-start | bytes 589828
  21.5 28.7 %copy-start.9 = (f32[3,3,256]{2,1,0:T(4,128)S(1)}, f32[3,3,256]{2,1,0:T(4,128)}, u32[]{:S(2)}) copy-start(f32[3,3,256]{2,1,0:T(4,128)} %short_ref.3) | copy-start | bytes 27652
  21.5 28.7 %copy-start.10 = (f32[256]{0:T(256)S(1)}, f32[256]{0:T(256)}, u32[]{:S(2)}) copy-start(f32[256]{0:T(256)} %param.15) | copy-start | bytes 3076
  21.5 28.6 %all-to-all-start.1 = ((bf16[128,2,384]{2,1,0:T(2,128)(2,1)}), bf16[128,2,384]{2,1,0:T(2,128)(2,1)S(1)}, u32[]{:S(2)}, u32[]{:S(2)}) async-start(bf16[128,2,384]{2,1,0:T(2,128)(2,1)} %bitcast.3), calls=%async_computation.1 | async-start | bytes 393216 | tf_op jit(solution)/shard_map/all_to_all | solution.py:383
  38.3 4.8 %collective-permute-start = (bf16[768,256]{1,0:T(8,128)(2,1)S(1)}, bf16[768,256]{1,0:T(8,128)(2,1)S(1)}, u32[]{:S(2)}, u32[]{:S(2)}) collective-permute-start(bf16[768,256]{1,0:T(8,128)(2,1)S(1)} %get-tuple-element.22), channel_id=1, source_target_pairs={{0,1},{1,0},{2,3},{3,2},{4,5},{5,4},{6,7},{7,6},{8,9},{9,8},{10,11... | collective-permute-start | bytes 1179656 | tf_op jit(solution)/shard_map/ppermute | solution.py:365
  43.3 10.0 %collective-permute-start.1 = (bf16[128,256]{1,0:T(8,128)(2,1)S(1)}, bf16[128,256]{1,0:T(8,128)(2,1)S(1)}, u32[]{:S(2)}, u32[]{:S(2)}) collective-permute-start(bf16[128,256]{1,0:T(8,128)(2,1)S(1)} %get-tuple-element.23), channel_id=1, source_target_pairs={{0,2},{1,3},{2,0},{3,1},{4,6},{5,7},{6,4},{7,5},{8,10},{9,11},{10,... | collective-permute-start | bytes 196616 | tf_op jit(solution)/shard_map/ppermute | solution.py:365
  50.2 0.9 %copy-start.8 = (f32[2,128,128]{2,1,0:T(8,128)S(1)}, f32[2,128,128]{2,1,0:T(8,128)}, u32[]{:S(2)}) copy-start(f32[2,128,128]{2,1,0:T(8,128)} %constant.11.clone.twist_ref) | copy-start | bytes 393220
  53.3 21.2 %all-to-all-start.2 = ((bf16[128,2,128]{2,1,0:T(2,128)(2,1)}), bf16[128,2,128]{2,1,0:T(2,128)(2,1)S(1)}, u32[]{:S(2)}, u32[]{:S(2)}) async-start(bf16[128,2,128]{2,1,0:T(2,128)(2,1)} %bitcast.8), calls=%async_computation.2 | async-start | bytes 131072 | tf_op jit(solution)/shard_map/all_to_all | solution.py:391
  66.5 18.5 %collective-permute-start.3 = (bf16[512,256]{1,0:T(8,128)(2,1)S(1)}, bf16[512,256]{1,0:T(8,128)(2,1)S(1)}, u32[]{:S(2)}, u32[]{:S(2)}) collective-permute-start(bf16[512,256]{1,0:T(8,128)(2,1)S(1)} %get-tuple-element.30), channel_id=1, source_target_pairs={{0,2},{1,3},{2,0},{3,1},{4,6},{5,7},{6,4},{7,5},{8,10},{9,11},{10,... | collective-permute-start | bytes 786440 | tf_op jit(solution)/shard_map/ppermute | solution.py:365
  70.3 4.1 %collective-permute-start.2 = (f32[8,256]{1,0:T(8,128)S(1)}, f32[8,256]{1,0:T(8,128)S(1)}, u32[]{:S(2)}, u32[]{:S(2)}) collective-permute-start(f32[8,256]{1,0:T(8,128)S(1)} %get-tuple-element.28), channel_id=1, source_target_pairs={{0,4},{4,8},{8,12},{12,16},{16,20},{20,24},{24,28},{28,32},{32,36}... | collective-permute-start | bytes 24584 | tf_op jit(solution)/shard_map/ppermute | solution.py:388

commit v7 on v6

--- a/solution.py
+++ b/solution.py
@@ -130,6 +130,28 @@
     )(parts, taps)
 
 
+ALONG_X = 4
+FIRST = (2, 12, 1)
+
+
+def group_order(devices):
+    along_z = devices // (2 * ALONG_X)
+    return [
+        (x + FIRST[0]) % ALONG_X * (2 * along_z) + (z + FIRST[1]) % along_z * 2 + (y + FIRST[2]) % 2
+        for z in range(along_z)
+        for x in range(ALONG_X)
+        for y in range(2)
+    ]
+
+
+def group_place(device, devices):
+    along_z = devices // (2 * ALONG_X)
+    x = lax.rem(lax.div(device, 2 * along_z) + ALONG_X - FIRST[0], ALONG_X)
+    z = lax.rem(lax.rem(lax.div(device, 2), along_z) + along_z - FIRST[1], along_z)
+    y = lax.rem(device + 2 - FIRST[2], 2)
+    return (z * ALONG_X + x) * 2 + y
+
+
 def split(values):
     high = values.astype(jnp.bfloat16)
     return high, (values - high.astype(jnp.float32)).astype(jnp.bfloat16)
@@ -154,24 +176,24 @@
     return jnp.where(col < by, carried, moved)
 
 
-def convolve_kernel(turn, code_ref, short_ref, skip_ref, first_ref, twist_ref, mid_ref, inv_ref, last_ref, out_ref, now_ref, mix_ref):
+def convolve_kernel(code_ref, order_ref, short_ref, skip_ref, first_ref, twist_ref, mid_ref, inv_ref, last_ref, out_ref, now_ref, mix_ref):
     rows, cols = twist_ref.shape[1:]
-    now_ref[...] = decode(code_ref[...])
-    pair = lax.rem(lax.axis_index("seq") + rows - turn, rows)
-    shift = short_ref.shape[2] - 2 * pair
+    now_ref[...] = code_ref[...].astype(jnp.float32)
+    shift = short_ref.shape[2] - 2 * group_place(lax.axis_index("seq"), rows)
     short = [pltpu.roll(short_ref[tap], shift, 1) for tap in range(3)]
     skip = pltpu.roll(skip_ref[...], shift, 1)
 
-    def turned_back(row):
-        return jnp.roll(now_ref[pl.ds(row, rows, stride=6), :], turn, axis=0)
+    def in_order(row):
+        code = now_ref[pl.ds(row, rows, stride=6), :].astype(jnp.bfloat16)
+        return decode(jnp.dot(order_ref[0], code, preferred_element_type=jnp.float32))
 
     def mixed(kind, j):
-        block = turned_back(2 * kind + j) * (1.0 / PROJ_SCALE)
+        block = in_order(2 * kind + j) * (1.0 / PROJ_SCALE)
         weights = [short[tap][kind + 1 : kind + 2, j : j + 1] for tap in range(3)]
         return weights[0] * block + weights[1] * delayed(block, 1) + weights[2] * delayed(block, 2)
 
     signal = [mixed(0, j) * mixed(1, j) for j in range(2)]
-    taps = [turned_back(4 + j) * (1.0 / TAP_SCALE) for j in range(2)]
+    taps = [in_order(4 + j) * (1.0 / TAP_SCALE) for j in range(2)]
     data = jnp.concatenate(signal + taps, axis=1)
     spread = dot_left(first_ref[...], data)
     t_re, t_im = twist_ref[0], twist_ref[1]
@@ -196,8 +218,10 @@
     convolved = dot_left(last_ref[...], stacked)
     for j in range(2):
         outcome = convolved[:, j * cols : (j + 1) * cols] + skip[:, j : j + 1] * signal[j]
-        mix_ref[pl.ds(j, rows, stride=2), :] = jnp.roll(outcome, -turn, axis=0)
-    out_ref[...] = (mix_ref[...] * jnp.abs(mix_ref[...])).astype(jnp.bfloat16)
+        code = (outcome * jnp.abs(outcome)).astype(jnp.bfloat16)
+        code = jnp.dot(order_ref[1], code, preferred_element_type=jnp.float32)
+        mix_ref[pl.ds(j, rows, stride=2), :] = code
+    out_ref[...] = mix_ref[...].astype(jnp.bfloat16)
 
 
 def tables(rows, cols):
@@ -229,16 +253,18 @@
     )
 
 
-def convolve(code, short, skip, rows, cols, turn):
-    return pl.pallas_call(
-        functools.partial(convolve_kernel, turn),
-        in_specs=[VMEM] * 8,
+def convolve(code, short, skip, rows, cols, order):
+    place = np.argsort(order)
+    order_table = jnp.asarray(np.stack([np.eye(rows)[place], np.eye(rows)[order]]), jnp.bfloat16)
+    return pl.pallas_call(
+        convolve_kernel,
+        in_specs=[VMEM] * 9,
         out_specs=VMEM,
         out_shape=jax.ShapeDtypeStruct((2 * rows, cols), jnp.bfloat16),
         scratch_shapes=[pltpu.VMEM((6 * rows, cols), jnp.float32), pltpu.VMEM((2 * rows, cols), jnp.float32)],
         compiler_params=PARAMS,
         name="convolve",
-    )(code, short, skip, *tables(rows, cols))
+    )(code, order_table, short, skip, *tables(rows, cols))
 
 
 def pair_query_kernel(own_ref, from_mate_ref, keep_ref, send_ref):
@@ -369,8 +395,8 @@
     seq_count = lax.axis_size("seq")
     fsdp_count = lax.axis_size("fsdp")
     channels, local_tok = long_filter.shape
-    turn = 88
-    group = [[(i + turn) % seq_count for i in range(seq_count)]]
+    order = group_order(seq_count)
+    group = [order]
     weights = w_in.transpose(1, 0, 2)
     partial = project(tokens, weights, 1, 2, fsdp_count)
     parts = lax.all_to_all(partial, "fsdp", 0, 0, tiled=True)
@@ -382,7 +408,7 @@
     packed = pack(parts, long_filter).reshape(seq_count, 3, 2, local_tok).transpose(0, 2, 1, 3)
     whole = lax.all_to_all(packed.reshape(seq_count, 2, -1), "seq", 0, 0, tiled=True, axis_index_groups=group)
     whole = whole.reshape(seq_count, 2, 3, local_tok).transpose(0, 2, 1, 3).reshape(-1, local_tok)
-    coded = convolve(whole, short_w, skip_gain.reshape(1, -1), seq_count, local_tok, turn)
+    coded = convolve(whole, short_w, skip_gain.reshape(1, -1), seq_count, local_tok, order)
     coded, other_chip, from_mate = lax.optimization_barrier((coded, other_chip, from_mate))
     query, edge, far = sum_query(keep, other_chip, w_out, from_mate)
     edge = lax.ppermute(edge, "seq", [(i, i + 1) for i in range(seq_count - 1)])

time: 87.6 us -> 88.2 us (level)
  waiting for transfers between devices: 7.22 us -> 8.63 us
  blocking collectives: 29.1 us -> 28 us
    ppermute x1, waiting for transfers between devices: 1.63 us -> 3.32 us  [on_device(): edge = lax.ppermute(edge, 'seq', [(i, i + 1) for i in range(seq_count - 1)])]
    all_gather x1, blocking collectives: 10.4 us -> 9.24 us  [on_device(): gathered = lax.all_gather(gated, 'fsdp', axis=0, tiled=True)]
    ppermute x1, starting transfers between devices: 2.49 us -> 1.58 us  [on_device(): edge = lax.ppermute(edge, 'seq', [(i, i + 1) for i in range(seq_count - 1)])]
    unnamed x22 -> x24, local copies, waits for them, and re-layouts: 0.95 us -> 1.79 us
  transfers between devices with their start and end apart: 6 -> 6, of which waited for: 3 -> 3; matrix products, arithmetic and copies ran while one was open for 0% -> 0% of each run, Pallas kernels for 3% -> 4%
where the time goes in v7:
time: 88.2 us; the launch traced here: 87.1 us
  starting transfers between devices  41.6 us (47%)
  blocking collectives  28 us (32%)
  waiting for transfers between devices  8.63 us (10%)
  Pallas kernels  6.94 us (8%)
  local copies, waits for them, and re-layouts  1.79 us (2%)
    all_to_all x1, blocking collectives, on_device(): parts = lax.all_to_all(partial, 'fsdp', 0, 0, tiled=True)  18.7 us
    all_to_all x1, starting transfers between devices, on_device(): lax.all_to_all(packed.reshape(seq_count, 2, -1), 'seq', 0, 0, tiled=True,...  17.2 us
    all_to_all x1, starting transfers between devices, on_device(): lax.all_to_all(coded.reshape(seq_count, 2, local_tok), 'seq', 0, 0, tiled...  13.7 us
    all_gather x1, blocking collectives, on_device(): gathered = lax.all_gather(gated, 'fsdp', axis=0, tiled=True)  9.24 us
    ppermute x3, starting transfers between devices, exchanged(): lax.ppermute(piece, axis, [(i, i ^ step) for i in range(lax.axis_size(axi...  9.1 us
    all_to_all x1, waiting for transfers between devices, on_device(): lax.all_to_all(packed.reshape(seq_count, 2, -1), 'seq', 0, 0, tiled=True,...  3.98 us
    ppermute x1, waiting for transfers between devices, on_device(): edge = lax.ppermute(edge, 'seq', [(i, i + 1) for i in range(seq_count - 1)])  3.32 us
    pallas_call x1, Pallas kernels, convolve(): pl.pallas_call(convolve_kernel, in_specs=[VMEM] * 9, out_specs=VMEM, out_...  2.5 us
  transfers between devices with their start and end apart: 6, of which 3 were waited for; matrix products, arithmetic and copies ran while one was open for 0% of the time, Pallas kernels for 4%

profile of v7, /device:TPU:1, one launch (start us, length us, event | category | flops | bytes accessed | tf_op | source)
XLA Modules:
  0.0 87.1 jit_solution(11087259991784036838)
XLA Ops:
  0.0 0.0 copy-start.8
  0.0 1.6 %project.1 = bf16[4,2,128,256]{3,2,1,0:T(8,128)(2,1)S(1)} custom-call(bf16[128,256]{1,0:T(8,128)(2,1)} %tokens_ref, bf16[3,256,1024]{2,1,0:T(8,128)(2,1)} %bitcast.14), custom_call_target="tpu_custom_call" | custom-call | tf_op jit(solution)/shard_map/project/pallas_call | solution.py:56
  1.6 0.0 copy-start
  1.7 0.0 copy-start.1
  1.7 0.0 copy-start.4
  1.7 18.7 %all_to_all.15.parts_ref = bf16[4,2,128,256]{3,2,1,0:T(8,128)(2,1)S(1)} all-to-all(bf16[4,2,128,256]{3,2,1,0:T(8,128)(2,1)S(1)} %project.1), channel_id=1, replica_groups=mesh['seq'=128,'fsdp'=4] {'fsdp'}, dimensions={0} | all-to-all | bytes 1048576 | tf_op jit(solution)/shard_map/all_to_all | solution.py:402
  20.4 0.0 copy-done.8
  20.4 1.1 %pack.1 = bf16[768,128]{1,0:T(8,128)(2,1)} custom-call(bf16[4,2,128,256]{3,2,1,0:T(8,128)(2,1)S(1)} %all_to_all.15.parts_ref, f32[256,128]{1,0:T(8,128)S(1)} %copy-done.8), custom_call_target="tpu_custom_call" | custom-call | tf_op jit(solution)/shard_map/pack/pallas_call | solution.py:119
  21.5 0.0 copy-start.2
  21.5 0.0 copy-start.3
  21.5 0.0 copy-start.5
  21.5 0.0 copy-start.6
  21.5 0.0 copy-start.10
  21.5 0.0 copy-start.11
  21.6 17.2 %all-to-all-start.1 = ((bf16[128,2,384]{2,1,0:T(2,128)(2,1)}), bf16[128,2,384]{2,1,0:T(2,128)(2,1)S(1)}, u32[]{:S(2)}, u32[]{:S(2)}) async-start(bf16[128,2,384]{2,1,0:T(2,128)(2,1)} %bitcast.3), calls=%async_computation.1 | async-start | bytes 393216 | tf_op jit(solution)/shard_map/all_to_all | solution.py:409
  38.8 0.0 copy-done
  38.8 0.0 copy-done.1
  38.8 0.0 copy-done.4
  38.8 0.3 project_query.1
  39.1 3.5 %collective-permute-start = (bf16[768,256]{1,0:T(8,128)(2,1)S(1)}, bf16[768,256]{1,0:T(8,128)(2,1)S(1)}, u32[]{:S(2)}, u32[]{:S(2)}) collective-permute-start(bf16[768,256]{1,0:T(8,128)(2,1)S(1)} %get-tuple-element.22), channel_id=1, source_target_pairs={{0,1},{1,0},{2,3},{3,2},{4,5},{5,4},{6,7},{7,6},{8,9},{9,8},{10,11... | collective-permute-start | bytes 1179656 | tf_op jit(solution)/shard_map/ppermute | solution.py:391
  42.6 1.3 %collective-permute-done.from_mate_ref = bf16[768,256]{1,0:T(8,128)(2,1)S(1)} collective-permute-done((bf16[768,256]{1,0:T(8,128)(2,1)S(1)}, bf16[768,256]{1,0:T(8,128)(2,1)S(1)}, u32[]{:S(2)}, u32[]{:S(2)}) %collective-permute-start) | collective-permute-done | bytes 393248 | tf_op jit(solution)/shard_map/ppermute | solution.py:391
  43.9 0.2 pair_query.1
  44.1 2.0 %collective-permute-start.1 = (bf16[128,256]{1,0:T(8,128)(2,1)S(1)}, bf16[128,256]{1,0:T(8,128)(2,1)S(1)}, u32[]{:S(2)}, u32[]{:S(2)}) collective-permute-start(bf16[128,256]{1,0:T(8,128)(2,1)S(1)} %get-tuple-element.23), channel_id=1, source_target_pairs={{0,2},{1,3},{2,0},{3,1},{4,6},{5,7},{6,4},{7,5},{8,10},{9,11},{10,... | collective-permute-start | bytes 196616 | tf_op jit(solution)/shard_map/ppermute | solution.py:391
  46.1 4.0 %all-to-all-done.1 = bf16[128,2,384]{2,1,0:T(2,128)(2,1)S(1)} async-done(((bf16[128,2,384]{2,1,0:T(2,128)(2,1)}), bf16[128,2,384]{2,1,0:T(2,128)(2,1)S(1)}, u32[]{:S(2)}, u32[]{:S(2)}) %all-to-all-start.1) | async-done | bytes 196640 | tf_op jit(solution)/shard_map/all_to_all | solution.py:409
  50.1 0.0 copy-done.2
  50.1 0.0 copy-done.3
  50.1 0.0 copy-done.5
  50.1 0.0 copy-done.6
  50.1 0.0 copy-done.10
  50.1 0.0 copy-done.11
  50.1 0.0 copy-start.7
  50.1 0.9 %copy-done.7 = f32[2,128,128]{2,1,0:T(8,128)S(1)} copy-done((f32[2,128,128]{2,1,0:T(8,128)S(1)}, f32[2,128,128]{2,1,0:T(8,128)}, u32[]{:S(2)}) %copy-start.7) | copy-done | bytes 131096
  51.0 0.0 copy-start.9
  51.0 0.8 copy-done.9
  51.9 2.5 %convolve.1 = bf16[256,128]{1,0:T(8,128)(2,1)} custom-call(bf16[768,128]{1,0:T(8,128)(2,1)S(1)} %bitcast.16, bf16[2,128,128]{2,1,0:T(8,128)(2,1)S(1)} %copy-done.9, f32[3,3,256]{2,1,0:T(4,128)S(1)} %copy-done.10, f32[1,256]{1,0:T(1,128)S(1)} %bitcast.18, bf16[256,384]{1,0:T(8,128)(2,1)S(1)} %copy-done.6, f32[2,128,128]{2,1,0:T(8,128)S(1)} %copy-done.7, ...), custom_call_target="tpu_custom_call" | custom-call | tf_op jit(solution)/shard_map/convolve/pallas_call | solution.py:259
  54.4 0.0 collective-permute-done.1.code_ref
  54.4 13.7 %all-to-all-start.2 = ((bf16[128,2,128]{2,1,0:T(2,128)(2,1)}), bf16[128,2,128]{2,1,0:T(2,128)(2,1)S(1)}, u32[]{:S(2)}, u32[]{:S(2)}) async-start(bf16[128,2,128]{2,1,0:T(2,128)(2,1)} %bitcast.8), calls=%async_computation.2 | async-start | bytes 131072 | tf_op jit(solution)/shard_map/all_to_all | solution.py:417
  68.1 0.1 sum_query.1
  68.1 3.6 %collective-permute-start.3 = (bf16[512,256]{1,0:T(8,128)(2,1)S(1)}, bf16[512,256]{1,0:T(8,128)(2,1)S(1)}, u32[]{:S(2)}, u32[]{:S(2)}) collective-permute-start(bf16[512,256]{1,0:T(8,128)(2,1)S(1)} %get-tuple-element.30), channel_id=1, source_target_pairs={{0,2},{1,3},{2,0},{3,1},{4,6},{5,7},{6,4},{7,5},{8,10},{9,11},{10,... | collective-permute-start | bytes 786440 | tf_op jit(solution)/shard_map/ppermute | solution.py:391
  71.8 1.6 %collective-permute-start.2 = (f32[8,256]{1,0:T(8,128)S(1)}, f32[8,256]{1,0:T(8,128)S(1)}, u32[]{:S(2)}, u32[]{:S(2)}) collective-permute-start(f32[8,256]{1,0:T(8,128)S(1)} %get-tuple-element.28), channel_id=1, source_target_pairs={{0,4},{4,8},{8,12},{12,16},{16,20},{20,24},{24,28},{28,32},{32,36}... | collective-permute-start | bytes 24584 | tf_op jit(solution)/shard_map/ppermute | solution.py:414
  73.3 3.3 %collective-permute-done.2.edge_ref = f32[8,256]{1,0:T(8,128)S(1)} collective-permute-done((f32[8,256]{1,0:T(8,128)S(1)}, f32[8,256]{1,0:T(8,128)S(1)}, u32[]{:S(2)}, u32[]{:S(2)}) %collective-permute-start.2) | collective-permute-done | bytes 8224 | tf_op jit(solution)/shard_map/ppermute | solution.py:414
  76.7 0.1 mix_query.1.query_ref
  76.8 0.0 all-to-all-done.2
  76.8 9.2 %all_gather.3.gated_ref = bf16[1024,128]{1,0:T(8,128)(2,1)S(1)} all-gather(bf16[256,128]{1,0:T(8,128)(2,1)S(1)} %gate.1), channel_id=1, replica_groups=mesh['seq'=128,'fsdp'=4] {'fsdp'}, dimensions={0}, use_global_device_ids=true | all-gather | bytes 327680 | tf_op jit(solution)/shard_map/all_gather | solution.py:419
  86.1 0.0 collective-permute-done.3.far_ref
  86.1 1.0 %output.1 = f32[128,256]{1,0:T(8,128)} custom-call(bf16[1024,128]{1,0:T(8,128)(2,1)S(1)} %all_gather.3.gated_ref, bf16[1024,256]{1,0:T(8,128)(2,1)S(1)} %copy-done.1, bf16[768,256]{1,0:T(8,128)(2,1)S(1)} %collective-permute-done.from_mate_ref, bf16[512,256]{1,0:T(8,128)(2,1)S(1)} %collective-permute-done.3.far_ref), custom_call_target="tpu_custom_call" | custom-call | tf_op jit(solution)/shard_map/output/pallas_call | solution.py:380
  (1 shorter events, 0.0 us)
Async XLA Ops:
  0.0 20.4 %copy-start.8 = (f32[256,128]{1,0:T(8,128)S(1)}, f32[256,128]{1,0:T(8,128)}, u32[]{:S(2)}) copy-start(f32[256,128]{1,0:T(8,128)} %taps_ref.1) | copy-start | bytes 393220
  1.6 37.1 %copy-start = (bf16[256,3,1024]{2,0,1:T(8,128)(2,1)S(1)}, bf16[256,3,1024]{2,0,1:T(8,128)(2,1)}, u32[]{:S(2)}) copy-start(bf16[256,3,1024]{2,0,1:T(8,128)(2,1)} %param.13) | copy-start | bytes 4718596
  1.7 37.1 %copy-start.1 = (bf16[1024,256]{1,0:T(8,128)(2,1)S(1)}, bf16[1024,256]{1,0:T(8,128)(2,1)}, u32[]{:S(2)}) copy-start(bf16[1024,256]{1,0:T(8,128)(2,1)} %w_out_ref.2) | copy-start | bytes 1572868
  1.7 37.1 %copy-start.4 = (bf16[128,256]{1,0:T(8,128)(2,1)S(1)}, bf16[128,256]{1,0:T(8,128)(2,1)}, u32[]{:S(2)}) copy-start(bf16[128,256]{1,0:T(8,128)(2,1)} %tokens_ref) | copy-start | bytes 196612
  21.5 28.6 %copy-start.2 = (bf16[768,256]{1,0:T(8,128)(2,1)S(1)}, bf16[768,256]{1,0:T(8,128)(2,1)}, u32[]{:S(2)}) copy-start(bf16[768,256]{1,0:T(8,128)(2,1)} %constant.16.clone.inv_ref) | copy-start | bytes 1179652
  21.5 28.6 %copy-start.3 = (bf16[768,256]{1,0:T(8,128)(2,1)S(1)}, bf16[768,256]{1,0:T(8,128)(2,1)}, u32[]{:S(2)}) copy-start(bf16[768,256]{1,0:T(8,128)(2,1)} %constant.15.clone.mid_ref) | copy-start | bytes 1179652
  21.5 28.6 %copy-start.5 = (bf16[128,768]{1,0:T(8,128)(2,1)S(1)}, bf16[128,768]{1,0:T(8,128)(2,1)}, u32[]{:S(2)}) copy-start(bf16[128,768]{1,0:T(8,128)(2,1)} %constant.17.clone.last_ref) | copy-start | bytes 589828
  21.5 28.6 %copy-start.6 = (bf16[256,384]{1,0:T(8,128)(2,1)S(1)}, bf16[256,384]{1,0:T(8,128)(2,1)}, u32[]{:S(2)}) copy-start(bf16[256,384]{1,0:T(8,128)(2,1)} %constant.13.clone.first_ref) | copy-start | bytes 589828
  21.5 28.6 %copy-start.10 = (f32[3,3,256]{2,1,0:T(4,128)S(1)}, f32[3,3,256]{2,1,0:T(4,128)}, u32[]{:S(2)}) copy-start(f32[3,3,256]{2,1,0:T(4,128)} %short_ref.3) | copy-start | bytes 27652
  21.5 28.6 %copy-start.11 = (f32[256]{0:T(256)S(1)}, f32[256]{0:T(256)}, u32[]{:S(2)}) copy-start(f32[256]{0:T(256)} %param.16) | copy-start | bytes 3076
  21.6 28.5 %all-to-all-start.1 = ((bf16[128,2,384]{2,1,0:T(2,128)(2,1)}), bf16[128,2,384]{2,1,0:T(2,128)(2,1)S(1)}, u32[]{:S(2)}, u32[]{:S(2)}) async-start(bf16[128,2,384]{2,1,0:T(2,128)(2,1)} %bitcast.3), calls=%async_computation.1 | async-start | bytes 393216 | tf_op jit(solution)/shard_map/all_to_all | solution.py:409
  39.1 4.8 %collective-permute-start = (bf16[768,256]{1,0:T(8,128)(2,1)S(1)}, bf16[768,256]{1,0:T(8,128)(2,1)S(1)}, u32[]{:S(2)}, u32[]{:S(2)}) collective-permute-start(bf16[768,256]{1,0:T(8,128)(2,1)S(1)} %get-tuple-element.22), channel_id=1, source_target_pairs={{0,1},{1,0},{2,3},{3,2},{4,5},{5,4},{6,7},{7,6},{8,9},{9,8},{10,11... | collective-permute-start | bytes 1179656 | tf_op jit(solution)/shard_map/ppermute | solution.py:391
  44.1 10.3 %collective-permute-start.1 = (bf16[128,256]{1,0:T(8,128)(2,1)S(1)}, bf16[128,256]{1,0:T(8,128)(2,1)S(1)}, u32[]{:S(2)}, u32[]{:S(2)}) collective-permute-start(bf16[128,256]{1,0:T(8,128)(2,1)S(1)} %get-tuple-element.23), channel_id=1, source_target_pairs={{0,2},{1,3},{2,0},{3,1},{4,6},{5,7},{6,4},{7,5},{8,10},{9,11},{10,... | collective-permute-start | bytes 196616 | tf_op jit(solution)/shard_map/ppermute | solution.py:391
  50.1 0.9 %copy-start.7 = (f32[2,128,128]{2,1,0:T(8,128)S(1)}, f32[2,128,128]{2,1,0:T(8,128)}, u32[]{:S(2)}) copy-start(f32[2,128,128]{2,1,0:T(8,128)} %constant.14.clone.twist_ref) | copy-start | bytes 393220
  51.0 0.8 copy-start.9
  54.4 22.4 %all-to-all-start.2 = ((bf16[128,2,128]{2,1,0:T(2,128)(2,1)}), bf16[128,2,128]{2,1,0:T(2,128)(2,1)S(1)}, u32[]{:S(2)}, u32[]{:S(2)}) async-start(bf16[128,2,128]{2,1,0:T(2,128)(2,1)} %bitcast.8), calls=%async_computation.2 | async-start | bytes 131072 | tf_op jit(solution)/shard_map/all_to_all | solution.py:417
  68.1 17.9 %collective-permute-start.3 = (bf16[512,256]{1,0:T(8,128)(2,1)S(1)}, bf16[512,256]{1,0:T(8,128)(2,1)S(1)}, u32[]{:S(2)}, u32[]{:S(2)}) collective-permute-start(bf16[512,256]{1,0:T(8,128)(2,1)S(1)} %get-tuple-element.30), channel_id=1, source_target_pairs={{0,2},{1,3},{2,0},{3,1},{4,6},{5,7},{6,4},{7,5},{8,10},{9,11},{10,... | collective-permute-start | bytes 786440 | tf_op jit(solution)/shard_map/ppermute | solution.py:391
  71.8 4.9 %collective-permute-start.2 = (f32[8,256]{1,0:T(8,128)S(1)}, f32[8,256]{1,0:T(8,128)S(1)}, u32[]{:S(2)}, u32[]{:S(2)}) collective-permute-start(f32[8,256]{1,0:T(8,128)S(1)} %get-tuple-element.28), channel_id=1, source_target_pairs={{0,4},{4,8},{8,12},{12,16},{16,20},{20,24},{24,28},{28,32},{32,36}... | collective-permute-start | bytes 24584 | tf_op jit(solution)/shard_map/ppermute | solution.py:414

commit v8 on v7

--- a/solution.py
+++ b/solution.py
@@ -176,7 +176,7 @@
     return jnp.where(col < by, carried, moved)
 
 
-def convolve_kernel(code_ref, order_ref, short_ref, skip_ref, first_ref, twist_ref, mid_ref, inv_ref, last_ref, out_ref, now_ref, mix_ref):
+def convolve_kernel(code_ref, order_ref, short_ref, skip_ref, first_ref, twist_ref, mid_ref, last_ref, out_ref, now_ref, mix_ref):
     rows, cols = twist_ref.shape[1:]
     now_ref[...] = code_ref[...].astype(jnp.float32)
     shift = short_ref.shape[2] - 2 * group_place(lax.axis_index("seq"), rows)
@@ -207,13 +207,13 @@
     for j in range(2):
         s_re, s_im = freq[j * rows : (j + 1) * rows, :cols], freq[j * rows : (j + 1) * rows, cols:]
         h_re, h_im = freq[(2 + j) * rows : (3 + j) * rows, :cols], freq[(2 + j) * rows : (3 + j) * rows, cols:]
-        both.append(jnp.concatenate([s_re * h_re - s_im * h_im, s_re * h_im + s_im * h_re], axis=1))
-    back = dot_right(jnp.concatenate(both, axis=0), inv_ref[...])
+        both.append(jnp.concatenate([s_re * h_re - s_im * h_im, -s_re * h_im - s_im * h_re], axis=1))
+    back = dot_right(jnp.concatenate(both, axis=0), mid_ref[...])
     real, imag = [], []
     for j in range(2):
         re, im = back[j * rows : (j + 1) * rows, :cols], back[j * rows : (j + 1) * rows, cols:]
-        real.append(re * t_re + im * t_im)
-        imag.append(im * t_re - re * t_im)
+        real.append(re * t_re - im * t_im)
+        imag.append(-im * t_re - re * t_im)
     stacked = jnp.concatenate([jnp.concatenate(real, axis=1), jnp.concatenate(imag, axis=1)], axis=0)
     convolved = dot_left(last_ref[...], stacked)
     for j in range(2):
@@ -248,7 +248,6 @@
         at_left(np.concatenate([first.real, first.imag])),
         jnp.asarray(np.stack([twist.real, twist.imag]).astype(np.float32)),
         at_right(np.block([[second.real, second.imag], [-second.imag, second.real]])),
-        at_right(np.block([[second.real, -second.imag], [second.imag, second.real]])),
         at_left(np.concatenate([first.real.T, first.imag.T], axis=1) / total),
     )
 
@@ -258,7 +257,7 @@
     order_table = jnp.asarray(np.stack([np.eye(rows)[place], np.eye(rows)[order]]), jnp.bfloat16)
     return pl.pallas_call(
         convolve_kernel,
-        in_specs=[VMEM] * 9,
+        in_specs=[VMEM] * 8,
         out_specs=VMEM,
         out_shape=jax.ShapeDtypeStruct((2 * rows, cols), jnp.bfloat16),
         scratch_shapes=[pltpu.VMEM((6 * rows, cols), jnp.float32), pltpu.VMEM((2 * rows, cols), jnp.float32)],

time: 88.2 us -> 86.5 us (0.981)
  local copies, waits for them, and re-layouts: 1.79 us -> 0.06 us
    unnamed x24 -> x22, local copies, waits for them, and re-layouts: 1.79 us -> 0.06 us
where the time goes in v8:
time: 86.5 us; the launch traced here: 85.4 us
  starting transfers between devices  41.6 us (48%)
  blocking collectives  28 us (32%)
  waiting for transfers between devices  8.58 us (10%)
  Pallas kernels  6.93 us (8%)
    all_to_all x1, blocking collectives, on_device(): parts = lax.all_to_all(partial, 'fsdp', 0, 0, tiled=True)  18.7 us
    all_to_all x1, starting transfers between devices, on_device(): lax.all_to_all(packed.reshape(seq_count, 2, -1), 'seq', 0, 0, tiled=True,...  17.2 us
    all_to_all x1, starting transfers between devices, on_device(): lax.all_to_all(coded.reshape(seq_count, 2, local_tok), 'seq', 0, 0, tiled...  14.4 us
    all_gather x1, blocking collectives, on_device(): gathered = lax.all_gather(gated, 'fsdp', axis=0, tiled=True)  9.32 us
    ppermute x3, starting transfers between devices, exchanged(): lax.ppermute(piece, axis, [(i, i ^ step) for i in range(lax.axis_size(axi...  8.37 us
    all_to_all x1, waiting for transfers between devices, on_device(): lax.all_to_all(packed.reshape(seq_count, 2, -1), 'seq', 0, 0, tiled=True,...  3.98 us
    ppermute x1, waiting for transfers between devices, on_device(): edge = lax.ppermute(edge, 'seq', [(i, i + 1) for i in range(seq_count - 1)])  3.27 us
    pallas_call x1, Pallas kernels, convolve(): pl.pallas_call(convolve_kernel, in_specs=[VMEM] * 8, out_specs=VMEM, out_...  2.51 us
  transfers between devices with their start and end apart: 6, of which 3 were waited for; matrix products, arithmetic and copies ran while one was open for 0% of the time, Pallas kernels for 4%

profile of v8, /device:TPU:1, one launch (start us, length us, event | category | flops | bytes accessed | tf_op | source)
XLA Modules:
  0.0 85.4 jit_solution(5840574758379997928)
XLA Ops:
  0.0 0.0 copy-start.6
  0.0 1.6 %project.1 = bf16[4,2,128,256]{3,2,1,0:T(8,128)(2,1)S(1)} custom-call(bf16[128,256]{1,0:T(8,128)(2,1)} %tokens_ref, bf16[3,256,1024]{2,1,0:T(8,128)(2,1)} %bitcast.14), custom_call_target="tpu_custom_call" | custom-call | tf_op jit(solution)/shard_map/project/pallas_call | solution.py:56
  1.6 0.0 copy-start
  1.7 0.0 copy-start.1
  1.7 0.0 copy-start.3
  1.7 18.7 %all_to_all.15.parts_ref = bf16[4,2,128,256]{3,2,1,0:T(8,128)(2,1)S(1)} all-to-all(bf16[4,2,128,256]{3,2,1,0:T(8,128)(2,1)S(1)} %project.1), channel_id=1, replica_groups=mesh['seq'=128,'fsdp'=4] {'fsdp'}, dimensions={0} | all-to-all | bytes 1048576 | tf_op jit(solution)/shard_map/all_to_all | solution.py:401
  20.4 0.0 copy-done.6
  20.4 1.1 %pack.1 = bf16[768,128]{1,0:T(8,128)(2,1)} custom-call(bf16[4,2,128,256]{3,2,1,0:T(8,128)(2,1)S(1)} %all_to_all.15.parts_ref, f32[256,128]{1,0:T(8,128)S(1)} %copy-done.6), custom_call_target="tpu_custom_call" | custom-call | tf_op jit(solution)/shard_map/pack/pallas_call | solution.py:119
  21.5 0.0 copy-start.2
  21.5 0.0 copy-start.4
  21.5 0.0 copy-start.5
  21.5 0.0 copy-start.7
  21.5 0.0 copy-start.8
  21.5 0.0 copy-start.9
  21.5 0.0 copy-start.10
  21.6 17.2 %all-to-all-start.1 = ((bf16[128,2,384]{2,1,0:T(2,128)(2,1)}), bf16[128,2,384]{2,1,0:T(2,128)(2,1)S(1)}, u32[]{:S(2)}, u32[]{:S(2)}) async-start(bf16[128,2,384]{2,1,0:T(2,128)(2,1)} %bitcast.3), calls=%async_computation.1 | async-start | bytes 393216 | tf_op jit(solution)/shard_map/all_to_all | solution.py:408
  38.8 0.0 copy-done
  38.8 0.0 copy-done.1
  38.8 0.0 copy-done.3
  38.8 0.3 project_query.1
  39.1 3.5 %collective-permute-start = (bf16[768,256]{1,0:T(8,128)(2,1)S(1)}, bf16[768,256]{1,0:T(8,128)(2,1)S(1)}, u32[]{:S(2)}, u32[]{:S(2)}) collective-permute-start(bf16[768,256]{1,0:T(8,128)(2,1)S(1)} %get-tuple-element.22), channel_id=1, source_target_pairs={{0,1},{1,0},{2,3},{3,2},{4,5},{5,4},{6,7},{7,6},{8,9},{9,8},{10,11... | collective-permute-start | bytes 1179656 | tf_op jit(solution)/shard_map/ppermute | solution.py:390
  42.6 1.3 %collective-permute-done.from_mate_ref = bf16[768,256]{1,0:T(8,128)(2,1)S(1)} collective-permute-done((bf16[768,256]{1,0:T(8,128)(2,1)S(1)}, bf16[768,256]{1,0:T(8,128)(2,1)S(1)}, u32[]{:S(2)}, u32[]{:S(2)}) %collective-permute-start) | collective-permute-done | bytes 393248 | tf_op jit(solution)/shard_map/ppermute | solution.py:390
  43.9 0.2 pair_query.1
  44.1 2.0 %collective-permute-start.1 = (bf16[128,256]{1,0:T(8,128)(2,1)S(1)}, bf16[128,256]{1,0:T(8,128)(2,1)S(1)}, u32[]{:S(2)}, u32[]{:S(2)}) collective-permute-start(bf16[128,256]{1,0:T(8,128)(2,1)S(1)} %get-tuple-element.23), channel_id=1, source_target_pairs={{0,2},{1,3},{2,0},{3,1},{4,6},{5,7},{6,4},{7,5},{8,10},{9,11},{10,... | collective-permute-start | bytes 196616 | tf_op jit(solution)/shard_map/ppermute | solution.py:390
  46.1 4.0 %all-to-all-done.1 = bf16[128,2,384]{2,1,0:T(2,128)(2,1)S(1)} async-done(((bf16[128,2,384]{2,1,0:T(2,128)(2,1)}), bf16[128,2,384]{2,1,0:T(2,128)(2,1)S(1)}, u32[]{:S(2)}, u32[]{:S(2)}) %all-to-all-start.1) | async-done | bytes 196640 | tf_op jit(solution)/shard_map/all_to_all | solution.py:408
  50.1 0.0 copy-done.2
  50.1 0.0 copy-done.4
  50.1 0.0 copy-done.5
  50.1 0.0 copy-done.7
  50.1 0.0 copy-done.8
  50.1 0.0 copy-done.9
  50.1 0.0 copy-done.10
  50.1 2.5 %convolve.1 = bf16[256,128]{1,0:T(8,128)(2,1)} custom-call(bf16[768,128]{1,0:T(8,128)(2,1)S(1)} %bitcast.16, bf16[2,128,128]{2,1,0:T(8,128)(2,1)S(1)} %copy-done.8, f32[3,3,256]{2,1,0:T(4,128)S(1)} %copy-done.9, f32[1,256]{1,0:T(1,128)S(1)} %bitcast.18, bf16[256,384]{1,0:T(8,128)(2,1)S(1)} %copy-done.5, f32[2,128,128]{2,1,0:T(8,128)S(1)} %copy-done.7, ...), custom_call_target="tpu_custom_call" | custom-call | tf_op jit(solution)/shard_map/convolve/pallas_call | solution.py:258
  52.6 0.0 collective-permute-done.1.code_ref
  52.6 14.4 %all-to-all-start.2 = ((bf16[128,2,128]{2,1,0:T(2,128)(2,1)}), bf16[128,2,128]{2,1,0:T(2,128)(2,1)S(1)}, u32[]{:S(2)}, u32[]{:S(2)}) async-start(bf16[128,2,128]{2,1,0:T(2,128)(2,1)} %bitcast.8), calls=%async_computation.2 | async-start | bytes 131072 | tf_op jit(solution)/shard_map/all_to_all | solution.py:416
  67.1 0.1 sum_query.1
  67.1 2.9 %collective-permute-start.3 = (bf16[512,256]{1,0:T(8,128)(2,1)S(1)}, bf16[512,256]{1,0:T(8,128)(2,1)S(1)}, u32[]{:S(2)}, u32[]{:S(2)}) collective-permute-start(bf16[512,256]{1,0:T(8,128)(2,1)S(1)} %get-tuple-element.30), channel_id=1, source_target_pairs={{0,2},{1,3},{2,0},{3,1},{4,6},{5,7},{6,4},{7,5},{8,10},{9,11},{10,... | collective-permute-start | bytes 786440 | tf_op jit(solution)/shard_map/ppermute | solution.py:390
  70.0 1.6 %collective-permute-start.2 = (f32[8,256]{1,0:T(8,128)S(1)}, f32[8,256]{1,0:T(8,128)S(1)}, u32[]{:S(2)}, u32[]{:S(2)}) collective-permute-start(f32[8,256]{1,0:T(8,128)S(1)} %get-tuple-element.28), channel_id=1, source_target_pairs={{0,4},{4,8},{8,12},{12,16},{16,20},{20,24},{24,28},{28,32},{32,36}... | collective-permute-start | bytes 24584 | tf_op jit(solution)/shard_map/ppermute | solution.py:413
  71.6 3.3 %collective-permute-done.2.edge_ref = f32[8,256]{1,0:T(8,128)S(1)} collective-permute-done((f32[8,256]{1,0:T(8,128)S(1)}, f32[8,256]{1,0:T(8,128)S(1)}, u32[]{:S(2)}, u32[]{:S(2)}) %collective-permute-start.2) | collective-permute-done | bytes 8224 | tf_op jit(solution)/shard_map/ppermute | solution.py:413
  74.9 0.1 mix_query.1.query_ref
  75.0 0.0 all-to-all-done.2
  75.0 9.3 %all_gather.3.gated_ref = bf16[1024,128]{1,0:T(8,128)(2,1)S(1)} all-gather(bf16[256,128]{1,0:T(8,128)(2,1)S(1)} %gate.1), channel_id=1, replica_groups=mesh['seq'=128,'fsdp'=4] {'fsdp'}, dimensions={0}, use_global_device_ids=true | all-gather | bytes 327680 | tf_op jit(solution)/shard_map/all_gather | solution.py:418
  84.4 0.0 collective-permute-done.3.far_ref
  84.4 1.0 %output.1 = f32[128,256]{1,0:T(8,128)} custom-call(bf16[1024,128]{1,0:T(8,128)(2,1)S(1)} %all_gather.3.gated_ref, bf16[1024,256]{1,0:T(8,128)(2,1)S(1)} %copy-done.1, bf16[768,256]{1,0:T(8,128)(2,1)S(1)} %collective-permute-done.from_mate_ref, bf16[512,256]{1,0:T(8,128)(2,1)S(1)} %collective-permute-done.3.far_ref), custom_call_target="tpu_custom_call" | custom-call | tf_op jit(solution)/shard_map/output/pallas_call | solution.py:379
  (1 shorter events, 0.0 us)
Async XLA Ops:
  0.0 20.4 %copy-start.6 = (f32[256,128]{1,0:T(8,128)S(1)}, f32[256,128]{1,0:T(8,128)}, u32[]{:S(2)}) copy-start(f32[256,128]{1,0:T(8,128)} %taps_ref.1) | copy-start | bytes 393220
  1.6 37.1 %copy-start = (bf16[256,3,1024]{2,0,1:T(8,128)(2,1)S(1)}, bf16[256,3,1024]{2,0,1:T(8,128)(2,1)}, u32[]{:S(2)}) copy-start(bf16[256,3,1024]{2,0,1:T(8,128)(2,1)} %param.12) | copy-start | bytes 4718596
  1.7 37.1 %copy-start.1 = (bf16[1024,256]{1,0:T(8,128)(2,1)S(1)}, bf16[1024,256]{1,0:T(8,128)(2,1)}, u32[]{:S(2)}) copy-start(bf16[1024,256]{1,0:T(8,128)(2,1)} %w_out_ref.2) | copy-start | bytes 1572868
  1.7 37.1 %copy-start.3 = (bf16[128,256]{1,0:T(8,128)(2,1)S(1)}, bf16[128,256]{1,0:T(8,128)(2,1)}, u32[]{:S(2)}) copy-start(bf16[128,256]{1,0:T(8,128)(2,1)} %tokens_ref) | copy-start | bytes 196612
  21.5 28.6 %copy-start.2 = (bf16[768,256]{1,0:T(8,128)(2,1)S(1)}, bf16[768,256]{1,0:T(8,128)(2,1)}, u32[]{:S(2)}) copy-start(bf16[768,256]{1,0:T(8,128)(2,1)} %constant.13.clone.mid_ref) | copy-start | bytes 1179652
  21.5 28.6 %copy-start.4 = (bf16[128,768]{1,0:T(8,128)(2,1)S(1)}, bf16[128,768]{1,0:T(8,128)(2,1)}, u32[]{:S(2)}) copy-start(bf16[128,768]{1,0:T(8,128)(2,1)} %constant.14.clone.last_ref) | copy-start | bytes 589828
  21.5 28.6 %copy-start.5 = (bf16[256,384]{1,0:T(8,128)(2,1)S(1)}, bf16[256,384]{1,0:T(8,128)(2,1)}, u32[]{:S(2)}) copy-start(bf16[256,384]{1,0:T(8,128)(2,1)} %constant.11.clone.first_ref) | copy-start | bytes 589828
  21.5 28.6 %copy-start.7 = (f32[2,128,128]{2,1,0:T(8,128)S(1)}, f32[2,128,128]{2,1,0:T(8,128)}, u32[]{:S(2)}) copy-start(f32[2,128,128]{2,1,0:T(8,128)} %constant.12.clone.twist_ref) | copy-start | bytes 393220
  21.5 28.6 %copy-start.8 = (bf16[2,128,128]{2,1,0:T(8,128)(2,1)S(1)}, bf16[2,128,128]{2,1,0:T(8,128)(2,1)}, u32[]{:S(2)}) copy-start(bf16[2,128,128]{2,1,0:T(8,128)(2,1)} %constant.10.clone.order_ref) | copy-start | bytes 196612
  21.5 28.6 %copy-start.9 = (f32[3,3,256]{2,1,0:T(4,128)S(1)}, f32[3,3,256]{2,1,0:T(4,128)}, u32[]{:S(2)}) copy-start(f32[3,3,256]{2,1,0:T(4,128)} %short_ref.3) | copy-start | bytes 27652
  21.5 28.6 %copy-start.10 = (f32[256]{0:T(256)S(1)}, f32[256]{0:T(256)}, u32[]{:S(2)}) copy-start(f32[256]{0:T(256)} %param.15) | copy-start | bytes 3076
  21.6 28.5 %all-to-all-start.1 = ((bf16[128,2,384]{2,1,0:T(2,128)(2,1)}), bf16[128,2,384]{2,1,0:T(2,128)(2,1)S(1)}, u32[]{:S(2)}, u32[]{:S(2)}) async-start(bf16[128,2,384]{2,1,0:T(2,128)(2,1)} %bitcast.3), calls=%async_computation.1 | async-start | bytes 393216 | tf_op jit(solution)/shard_map/all_to_all | solution.py:408
  39.1 4.8 %collective-permute-start = (bf16[768,256]{1,0:T(8,128)(2,1)S(1)}, bf16[768,256]{1,0:T(8,128)(2,1)S(1)}, u32[]{:S(2)}, u32[]{:S(2)}) collective-permute-start(bf16[768,256]{1,0:T(8,128)(2,1)S(1)} %get-tuple-element.22), channel_id=1, source_target_pairs={{0,1},{1,0},{2,3},{3,2},{4,5},{5,4},{6,7},{7,6},{8,9},{9,8},{10,11... | collective-permute-start | bytes 1179656 | tf_op jit(solution)/shard_map/ppermute | solution.py:390
  44.1 8.5 %collective-permute-start.1 = (bf16[128,256]{1,0:T(8,128)(2,1)S(1)}, bf16[128,256]{1,0:T(8,128)(2,1)S(1)}, u32[]{:S(2)}, u32[]{:S(2)}) collective-permute-start(bf16[128,256]{1,0:T(8,128)(2,1)S(1)} %get-tuple-element.23), channel_id=1, source_target_pairs={{0,2},{1,3},{2,0},{3,1},{4,6},{5,7},{6,4},{7,5},{8,10},{9,11},{10,... | collective-permute-start | bytes 196616 | tf_op jit(solution)/shard_map/ppermute | solution.py:390
  52.6 22.3 %all-to-all-start.2 = ((bf16[128,2,128]{2,1,0:T(2,128)(2,1)}), bf16[128,2,128]{2,1,0:T(2,128)(2,1)S(1)}, u32[]{:S(2)}, u32[]{:S(2)}) async-start(bf16[128,2,128]{2,1,0:T(2,128)(2,1)} %bitcast.8), calls=%async_computation.2 | async-start | bytes 131072 | tf_op jit(solution)/shard_map/all_to_all | solution.py:416
  67.1 17.2 %collective-permute-start.3 = (bf16[512,256]{1,0:T(8,128)(2,1)S(1)}, bf16[512,256]{1,0:T(8,128)(2,1)S(1)}, u32[]{:S(2)}, u32[]{:S(2)}) collective-permute-start(bf16[512,256]{1,0:T(8,128)(2,1)S(1)} %get-tuple-element.30), channel_id=1, source_target_pairs={{0,2},{1,3},{2,0},{3,1},{4,6},{5,7},{6,4},{7,5},{8,10},{9,11},{10,... | collective-permute-start | bytes 786440 | tf_op jit(solution)/shard_map/ppermute | solution.py:390
  70.0 4.9 %collective-permute-start.2 = (f32[8,256]{1,0:T(8,128)S(1)}, f32[8,256]{1,0:T(8,128)S(1)}, u32[]{:S(2)}, u32[]{:S(2)}) collective-permute-start(f32[8,256]{1,0:T(8,128)S(1)} %get-tuple-element.28), channel_id=1, source_target_pairs={{0,4},{4,8},{8,12},{12,16},{16,20},{20,24},{24,28},{28,32},{32,36}... | collective-permute-start | bytes 24584 | tf_op jit(solution)/shard_map/ppermute | solution.py:413

commit v9 on v8

--- a/solution.py
+++ b/solution.py
@@ -183,9 +183,11 @@
     short = [pltpu.roll(short_ref[tap], shift, 1) for tap in range(3)]
     skip = pltpu.roll(skip_ref[...], shift, 1)
 
+    codes = [now_ref[pl.ds(row, rows, stride=6), :].astype(jnp.bfloat16) for row in range(6)]
+    codes = jnp.dot(order_ref[0], jnp.concatenate(codes, axis=1), preferred_element_type=jnp.float32)
+
     def in_order(row):
-        code = now_ref[pl.ds(row, rows, stride=6), :].astype(jnp.bfloat16)
-        return decode(jnp.dot(order_ref[0], code, preferred_element_type=jnp.float32))
+        return decode(codes[:, row * cols : (row + 1) * cols])
 
     def mixed(kind, j):
         block = in_order(2 * kind + j) * (1.0 / PROJ_SCALE)
@@ -216,11 +218,12 @@
         imag.append(-im * t_re - re * t_im)
     stacked = jnp.concatenate([jnp.concatenate(real, axis=1), jnp.concatenate(imag, axis=1)], axis=0)
     convolved = dot_left(last_ref[...], stacked)
+    outcomes = [convolved[:, j * cols : (j + 1) * cols] + skip[:, j : j + 1] * signal[j] for j in range(2)]
+    outcome = jnp.concatenate(outcomes, axis=1)
+    code = (outcome * jnp.abs(outcome)).astype(jnp.bfloat16)
+    code = jnp.dot(order_ref[1], code, preferred_element_type=jnp.float32)
     for j in range(2):
-        outcome = convolved[:, j * cols : (j + 1) * cols] + skip[:, j : j + 1] * signal[j]
-        code = (outcome * jnp.abs(outcome)).astype(jnp.bfloat16)
-        code = jnp.dot(order_ref[1], code, preferred_element_type=jnp.float32)
-        mix_ref[pl.ds(j, rows, stride=2), :] = code
+        mix_ref[pl.ds(j, rows, stride=2), :] = code[:, j * cols : (j + 1) * cols]
     out_ref[...] = mix_ref[...].astype(jnp.bfloat16)
 
 

time: 86.5 us -> 86.5 us (level)
  no operation moved by 1% of the time
where the time goes in v9:
time: 86.5 us; the launch traced here: 85.4 us
  starting transfers between devices  41.6 us (48%)
  blocking collectives  28 us (32%)
  waiting for transfers between devices  8.58 us (10%)
  Pallas kernels  6.95 us (8%)
    all_to_all x1, blocking collectives, on_device(): parts = lax.all_to_all(partial, 'fsdp', 0, 0, tiled=True)  18.7 us
    all_to_all x1, starting transfers between devices, on_device(): lax.all_to_all(packed.reshape(seq_count, 2, -1), 'seq', 0, 0, tiled=True,...  17.2 us
    all_to_all x1, starting transfers between devices, on_device(): lax.all_to_all(coded.reshape(seq_count, 2, local_tok), 'seq', 0, 0, tiled...  14.4 us
    all_gather x1, blocking collectives, on_device(): gathered = lax.all_gather(gated, 'fsdp', axis=0, tiled=True)  9.32 us
    ppermute x3, starting transfers between devices, exchanged(): lax.ppermute(piece, axis, [(i, i ^ step) for i in range(lax.axis_size(axi...  8.39 us
    all_to_all x1, waiting for transfers between devices, on_device(): lax.all_to_all(packed.reshape(seq_count, 2, -1), 'seq', 0, 0, tiled=True,...  3.98 us
    ppermute x1, waiting for transfers between devices, on_device(): edge = lax.ppermute(edge, 'seq', [(i, i + 1) for i in range(seq_count - 1)])  3.26 us
    pallas_call x1, Pallas kernels, convolve(): pl.pallas_call(convolve_kernel, in_specs=[VMEM] * 8, out_specs=VMEM, out_...  2.53 us
  transfers between devices with their start and end apart: 6, of which 3 were waited for; matrix products, arithmetic and copies ran while one was open for 0% of the time, Pallas kernels for 4%

profile of v9, /device:TPU:1, one launch (start us, length us, event | category | flops | bytes accessed | tf_op | source)
XLA Modules:
  0.0 85.4 jit_solution(3918798762790750482)
XLA Ops:
  0.0 0.0 copy-start.6
  0.0 1.6 %project.1 = bf16[4,2,128,256]{3,2,1,0:T(8,128)(2,1)S(1)} custom-call(bf16[128,256]{1,0:T(8,128)(2,1)} %tokens_ref, bf16[3,256,1024]{2,1,0:T(8,128)(2,1)} %bitcast.14), custom_call_target="tpu_custom_call" | custom-call | tf_op jit(solution)/shard_map/project/pallas_call | solution.py:56
  1.6 0.0 copy-start
  1.7 0.0 copy-start.1
  1.7 0.0 copy-start.3
  1.7 18.7 %all_to_all.15.parts_ref = bf16[4,2,128,256]{3,2,1,0:T(8,128)(2,1)S(1)} all-to-all(bf16[4,2,128,256]{3,2,1,0:T(8,128)(2,1)S(1)} %project.1), channel_id=1, replica_groups=mesh['seq'=128,'fsdp'=4] {'fsdp'}, dimensions={0} | all-to-all | bytes 1048576 | tf_op jit(solution)/shard_map/all_to_all | solution.py:404
  20.4 0.0 copy-done.6
  20.4 1.1 %pack.1 = bf16[768,128]{1,0:T(8,128)(2,1)} custom-call(bf16[4,2,128,256]{3,2,1,0:T(8,128)(2,1)S(1)} %all_to_all.15.parts_ref, f32[256,128]{1,0:T(8,128)S(1)} %copy-done.6), custom_call_target="tpu_custom_call" | custom-call | tf_op jit(solution)/shard_map/pack/pallas_call | solution.py:119
  21.5 0.0 copy-start.2
  21.5 0.0 copy-start.4
  21.5 0.0 copy-start.5
  21.5 0.0 copy-start.7
  21.5 0.0 copy-start.8
  21.5 0.0 copy-start.9
  21.5 0.0 copy-start.10
  21.6 17.2 %all-to-all-start.1 = ((bf16[128,2,384]{2,1,0:T(2,128)(2,1)}), bf16[128,2,384]{2,1,0:T(2,128)(2,1)S(1)}, u32[]{:S(2)}, u32[]{:S(2)}) async-start(bf16[128,2,384]{2,1,0:T(2,128)(2,1)} %bitcast.3), calls=%async_computation.1 | async-start | bytes 393216 | tf_op jit(solution)/shard_map/all_to_all | solution.py:411
  38.8 0.0 copy-done
  38.8 0.0 copy-done.1
  38.8 0.0 copy-done.3
  38.8 0.3 project_query.1
  39.1 3.5 %collective-permute-start = (bf16[768,256]{1,0:T(8,128)(2,1)S(1)}, bf16[768,256]{1,0:T(8,128)(2,1)S(1)}, u32[]{:S(2)}, u32[]{:S(2)}) collective-permute-start(bf16[768,256]{1,0:T(8,128)(2,1)S(1)} %get-tuple-element.22), channel_id=1, source_target_pairs={{0,1},{1,0},{2,3},{3,2},{4,5},{5,4},{6,7},{7,6},{8,9},{9,8},{10,11... | collective-permute-start | bytes 1179656 | tf_op jit(solution)/shard_map/ppermute | solution.py:393
  42.6 1.3 %collective-permute-done.from_mate_ref = bf16[768,256]{1,0:T(8,128)(2,1)S(1)} collective-permute-done((bf16[768,256]{1,0:T(8,128)(2,1)S(1)}, bf16[768,256]{1,0:T(8,128)(2,1)S(1)}, u32[]{:S(2)}, u32[]{:S(2)}) %collective-permute-start) | collective-permute-done | bytes 393248 | tf_op jit(solution)/shard_map/ppermute | solution.py:393
  43.9 0.2 pair_query.1
  44.1 2.0 %collective-permute-start.1 = (bf16[128,256]{1,0:T(8,128)(2,1)S(1)}, bf16[128,256]{1,0:T(8,128)(2,1)S(1)}, u32[]{:S(2)}, u32[]{:S(2)}) collective-permute-start(bf16[128,256]{1,0:T(8,128)(2,1)S(1)} %get-tuple-element.23), channel_id=1, source_target_pairs={{0,2},{1,3},{2,0},{3,1},{4,6},{5,7},{6,4},{7,5},{8,10},{9,11},{10,... | collective-permute-start | bytes 196616 | tf_op jit(solution)/shard_map/ppermute | solution.py:393
  46.1 4.0 %all-to-all-done.1 = bf16[128,2,384]{2,1,0:T(2,128)(2,1)S(1)} async-done(((bf16[128,2,384]{2,1,0:T(2,128)(2,1)}), bf16[128,2,384]{2,1,0:T(2,128)(2,1)S(1)}, u32[]{:S(2)}, u32[]{:S(2)}) %all-to-all-start.1) | async-done | bytes 196640 | tf_op jit(solution)/shard_map/all_to_all | solution.py:411
  50.1 0.0 copy-done.2
  50.1 0.0 copy-done.4
  50.1 0.0 copy-done.5
  50.1 0.0 copy-done.7
  50.1 0.0 copy-done.8
  50.1 0.0 copy-done.9
  50.1 0.0 copy-done.10
  50.1 2.5 %convolve.1 = bf16[256,128]{1,0:T(8,128)(2,1)} custom-call(bf16[768,128]{1,0:T(8,128)(2,1)S(1)} %bitcast.16, bf16[2,128,128]{2,1,0:T(8,128)(2,1)S(1)} %copy-done.8, f32[3,3,256]{2,1,0:T(4,128)S(1)} %copy-done.9, f32[1,256]{1,0:T(1,128)S(1)} %bitcast.18, bf16[256,384]{1,0:T(8,128)(2,1)S(1)} %copy-done.5, f32[2,128,128]{2,1,0:T(8,128)S(1)} %copy-done.7, ...), custom_call_target="tpu_custom_call" | custom-call | tf_op jit(solution)/shard_map/convolve/pallas_call | solution.py:261
  52.7 0.0 collective-permute-done.1.code_ref
  52.7 14.4 %all-to-all-start.2 = ((bf16[128,2,128]{2,1,0:T(2,128)(2,1)}), bf16[128,2,128]{2,1,0:T(2,128)(2,1)S(1)}, u32[]{:S(2)}, u32[]{:S(2)}) async-start(bf16[128,2,128]{2,1,0:T(2,128)(2,1)} %bitcast.8), calls=%async_computation.2 | async-start | bytes 131072 | tf_op jit(solution)/shard_map/all_to_all | solution.py:419
  67.1 0.1 sum_query.1
  67.1 2.9 %collective-permute-start.3 = (bf16[512,256]{1,0:T(8,128)(2,1)S(1)}, bf16[512,256]{1,0:T(8,128)(2,1)S(1)}, u32[]{:S(2)}, u32[]{:S(2)}) collective-permute-start(bf16[512,256]{1,0:T(8,128)(2,1)S(1)} %get-tuple-element.30), channel_id=1, source_target_pairs={{0,2},{1,3},{2,0},{3,1},{4,6},{5,7},{6,4},{7,5},{8,10},{9,11},{10,... | collective-permute-start | bytes 786440 | tf_op jit(solution)/shard_map/ppermute | solution.py:393
  70.0 1.6 %collective-permute-start.2 = (f32[8,256]{1,0:T(8,128)S(1)}, f32[8,256]{1,0:T(8,128)S(1)}, u32[]{:S(2)}, u32[]{:S(2)}) collective-permute-start(f32[8,256]{1,0:T(8,128)S(1)} %get-tuple-element.28), channel_id=1, source_target_pairs={{0,4},{4,8},{8,12},{12,16},{16,20},{20,24},{24,28},{28,32},{32,36}... | collective-permute-start | bytes 24584 | tf_op jit(solution)/shard_map/ppermute | solution.py:416
  71.6 3.3 %collective-permute-done.2.edge_ref = f32[8,256]{1,0:T(8,128)S(1)} collective-permute-done((f32[8,256]{1,0:T(8,128)S(1)}, f32[8,256]{1,0:T(8,128)S(1)}, u32[]{:S(2)}, u32[]{:S(2)}) %collective-permute-start.2) | collective-permute-done | bytes 8224 | tf_op jit(solution)/shard_map/ppermute | solution.py:416
  74.9 0.1 mix_query.1.query_ref
  75.0 0.0 all-to-all-done.2
  75.1 9.3 %all_gather.3.gated_ref = bf16[1024,128]{1,0:T(8,128)(2,1)S(1)} all-gather(bf16[256,128]{1,0:T(8,128)(2,1)S(1)} %gate.1), channel_id=1, replica_groups=mesh['seq'=128,'fsdp'=4] {'fsdp'}, dimensions={0}, use_global_device_ids=true | all-gather | bytes 327680 | tf_op jit(solution)/shard_map/all_gather | solution.py:421
  84.4 0.0 collective-permute-done.3.far_ref
  84.4 1.0 %output.1 = f32[128,256]{1,0:T(8,128)} custom-call(bf16[1024,128]{1,0:T(8,128)(2,1)S(1)} %all_gather.3.gated_ref, bf16[1024,256]{1,0:T(8,128)(2,1)S(1)} %copy-done.1, bf16[768,256]{1,0:T(8,128)(2,1)S(1)} %collective-permute-done.from_mate_ref, bf16[512,256]{1,0:T(8,128)(2,1)S(1)} %collective-permute-done.3.far_ref), custom_call_target="tpu_custom_call" | custom-call | tf_op jit(solution)/shard_map/output/pallas_call | solution.py:382
  (1 shorter events, 0.0 us)
Async XLA Ops:
  0.0 20.4 %copy-start.6 = (f32[256,128]{1,0:T(8,128)S(1)}, f32[256,128]{1,0:T(8,128)}, u32[]{:S(2)}) copy-start(f32[256,128]{1,0:T(8,128)} %taps_ref.1) | copy-start | bytes 393220
  1.6 37.1 %copy-start = (bf16[256,3,1024]{2,0,1:T(8,128)(2,1)S(1)}, bf16[256,3,1024]{2,0,1:T(8,128)(2,1)}, u32[]{:S(2)}) copy-start(bf16[256,3,1024]{2,0,1:T(8,128)(2,1)} %param.12) | copy-start | bytes 4718596
  1.7 37.1 %copy-start.1 = (bf16[1024,256]{1,0:T(8,128)(2,1)S(1)}, bf16[1024,256]{1,0:T(8,128)(2,1)}, u32[]{:S(2)}) copy-start(bf16[1024,256]{1,0:T(8,128)(2,1)} %w_out_ref.2) | copy-start | bytes 1572868
  1.7 37.1 %copy-start.3 = (bf16[128,256]{1,0:T(8,128)(2,1)S(1)}, bf16[128,256]{1,0:T(8,128)(2,1)}, u32[]{:S(2)}) copy-start(bf16[128,256]{1,0:T(8,128)(2,1)} %tokens_ref) | copy-start | bytes 196612
  21.5 28.6 %copy-start.2 = (bf16[768,256]{1,0:T(8,128)(2,1)S(1)}, bf16[768,256]{1,0:T(8,128)(2,1)}, u32[]{:S(2)}) copy-start(bf16[768,256]{1,0:T(8,128)(2,1)} %constant.13.clone.mid_ref) | copy-start | bytes 1179652
  21.5 28.6 %copy-start.4 = (bf16[128,768]{1,0:T(8,128)(2,1)S(1)}, bf16[128,768]{1,0:T(8,128)(2,1)}, u32[]{:S(2)}) copy-start(bf16[128,768]{1,0:T(8,128)(2,1)} %constant.14.clone.last_ref) | copy-start | bytes 589828
  21.5 28.6 %copy-start.5 = (bf16[256,384]{1,0:T(8,128)(2,1)S(1)}, bf16[256,384]{1,0:T(8,128)(2,1)}, u32[]{:S(2)}) copy-start(bf16[256,384]{1,0:T(8,128)(2,1)} %constant.11.clone.first_ref) | copy-start | bytes 589828
  21.5 28.6 %copy-start.7 = (f32[2,128,128]{2,1,0:T(8,128)S(1)}, f32[2,128,128]{2,1,0:T(8,128)}, u32[]{:S(2)}) copy-start(f32[2,128,128]{2,1,0:T(8,128)} %constant.12.clone.twist_ref) | copy-start | bytes 393220
  21.5 28.6 %copy-start.8 = (bf16[2,128,128]{2,1,0:T(8,128)(2,1)S(1)}, bf16[2,128,128]{2,1,0:T(8,128)(2,1)}, u32[]{:S(2)}) copy-start(bf16[2,128,128]{2,1,0:T(8,128)(2,1)} %constant.10.clone.order_ref) | copy-start | bytes 196612
  21.5 28.6 %copy-start.9 = (f32[3,3,256]{2,1,0:T(4,128)S(1)}, f32[3,3,256]{2,1,0:T(4,128)}, u32[]{:S(2)}) copy-start(f32[3,3,256]{2,1,0:T(4,128)} %short_ref.3) | copy-start | bytes 27652
  21.5 28.6 %copy-start.10 = (f32[256]{0:T(256)S(1)}, f32[256]{0:T(256)}, u32[]{:S(2)}) copy-start(f32[256]{0:T(256)} %param.15) | copy-start | bytes 3076
  21.6 28.5 %all-to-all-start.1 = ((bf16[128,2,384]{2,1,0:T(2,128)(2,1)}), bf16[128,2,384]{2,1,0:T(2,128)(2,1)S(1)}, u32[]{:S(2)}, u32[]{:S(2)}) async-start(bf16[128,2,384]{2,1,0:T(2,128)(2,1)} %bitcast.3), calls=%async_computation.1 | async-start | bytes 393216 | tf_op jit(solution)/shard_map/all_to_all | solution.py:411
  39.1 4.8 %collective-permute-start = (bf16[768,256]{1,0:T(8,128)(2,1)S(1)}, bf16[768,256]{1,0:T(8,128)(2,1)S(1)}, u32[]{:S(2)}, u32[]{:S(2)}) collective-permute-start(bf16[768,256]{1,0:T(8,128)(2,1)S(1)} %get-tuple-element.22), channel_id=1, source_target_pairs={{0,1},{1,0},{2,3},{3,2},{4,5},{5,4},{6,7},{7,6},{8,9},{9,8},{10,11... | collective-permute-start | bytes 1179656 | tf_op jit(solution)/shard_map/ppermute | solution.py:393
  44.1 8.6 %collective-permute-start.1 = (bf16[128,256]{1,0:T(8,128)(2,1)S(1)}, bf16[128,256]{1,0:T(8,128)(2,1)S(1)}, u32[]{:S(2)}, u32[]{:S(2)}) collective-permute-start(bf16[128,256]{1,0:T(8,128)(2,1)S(1)} %get-tuple-element.23), channel_id=1, source_target_pairs={{0,2},{1,3},{2,0},{3,1},{4,6},{5,7},{6,4},{7,5},{8,10},{9,11},{10,... | collective-permute-start | bytes 196616 | tf_op jit(solution)/shard_map/ppermute | solution.py:393
  52.7 22.3 %all-to-all-start.2 = ((bf16[128,2,128]{2,1,0:T(2,128)(2,1)}), bf16[128,2,128]{2,1,0:T(2,128)(2,1)S(1)}, u32[]{:S(2)}, u32[]{:S(2)}) async-start(bf16[128,2,128]{2,1,0:T(2,128)(2,1)} %bitcast.8), calls=%async_computation.2 | async-start | bytes 131072 | tf_op jit(solution)/shard_map/all_to_all | solution.py:419
  67.1 17.2 %collective-permute-start.3 = (bf16[512,256]{1,0:T(8,128)(2,1)S(1)}, bf16[512,256]{1,0:T(8,128)(2,1)S(1)}, u32[]{:S(2)}, u32[]{:S(2)}) collective-permute-start(bf16[512,256]{1,0:T(8,128)(2,1)S(1)} %get-tuple-element.30), channel_id=1, source_target_pairs={{0,2},{1,3},{2,0},{3,1},{4,6},{5,7},{6,4},{7,5},{8,10},{9,11},{10,... | collective-permute-start | bytes 786440 | tf_op jit(solution)/shard_map/ppermute | solution.py:393
  70.0 4.8 %collective-permute-start.2 = (f32[8,256]{1,0:T(8,128)S(1)}, f32[8,256]{1,0:T(8,128)S(1)}, u32[]{:S(2)}, u32[]{:S(2)}) collective-permute-start(f32[8,256]{1,0:T(8,128)S(1)} %get-tuple-element.28), channel_id=1, source_target_pairs={{0,4},{4,8},{8,12},{12,16},{16,20},{20,24},{24,28},{28,32},{32,36}... | collective-permute-start | bytes 24584 | tf_op jit(solution)/shard_map/ppermute | solution.py:416
